TPU v7x, 32 devices: a whole 2x2x4 slice. The times are simulated.
32 devices in a mesh: groups: 2 (over y), renv: 16 (over z, x, core).
Axes of the slice: x: 2, y: 2, z: 4, core: 2. Of those that a mesh axis runs over, the one named last changes fastest.
Arguments:
- psi: float32 [256, 16384], P(('groups', 'renv')), parts along dimension 0, may hold values from -18 to 18, as said below
- left_env: float32 [128, 16384], P('groups'), parts along dimension 0, may hold values from -1 to 1.5
- right_env: float32 [512, 16384], P(('groups', 'renv')), parts along dimension 0, may hold values from -1 to 1.5
- send_block: int32 [512, 1], P(('groups', 'renv')), parts along dimension 0, may hold values from 0 to 7
- send_left: int32 [512, 1, 2], P(('groups', 'renv')), parts along dimension 0, may hold values from 0 to 63
- send_live: int32 [512, 1, 2], P(('groups', 'renv')), parts along dimension 0, may hold values from 0 to 1, as said below
- recv_right: int32 [512, 1, 2], P(('groups', 'renv')), parts along dimension 0, may hold values from 0 to 15
- recv_out: int32 [512, 1, 2], P(('groups', 'renv')), parts along dimension 0, may hold values from 0 to 7
- loc_block: int32 [1024], P(('groups', 'renv')), parts along dimension 0, may hold values from 0 to 7
- loc_left: int32 [1024], P(('groups', 'renv')), parts along dimension 0, may hold values from 0 to 63
- loc_right: int32 [1024], P(('groups', 'renv')), parts along dimension 0, may hold values from 0 to 15
Outputs:
- hpsi: float32 [256, 16384], P(('groups', 'renv')), parts along dimension 0
- residual: float32 [256, 16384], P(('groups', 'renv')), parts along dimension 0
There are 2 independent parts, one for each index of `groups`. A program takes and returns all parts, laid end to end along the dimension named above; each array names one. Nothing has to cross between parts.
Inputs may be any that keep to these rules, and one draw needn't show every extreme that they name: psi blocks of owner-ordered index i have entries of size growing with i. `send_live`: in every draw some receiver has every term live from every sender.
All inputs are finite; a program needn't handle non-finite values.
Results may differ from a plain program's by a relative error of at most 0.0003.
Values sent between devices are 32-bit elements; how exact they have to be, the bound alone decides.
No kernel may reach another device: no remote copies, remote signals or barrier semaphores. Data moves between devices by JAX's collectives and lax.ppermute only.
A program may use at most 128 MiB of HBM per device.

v0:
```python
import math

import jax
import jax.numpy as jnp
from jax import lax
from jax.experimental import pallas as pl
from jax.experimental.pallas import tpu as pltpu
from jax.sharding import PartitionSpec as P

F32 = jnp.float32
BF16 = jnp.bfloat16
SUB = 8
VMEM = pl.BlockSpec(memory_space=pltpu.VMEM)
SMEM = pl.BlockSpec(memory_space=pltpu.SMEM)
HBM = pl.BlockSpec(memory_space=pltpu.HBM)
MIB = 2**20
LIGHT = pl.CostEstimate(flops=10**6, bytes_accessed=2**16, transcendentals=0)


def as_rows(blocks, sector):
    count = blocks.shape[0]
    split = blocks.reshape(count // SUB, SUB, sector, sector)
    return split.transpose(0, 2, 1, 3).reshape(count * sector, sector)


def from_rows(rows, count):
    sector = rows.shape[1]
    split = rows.reshape(count // SUB, sector, SUB, sector)
    return split.transpose(0, 2, 1, 3).reshape(count, sector * sector)


def pick(ref, block):
    sector = ref.shape[1]
    start = (block // SUB) * (SUB * sector) + block % SUB
    return ref[pl.ds(start, sector, stride=SUB), :]


def halves(mat):
    high = mat.astype(BF16)
    low = (mat - high.astype(F32)).astype(BF16)
    return jnp.concatenate([high, low], axis=1)


def doubled(mat):
    both = halves(mat)
    return jnp.concatenate([both, both], axis=0)


def product(left, right):
    sector = right.shape[1] // 2
    wide = jnp.dot(left, right, preferred_element_type=F32)
    return wide[:, :sector] + wide[:, sector:]


def stacked(mat):
    high = mat.astype(BF16)
    low = (mat - high.astype(F32)).astype(BF16)
    rows = [jnp.concatenate([part, part], axis=1) for part in (high, low)]
    return jnp.concatenate(rows, axis=0)


def product_t(left, right):
    sector = right.shape[0] // 2
    wide = lax.dot_general(left, right, (((1,), (1,)), ((), ())), preferred_element_type=F32)
    return wide[:, :sector] + wide[:, sector:]


def twice(part):
    return jnp.concatenate([part, part], axis=0)


def roomy(mib):
    return pltpu.CompilerParams(vmem_limit_bytes=mib * MIB)


def gather_kernel(block_ref, left_ref, live_ref, psi_rows, out_hbm, stage, sems):
    slots, terms, _ = left_ref.shape
    sector = psi_rows.shape[1]
    lane = lax.broadcasted_iota(jnp.int32, (SUB, sector), 1)
    puts = []
    for i in range(stage.shape[0]):
        stage[i, :sector] = pick(psi_rows, block_ref[i])
        values = jnp.zeros(lane.shape, jnp.int32)
        for g in range(terms):
            values = jnp.where(lane == g, left_ref[i % slots, g, i // slots], values)
            values = jnp.where(lane == terms + g, live_ref[i % slots, g, i // slots], values)
        stage[i, sector:] = values.astype(F32)
        put = pltpu.make_async_copy(stage.at[i], out_hbm.at[i], sems.at[i])
        put.start()
        puts.append(put)
    for put in puts:
        put.wait()


def prepare_kernel(
    sent_hbm,
    rindex_ref,
    out_index_ref,
    block_ref,
    left_ref,
    right_ref,
    psi_rows,
    right_rows,
    left_rows,
    turned_ref,
    parts_ref,
    near_ref,
    psis_ref,
    stacks_ref,
    moved_ref,
):
    slots, terms, _ = rindex_ref.shape
    sector = psi_rows.shape[1]

    rights = right_rows.shape[0] // sector
    lefts = left_rows.shape[0] // sector

    def split_right(i, carry):
        mat = pick(right_rows, i)
        parts_ref[lefts + i] = halves(mat)
        stacks_ref[i] = stacked(mat)
        return carry

    lax.fori_loop(0, rights, split_right, 0, unroll=4)

    def split_psi(i, carry):
        psis_ref[i] = halves(pick(psi_rows, i))
        return carry

    lax.fori_loop(0, psis_ref.shape[0], split_psi, 0, unroll=4)

    def turn(i, carry):
        for g in range(terms):
            right = stacks_ref[rindex_ref[i % slots, g, i // slots]]
            psi = psis_ref[out_index_ref[i % slots, g, i // slots]]
            turned_ref[i, g * sector : (g + 1) * sector] = product_t(psi, right)
        turned_ref[i, terms * sector :] = jnp.zeros((SUB, sector), F32)
        return carry

    slabs = near_ref.shape[0] // terms
    senders = turned_ref.shape[0] - slabs
    lax.fori_loop(0, senders, turn, 0, unroll=4)

    def split_left(i, carry):
        parts_ref[i] = halves(pick(left_rows, i))
        return carry

    lax.fori_loop(0, lefts, split_left, 0, unroll=8)

    def left_step(k, carry):
        moved_ref[k] = halves(product(parts_ref[left_ref[k]], twice(psis_ref[block_ref[k]])))
        return carry

    lax.fori_loop(0, block_ref.shape[0], left_step, 0, unroll=8)
    near_ref[...] = jnp.zeros_like(near_ref)

    def right_step(k, carry):
        near_ref[block_ref[k]] += product(moved_ref[k], twice(parts_ref[lefts + right_ref[k]]))
        return carry

    lax.fori_loop(0, block_ref.shape[0], right_step, 0, unroll=8)
    corr = jnp.zeros((1, sector), F32)
    norm = jnp.zeros((1, sector), F32)
    for b in range(near_ref.shape[0]):
        mat = pick(psi_rows, b)
        turned_ref[senders + b // terms, (b % terms) * sector : (b % terms + 1) * sector] = near_ref[b]
        corr += jnp.sum(mat * near_ref[b], axis=0, keepdims=True)
        norm += jnp.sum(mat * mat, axis=0, keepdims=True)
    row = lax.broadcasted_iota(jnp.int32, (SUB, sector), 0)
    turned_ref[0, terms * sector :] = jnp.where(row == 0, corr, jnp.where(row == 1, norm, 0.0))


def arrive_kernel(terms, came_ref, turned_hbm, parts_hbm, moved_ref, sums_ref, marks, turned_ref, lefts_ref, sems):
    count, height, sector = came_ref.shape
    get_marks = pltpu.make_async_copy(came_ref.at[:, pl.ds(sector, height - sector)], marks, sems.at[0])
    get_lefts = pltpu.make_async_copy(parts_hbm.at[pl.ds(0, lefts_ref.shape[0])], lefts_ref, sems.at[1])
    get_turned = pltpu.make_async_copy(turned_hbm.at[pl.ds(0, count)], turned_ref, sems.at[2])
    get_marks.start()
    get_lefts.start()
    get_turned.start()
    get_marks.wait()
    get_lefts.wait()
    get_turned.wait()

    def block(i, total):
        stack = [lefts_ref[marks[i, 0, g].astype(jnp.int32)] for g in range(terms)]
        moved = product(jnp.concatenate(stack, axis=0), doubled(came_ref[i, :sector]))
        for g in range(terms):
            part = slice(g * sector, (g + 1) * sector)
            one = moved[part] * marks[i, 0, terms + g]
            moved_ref[i, part] = halves(one)
            total += jnp.sum((one * turned_ref[i, part]).reshape(-1, SUB, sector), axis=0)
        return total

    total = lax.fori_loop(0, count, block, jnp.zeros((SUB, sector), F32), unroll=4)
    corr = jnp.sum(total, axis=0, keepdims=True)
    row = lax.broadcasted_iota(jnp.int32, total.shape, 0)
    mine = turned_ref[0, terms * sector :] + jnp.where(row == 0, corr, 0.0)
    for i in range(sums_ref.shape[0]):
        sums_ref[i] = mine


def remote_kernel(rindex_ref, out_index_ref, moved_ref, turned_hbm, parts_hbm, hpsi_rows, hpsi_hbm, acc, rights_ref, sems):
    slots, terms, _ = rindex_ref.shape
    senders, height, _ = moved_ref.shape
    sector = height // terms
    rights = rights_ref.shape[0]
    rights_hbm = parts_hbm.at[pl.ds(parts_hbm.shape[0] - rights, rights)]
    get_rights = pltpu.make_async_copy(rights_hbm, rights_ref, sems.at[0])
    get_rights.start()
    slabs = []
    for k in range(acc.shape[0] // height):
        near = turned_hbm.at[senders + k, pl.ds(0, height)]
        slabs.append(pltpu.make_async_copy(near, acc.at[pl.ds(k * height, height)], sems.at[1 + k]))
        slabs[k].start()
    get_rights.wait()
    for copy in slabs:
        copy.wait()

    def right_step(i, carry):
        for g in range(terms):
            right = rights_ref[rindex_ref[i % slots, g, i // slots]]
            spot = pl.multiple_of(out_index_ref[i % slots, g, i // slots] * sector, sector)
            acc[pl.ds(spot, sector)] += product(moved_ref[i, g * sector : (g + 1) * sector], twice(right))
        return carry

    lax.fori_loop(0, senders, right_step, 0, unroll=4)
    for b in range(acc.shape[0] // sector):
        start = (b // SUB) * (SUB * sector) + b % SUB
        hpsi_rows[pl.ds(start, sector, stride=SUB), :] = acc[b * sector : (b + 1) * sector]
    put = pltpu.make_async_copy(hpsi_rows, hpsi_hbm, sems.at[0])
    put.start()
    put.wait()


def residual_kernel(sums_ref, hpsi_rows, psi_rows, out_ref):
    total = jnp.sum(sums_ref[...], axis=0)
    whole = jnp.sum(total, axis=1, keepdims=True)
    theta = whole[0:1] / (whole[1:2] + 1e-06)
    out_ref[...] = hpsi_rows[...] - theta * psi_rows[...]


def shards(
    psi,
    left_env,
    right_env,
    send_block,
    send_left,
    send_live,
    recv_right,
    recv_out,
    loc_block,
    loc_left,
    loc_right,
):
    peers = lax.axis_size("renv")
    owned = psi.shape[0]
    sector = math.isqrt(psi.shape[1])
    slots = send_block.shape[1]
    terms = send_left.shape[2]
    count = peers * slots
    lefts = left_env.shape[0]
    rights = right_env.shape[0]
    height = sector + SUB
    psi_rows = as_rows(psi, sector)
    left_rows = as_rows(left_env, sector)
    right_rows = as_rows(right_env, sector)
    by_slot = [index.transpose(1, 2, 0) for index in (send_left, send_live, recv_right, recv_out)]
    blocks = jax.ShapeDtypeStruct((count, height, sector), F32)
    rows = jax.ShapeDtypeStruct((owned * sector, sector), F32)

    sent = pl.pallas_call(
        gather_kernel,
        out_shape=blocks,
        in_specs=[SMEM] * 3 + [VMEM],
        out_specs=HBM,
        scratch_shapes=[pltpu.VMEM(blocks.shape, F32), pltpu.SemaphoreType.DMA((count,))],
        compiler_params=roomy(56),
        name="gather_blocks",
    )(send_block.reshape(-1), *by_slot[:2], psi_rows)
    came = lax.all_to_all(sent.reshape(peers, slots, height, sector), "renv", split_axis=0, concat_axis=0, tiled=True)
    came = came.reshape(count, height, sector)

    slabs = owned // terms
    turned, parts = pl.pallas_call(
        prepare_kernel,
        out_shape=(
            jax.ShapeDtypeStruct((count + slabs, terms * sector + SUB, sector), F32),
            jax.ShapeDtypeStruct((lefts + rights, sector, 2 * sector), BF16),
        ),
        in_specs=[HBM] + [SMEM] * 5 + [VMEM] * 3,
        out_specs=(VMEM,) * 2,
        scratch_shapes=[
            pltpu.VMEM((owned, sector, sector), F32),
            pltpu.VMEM((owned, sector, 2 * sector), BF16),
            pltpu.VMEM((rights, 2 * sector, 2 * sector), BF16),
            pltpu.VMEM((loc_block.shape[0], sector, 2 * sector), BF16),
        ],
        compiler_params=roomy(56),
        cost_estimate=LIGHT,
        name="prepare",
    )(sent, *by_slot[2:], loc_block, loc_left, loc_right, psi_rows, right_rows, left_rows)

    chunk = math.gcd(count, 16)
    moved = []
    sums = 0.0
    for first in range(0, count, chunk):
        part = slice(first, first + chunk) if count > chunk else slice(None)
        kept, share = pl.pallas_call(
            lambda *refs: arrive_kernel(terms, *refs),
            out_shape=(
                jax.ShapeDtypeStruct((chunk, terms * sector, 2 * sector), BF16),
                jax.ShapeDtypeStruct((peers, SUB, sector), F32),
            ),
            in_specs=[VMEM] + [HBM] * 2,
            out_specs=(VMEM,) * 2,
            scratch_shapes=[
                pltpu.SMEM((chunk, SUB, sector), F32),
                pltpu.VMEM((chunk, terms * sector + SUB, sector), F32),
                pltpu.VMEM((lefts, sector, 2 * sector), BF16),
                pltpu.SemaphoreType.DMA((3,)),
            ],
            compiler_params=roomy(50),
            name="arrive",
        )(came[part], turned if count == chunk else turned[part], parts)
        moved.append(kept)
        sums = share if count == chunk else sums + share
    moved = moved[0] if len(moved) == 1 else jnp.concatenate(moved, axis=0)
    totals = lax.all_to_all(sums, "renv", split_axis=0, concat_axis=0, tiled=True)

    hpsi_rows, hpsi = pl.pallas_call(
        remote_kernel,
        out_shape=(rows, rows),
        in_specs=[SMEM] * 2 + [VMEM] + [HBM] * 2,
        out_specs=(VMEM, HBM),
        scratch_shapes=[
            pltpu.VMEM(rows.shape, F32),
            pltpu.VMEM((rights, sector, 2 * sector), BF16),
            pltpu.SemaphoreType.DMA((1 + slabs,)),
        ],
        compiler_params=roomy(50),
        cost_estimate=pl.CostEstimate(flops=4 * 10**9, bytes_accessed=6 * MIB, transcendentals=0),
        name="remote_terms",
    )(*by_slot[2:], moved, turned, parts)

    residual_rows = pl.pallas_call(
        residual_kernel,
        out_shape=rows,
        in_specs=[VMEM] * 3,
        out_specs=VMEM,
        compiler_params=roomy(16),
        name="residual",
    )(totals, hpsi_rows, psi_rows)
    return (from_rows(hpsi, owned), from_rows(residual_rows, owned))


def solution(mesh):
    placed = (
        P(("groups", "renv"), None),
        P("groups", None),
        P(("groups", "renv"), None),
        P(("groups", "renv"), None),
        P(("groups", "renv"), None, None),
        P(("groups", "renv"), None, None),
        P(("groups", "renv"), None, None),
        P(("groups", "renv"), None, None),
        P(("groups", "renv")),
        P(("groups", "renv")),
        P(("groups", "renv")),
    )
    return jax.shard_map(
        shards,
        mesh=mesh,
        in_specs=placed,
        out_specs=(P(("groups", "renv"), None), P(("groups", "renv"), None)),
        check_vma=False,
    )
```

profile of v0, /device:TPU:0, one launch (start us, length us, event | category | flops | bytes accessed | tf_op | source)
XLA Modules:
  0.0 54.3 jit_solution(14268184440248870309)
XLA Ops:
  0.6 2.3 %gather_blocks.1.sent_hbm = f32[16,136,128]{2,1,0:T(8,128)} custom-call(s32[16]{0:T(128)} %bitcast.48, s32[1,2,16]{2,1,0:T(2,128)} %bitcast.46, s32[1,2,16]{2,1,0:T(2,128)} %bitcast.47, f32[1024,128]{1,0:T(8,128)} %bitcast.34), custom_call_target="tpu_custom_call" | custom-call | tf_op jit(solution)/shard_map/gather_blocks/pallas_call | solution.py:272
  2.9 7.4 %all-to-all-start = ((f32[16,1,136,128]{3,2,1,0:T(8,128)}), f32[16,1,136,128]{3,2,1,0:T(8,128)S(1)}, u32[]{:S(2)}, u32[]{:S(2)}) async-start(f32[16,1,136,128]{3,2,1,0:T(8,128)} %bitcast.42), calls=%async_computation | async-start | bytes 2228224 | tf_op jit(solution)/shard_map/all_to_all | solution.py:281
  10.3 11.6 %prepare.1 = (f32[20,264,128]{2,1,0:T(8,128)}, bf16[80,128,256]{2,1,0:T(8,128)(2,1)}) custom-call(f32[16,136,128]{2,1,0:T(8,128)} %gather_blocks.1.sent_hbm, s32[1,2,16]{2,1,0:T(2,128)} %bitcast.38, s32[1,2,16]{2,1,0:T(2,128)} %bitcast.40, s32[32]{0:T(128)} %block_ref.1, s32[32]{0:T(128)} %left_ref.1, s32[32]{0:T(128)} %right_ref.1, f32[1024,128]{1,0:T(8,128)} %bitcast.35, ...), custom_call_target="tpu_custom_call" | custom-call | flops 1000000 | bytes 65536 | tf_op jit(solution)/shard_map/prepare/pallas_call | solution.py:285
  21.9 12.4 %all-to-all-done = f32[16,1,136,128]{3,2,1,0:T(8,128)S(1)} async-done(((f32[16,1,136,128]{3,2,1,0:T(8,128)}), f32[16,1,136,128]{3,2,1,0:T(8,128)S(1)}, u32[]{:S(2)}, u32[]{:S(2)}) %all-to-all-start) | async-done | bytes 1114144 | tf_op jit(solution)/shard_map/all_to_all | solution.py:281
  34.3 0.0 copy-start.1
  34.3 0.0 copy-start.2
  34.3 4.8 %arrive.1 = (bf16[16,256,256]{2,1,0:T(8,128)(2,1)S(1)}, f32[16,8,128]{2,1,0:T(8,128)}) custom-call(f32[16,136,128]{2,1,0:T(8,128)S(1)} %bitcast.37, f32[20,264,128]{2,1,0:T(8,128)} %get-tuple-element.8.refs_1_.turned_hbm, bf16[80,128,256]{2,1,0:T(8,128)(2,1)} %get-tuple-element.9.refs_2_.parts_hbm), custom_call_target="tpu_custom_call" | custom-call | tf_op jit(solution)/shard_map/arrive/pallas_call | solution.py:309
  39.2 7.2 %all-to-all-start.1 = ((f32[16,8,128]{2,1,0:T(8,128)}), f32[16,8,128]{2,1,0:T(8,128)S(1)}, u32[]{:S(2)}, u32[]{:S(2)}) async-start(f32[16,8,128]{2,1,0:T(8,128)} %get-tuple-element.12), calls=%async_computation.1 | async-start | bytes 131072 | tf_op jit(solution)/shard_map/all_to_all | solution.py:329
  46.4 0.0 copy-done.1
  46.4 0.0 copy-done.2
  46.4 0.0 copy-start
  46.4 4.1 %remote_terms.1 = (f32[1024,128]{1,0:T(8,128)S(1)}, f32[1024,128]{1,0:T(8,128)}) custom-call(s32[1,2,16]{2,1,0:T(2,128)S(1)} %bitcast.39, s32[1,2,16]{2,1,0:T(2,128)S(1)} %bitcast.41, bf16[16,256,256]{2,1,0:T(8,128)(2,1)S(1)} %get-tuple-element.10.moved_ref, f32[20,264,128]{2,1,0:T(8,128)} %get-tuple-element.8.refs_1_.turned_hbm, ...), custom_call_target="tpu_custom_call" | custom-call | flops 4000000000 | bytes 6291456 | tf_op jit(solution)/shard_map/remote_terms/pallas_call | solution.py:331
  50.6 2.7 %all-to-all-done.1.sums_ref = f32[16,8,128]{2,1,0:T(8,128)S(1)} async-done(((f32[16,8,128]{2,1,0:T(8,128)}), f32[16,8,128]{2,1,0:T(8,128)S(1)}, u32[]{:S(2)}, u32[]{:S(2)}) %all-to-all-start.1) | async-done | bytes 65568 | tf_op jit(solution)/shard_map/all_to_all | solution.py:329
  53.3 0.0 copy-done
  53.3 1.0 %residual.1 = f32[1024,128]{1,0:T(8,128)} custom-call(f32[16,8,128]{2,1,0:T(8,128)S(1)} %all-to-all-done.1.sums_ref, f32[1024,128]{1,0:T(8,128)S(1)} %get-tuple-element.13.hpsi_rows, f32[1024,128]{1,0:T(8,128)S(1)} %bitcast.36), custom_call_target="tpu_custom_call" | custom-call | tf_op jit(solution)/shard_map/residual/pallas_call | solution.py:346
Async XLA Ops:
  2.9 31.4 %all-to-all-start = ((f32[16,1,136,128]{3,2,1,0:T(8,128)}), f32[16,1,136,128]{3,2,1,0:T(8,128)S(1)}, u32[]{:S(2)}, u32[]{:S(2)}) async-start(f32[16,1,136,128]{3,2,1,0:T(8,128)} %bitcast.42), calls=%async_computation | async-start | bytes 2228224 | tf_op jit(solution)/shard_map/all_to_all | solution.py:281
  34.3 12.1 %copy-start.1 = (s32[16,1,2]{0,2,1:T(2,128)S(1)}, s32[16,1,2]{0,2,1:T(2,128)}, u32[]{:S(2)}) copy-start(s32[16,1,2]{0,2,1:T(2,128)} %param.17) | copy-start | bytes 388
  34.3 12.1 %copy-start.2 = (s32[16,1,2]{0,2,1:T(2,128)S(1)}, s32[16,1,2]{0,2,1:T(2,128)}, u32[]{:S(2)}) copy-start(s32[16,1,2]{0,2,1:T(2,128)} %param.18) | copy-start | bytes 388
  39.2 14.1 %all-to-all-start.1 = ((f32[16,8,128]{2,1,0:T(8,128)}), f32[16,8,128]{2,1,0:T(8,128)S(1)}, u32[]{:S(2)}, u32[]{:S(2)}) async-start(f32[16,8,128]{2,1,0:T(8,128)} %get-tuple-element.12), calls=%async_computation.1 | async-start | bytes 131072 | tf_op jit(solution)/shard_map/all_to_all | solution.py:329
  46.4 6.9 %copy-start = (f32[8,16384]{1,0:T(8,128)S(1)}, f32[8,16384]{1,0:T(8,128)}, u32[]{:S(2)}) copy-start(f32[8,16384]{1,0:T(8,128)} %param.11) | copy-start | bytes 1572868
where the time goes:
time: 54.6 us; the launch traced here: 54.3 us
  Pallas kernels  23.9 us (44%)
  waiting for transfers between devices  15.1 us (28%)
  starting transfers between devices  14.6 us (27%)
  between operations  0.7 us (1%)
    all_to_all x1, waiting for transfers between devices, shards(): lax.all_to_all(sent.reshape(peers, slots, height, sector), 'renv', split_...  12.4 us
    pallas_call x1, Pallas kernels, shards(): pl.pallas_call(prepare_kernel, out_shape=(jax.ShapeDtypeStruct((count + s...  11.6 us
    all_to_all x1, starting transfers between devices, shards(): lax.all_to_all(sent.reshape(peers, slots, height, sector), 'renv', split_...  7.37 us
    all_to_all x1, starting transfers between devices, shards(): lax.all_to_all(sums, 'renv', split_axis=0, concat_axis=0, tiled=True)  7.2 us
    pallas_call x1, Pallas kernels, shards(): pl.pallas_call(lambda *refs: arrive_kernel(terms, *refs), out_shape=(jax....  4.83 us
    pallas_call x1, Pallas kernels, shards(): pl.pallas_call(remote_kernel, out_shape=(rows, rows), in_specs=[SMEM] * 2...  4.15 us
    all_to_all x1, waiting for transfers between devices, shards(): lax.all_to_all(sums, 'renv', split_axis=0, concat_axis=0, tiled=True)  2.71 us
    pallas_call x1, Pallas kernels, shards(): pl.pallas_call(gather_kernel, out_shape=blocks, in_specs=[SMEM] * 3 + [VM...  2.28 us
  transfers between devices with their start and end apart: 2, of which 2 were waited for; matrix products, arithmetic and copies ran while one was open for 0% of the time, Pallas kernels for 29%

commit v1 on v0

--- a/solution.py
+++ b/solution.py
@@ -200,22 +200,20 @@
         sums_ref[i] = mine
 
 
-def remote_kernel(rindex_ref, out_index_ref, moved_ref, turned_hbm, parts_hbm, hpsi_rows, hpsi_hbm, acc, rights_ref, sems):
+def remote_kernel(sums_hbm, rindex_ref, out_index_ref, moved_ref, turned_hbm, parts_hbm, hpsi_rows, acc, near_ref, rights_ref, sems):
     slots, terms, _ = rindex_ref.shape
     senders, height, _ = moved_ref.shape
     sector = height // terms
     rights = rights_ref.shape[0]
-    rights_hbm = parts_hbm.at[pl.ds(parts_hbm.shape[0] - rights, rights)]
-    get_rights = pltpu.make_async_copy(rights_hbm, rights_ref, sems.at[0])
+    get_rights = pltpu.make_async_copy(parts_hbm.at[pl.ds(parts_hbm.shape[0] - rights, rights)], rights_ref, sems.at[0])
     get_rights.start()
     slabs = []
     for k in range(acc.shape[0] // height):
         near = turned_hbm.at[senders + k, pl.ds(0, height)]
-        slabs.append(pltpu.make_async_copy(near, acc.at[pl.ds(k * height, height)], sems.at[1 + k]))
+        slabs.append(pltpu.make_async_copy(near, near_ref.at[pl.ds(k * height, height)], sems.at[1 + k]))
         slabs[k].start()
+    acc[...] = jnp.zeros_like(acc)
     get_rights.wait()
-    for copy in slabs:
-        copy.wait()
 
     def right_step(i, carry):
         for g in range(terms):
@@ -225,19 +223,22 @@
         return carry
 
     lax.fori_loop(0, senders, right_step, 0, unroll=4)
+    for copy in slabs:
+        copy.wait()
     for b in range(acc.shape[0] // sector):
         start = (b // SUB) * (SUB * sector) + b % SUB
-        hpsi_rows[pl.ds(start, sector, stride=SUB), :] = acc[b * sector : (b + 1) * sector]
-    put = pltpu.make_async_copy(hpsi_rows, hpsi_hbm, sems.at[0])
+        part = slice(b * sector, (b + 1) * sector)
+        hpsi_rows[pl.ds(start, sector, stride=SUB), :] = acc[part] + near_ref[part]
+
+
+def residual_kernel(sums_ref, hpsi_rows, psi_rows, hpsi_hbm, out_ref, sem):
+    put = pltpu.make_async_copy(hpsi_rows, hpsi_hbm, sem)
     put.start()
-    put.wait()
-
-
-def residual_kernel(sums_ref, hpsi_rows, psi_rows, out_ref):
     total = jnp.sum(sums_ref[...], axis=0)
     whole = jnp.sum(total, axis=1, keepdims=True)
     theta = whole[0:1] / (whole[1:2] + 1e-06)
     out_ref[...] = hpsi_rows[...] - theta * psi_rows[...]
+    put.wait()
 
 
 def shards(
@@ -301,6 +302,7 @@
         name="prepare",
     )(sent, *by_slot[2:], loc_block, loc_left, loc_right, psi_rows, right_rows, left_rows)
 
+    near_by = math.gcd(peers, 4)
     chunk = math.gcd(count, 16)
     moved = []
     sums = 0.0
@@ -310,7 +312,7 @@
             lambda *refs: arrive_kernel(terms, *refs),
             out_shape=(
                 jax.ShapeDtypeStruct((chunk, terms * sector, 2 * sector), BF16),
-                jax.ShapeDtypeStruct((peers, SUB, sector), F32),
+                jax.ShapeDtypeStruct((near_by, SUB, sector), F32),
             ),
             in_specs=[VMEM] + [HBM] * 2,
             out_specs=(VMEM,) * 2,
@@ -326,14 +328,20 @@
         moved.append(kept)
         sums = share if count == chunk else sums + share
     moved = moved[0] if len(moved) == 1 else jnp.concatenate(moved, axis=0)
-    totals = lax.all_to_all(sums, "renv", split_axis=0, concat_axis=0, tiled=True)
-
-    hpsi_rows, hpsi = pl.pallas_call(
+    together = [list(range(first, first + near_by)) for first in range(0, peers, near_by)]
+    across = [list(range(first, peers, near_by)) for first in range(near_by)]
+    totals = lax.all_to_all(sums, "renv", split_axis=0, concat_axis=0, tiled=True, axis_index_groups=together)
+    first_sums = jnp.sum(totals, axis=0)
+    totals = jnp.broadcast_to(first_sums[None], (peers // near_by, SUB, sector))
+    totals = lax.all_to_all(totals, "renv", split_axis=0, concat_axis=0, tiled=True, axis_index_groups=across)
+
+    hpsi_rows = pl.pallas_call(
         remote_kernel,
-        out_shape=(rows, rows),
-        in_specs=[SMEM] * 2 + [VMEM] + [HBM] * 2,
-        out_specs=(VMEM, HBM),
+        out_shape=rows,
+        in_specs=[HBM] + [SMEM] * 2 + [VMEM] + [HBM] * 2,
+        out_specs=VMEM,
         scratch_shapes=[
+            pltpu.VMEM(rows.shape, F32),
             pltpu.VMEM(rows.shape, F32),
             pltpu.VMEM((rights, sector, 2 * sector), BF16),
             pltpu.SemaphoreType.DMA((1 + slabs,)),
@@ -341,13 +349,14 @@
         compiler_params=roomy(50),
         cost_estimate=pl.CostEstimate(flops=4 * 10**9, bytes_accessed=6 * MIB, transcendentals=0),
         name="remote_terms",
-    )(*by_slot[2:], moved, turned, parts)
-
-    residual_rows = pl.pallas_call(
+    )(first_sums, *by_slot[2:], moved, turned, parts)
+
+    hpsi, residual_rows = pl.pallas_call(
         residual_kernel,
-        out_shape=rows,
+        out_shape=(rows, rows),
         in_specs=[VMEM] * 3,
-        out_specs=VMEM,
+        out_specs=(HBM, VMEM),
+        scratch_shapes=[pltpu.SemaphoreType.DMA],
         compiler_params=roomy(16),
         name="residual",
     )(totals, hpsi_rows, psi_rows)

time: 54.6 us -> 59.6 us (1.092)
  blocking collectives: 0 us -> 7.33 us
  starting transfers between devices: 14.6 us -> 12.9 us
  Pallas kernels: 23.9 us -> 23 us
  local copies, waits for them, and re-layouts: 0.01 us -> 0.62 us
    all_to_all x0 -> x1, blocking collectives: none -> 7.33 us  [shards(): lax.all_to_all(sums, 'renv', split_axis=0, concat_axis=0, tiled=True, axi...]
    all_to_all x1, starting transfers between devices: 7.2 us -> 5.54 us  [shards(): lax.all_to_all(totals, 'renv', split_axis=0, concat_axis=0, tiled=True, a...]
    pallas_call x1, Pallas kernels: 4.83 us -> 4.21 us  [shards(): pl.pallas_call(lambda *refs: arrive_kernel(terms, *refs), out_shape=(jax....]
    broadcast_in_dim x0 -> x1, local copies, waits for them, and re-layouts: none -> 0.61 us  [shards(): totals = jnp.broadcast_to(first_sums[None], (peers // near_by, SUB, sector))]
  transfers between devices with their start and end apart: 2 -> 2, of which waited for: 2 -> 2; matrix products, arithmetic and copies ran while one was open for 0% -> 0% of each run, Pallas kernels for 29% -> 25%
where the time goes in v1:
time: 59.6 us; the launch traced here: 59.2 us
  Pallas kernels  23 us (39%)
  waiting for transfers between devices  14.7 us (25%)
  starting transfers between devices  12.9 us (22%)
  blocking collectives  7.33 us (12%)
  between operations  0.67 us (1%)
  local copies, waits for them, and re-layouts  0.62 us (1%)
    all_to_all x1, waiting for transfers between devices, shards(): lax.all_to_all(sent.reshape(peers, slots, height, sector), 'renv', split_...  12.4 us
    pallas_call x1, Pallas kernels, shards(): pl.pallas_call(prepare_kernel, out_shape=(jax.ShapeDtypeStruct((count + s...  11.6 us
    all_to_all x1, starting transfers between devices, shards(): lax.all_to_all(sent.reshape(peers, slots, height, sector), 'renv', split_...  7.37 us
    all_to_all x1, blocking collectives, shards(): lax.all_to_all(sums, 'renv', split_axis=0, concat_axis=0, tiled=True, axi...  7.33 us
    all_to_all x1, starting transfers between devices, shards(): lax.all_to_all(totals, 'renv', split_axis=0, concat_axis=0, tiled=True, a...  5.54 us
    pallas_call x1, Pallas kernels, shards(): pl.pallas_call(lambda *refs: arrive_kernel(terms, *refs), out_shape=(jax....  4.21 us
    pallas_call x1, Pallas kernels, shards(): pl.pallas_call(remote_kernel, out_shape=rows, in_specs=[HBM] + [SMEM] * 2...  3.26 us
    all_to_all x1, waiting for transfers between devices, shards(): lax.all_to_all(totals, 'renv', split_axis=0, concat_axis=0, tiled=True, a...  2.33 us
  transfers between devices with their start and end apart: 2, of which 2 were waited for; matrix products, arithmetic and copies ran while one was open for 0% of the time, Pallas kernels for 25%

profile of v1, /device:TPU:0, one launch (start us, length us, event | category | flops | bytes accessed | tf_op | source)
XLA Modules:
  0.0 59.2 jit_solution(1666766493277115812)
XLA Ops:
  0.6 2.3 %gather_blocks.1.sent_hbm = f32[16,136,128]{2,1,0:T(8,128)} custom-call(s32[16]{0:T(128)} %bitcast.47, s32[1,2,16]{2,1,0:T(2,128)} %bitcast.45, s32[1,2,16]{2,1,0:T(2,128)} %bitcast.46, f32[1024,128]{1,0:T(8,128)} %bitcast.34), custom_call_target="tpu_custom_call" | custom-call | tf_op jit(solution)/shard_map/gather_blocks/pallas_call | solution.py:273
  2.9 7.4 %all-to-all-start = ((f32[16,1,136,128]{3,2,1,0:T(8,128)}), f32[16,1,136,128]{3,2,1,0:T(8,128)S(1)}, u32[]{:S(2)}, u32[]{:S(2)}) async-start(f32[16,1,136,128]{3,2,1,0:T(8,128)} %bitcast.42), calls=%async_computation | async-start | bytes 2228224 | tf_op jit(solution)/shard_map/all_to_all | solution.py:282
  10.3 11.6 %prepare.1 = (f32[20,264,128]{2,1,0:T(8,128)}, bf16[80,128,256]{2,1,0:T(8,128)(2,1)}) custom-call(f32[16,136,128]{2,1,0:T(8,128)} %gather_blocks.1.sent_hbm, s32[1,2,16]{2,1,0:T(2,128)} %bitcast.38, s32[1,2,16]{2,1,0:T(2,128)} %bitcast.40, s32[32]{0:T(128)} %block_ref.1, s32[32]{0:T(128)} %left_ref.1, s32[32]{0:T(128)} %right_ref.1, f32[1024,128]{1,0:T(8,128)} %bitcast.35, ...), custom_call_target="tpu_custom_call" | custom-call | flops 1000000 | bytes 65536 | tf_op jit(solution)/shard_map/prepare/pallas_call | solution.py:286
  22.0 12.4 %all-to-all-done = f32[16,1,136,128]{3,2,1,0:T(8,128)S(1)} async-done(((f32[16,1,136,128]{3,2,1,0:T(8,128)}), f32[16,1,136,128]{3,2,1,0:T(8,128)S(1)}, u32[]{:S(2)}, u32[]{:S(2)}) %all-to-all-start) | async-done | bytes 1114144 | tf_op jit(solution)/shard_map/all_to_all | solution.py:282
  34.3 0.0 copy-start.1
  34.3 0.0 copy-start.2
  34.3 4.2 %arrive.1 = (bf16[16,256,256]{2,1,0:T(8,128)(2,1)S(1)}, f32[4,8,128]{2,1,0:T(8,128)S(1)}) custom-call(f32[16,136,128]{2,1,0:T(8,128)S(1)} %bitcast.37, f32[20,264,128]{2,1,0:T(8,128)} %get-tuple-element.8.refs_1_.turned_hbm, bf16[80,128,256]{2,1,0:T(8,128)(2,1)} %get-tuple-element.9.refs_2_.parts_hbm), custom_call_target="tpu_custom_call" | custom-call | tf_op jit(solution)/shard_map/arrive/pallas_call | solution.py:311
  38.6 7.3 %all_to_all.15 = f32[4,8,128]{2,1,0:T(8,128)S(1)} all-to-all(f32[4,8,128]{2,1,0:T(8,128)S(1)} %get-tuple-element.10), channel_id=1, replica_groups={{0,1,2,3},{4,5,6,7},{8,9,10,11},{12,13,14,15},{16,17,18,19},{20,21,22,2..., dimensions={0} | all-to-all | bytes 32768 | tf_op jit(solution)/shard_map/all_to_all | solution.py:333
  45.9 0.6 %broadcast_in_dim.2 = f32[4,8,128]{2,1,0:T(8,128)} broadcast(f32[8,128]{1,0:T(8,128)S(1)} %reduce_sum.9.sums_hbm), dimensions={1,2} | broadcast | bytes 20480 | tf_op jit(solution)/shard_map/broadcast_in_dim | solution.py:335
  46.5 5.5 %all-to-all-start.2 = ((f32[4,8,128]{2,1,0:T(8,128)}), f32[4,8,128]{2,1,0:T(8,128)S(1)}, u32[]{:S(2)}, u32[]{:S(2)}) async-start(f32[4,8,128]{2,1,0:T(8,128)} %broadcast_in_dim.2), calls=%async_computation.2 | async-start | bytes 32768 | tf_op jit(solution)/shard_map/all_to_all | solution.py:336
  52.0 0.0 copy-done.1
  52.0 0.0 copy-done.2
  52.0 0.0 copy-start
  52.0 3.3 %remote_terms.1.hpsi_rows = f32[1024,128]{1,0:T(8,128)S(1)} custom-call(f32[8,128]{1,0:T(8,128)S(1)} %reduce_sum.9.sums_hbm, s32[1,2,16]{2,1,0:T(2,128)S(1)} %bitcast.39, s32[1,2,16]{2,1,0:T(2,128)S(1)} %bitcast.41, bf16[16,256,256]{2,1,0:T(8,128)(2,1)S(1)} %get-tuple-element.11.moved_ref, f32[20,264,128]{2,1,0:T(8,128)} %get-tuple-element.8.refs_1_.turned_hbm, ...), custom_call_target="tpu_custom_call" | custom-call | flops 4000000000 | bytes 6291456 | tf_op jit(solution)/shard_map/remote_terms/pallas_call | solution.py:338
  55.3 2.3 %all-to-all-done.2.sums_ref = f32[4,8,128]{2,1,0:T(8,128)S(1)} async-done(((f32[4,8,128]{2,1,0:T(8,128)}), f32[4,8,128]{2,1,0:T(8,128)S(1)}, u32[]{:S(2)}, u32[]{:S(2)}) %all-to-all-start.2) | async-done | bytes 16416 | tf_op jit(solution)/shard_map/all_to_all | solution.py:336
  57.6 0.0 copy-done
  57.7 1.6 %residual.1 = (f32[1024,128]{1,0:T(8,128)}, f32[1024,128]{1,0:T(8,128)}) custom-call(f32[4,8,128]{2,1,0:T(8,128)S(1)} %all-to-all-done.2.sums_ref, f32[1024,128]{1,0:T(8,128)S(1)} %remote_terms.1.hpsi_rows, f32[1024,128]{1,0:T(8,128)S(1)} %bitcast.36), custom_call_target="tpu_custom_call" | custom-call | tf_op jit(solution)/shard_map/residual/pallas_call | solution.py:354
  (1 shorter events, 0.0 us)
Async XLA Ops:
  2.9 31.4 %all-to-all-start = ((f32[16,1,136,128]{3,2,1,0:T(8,128)}), f32[16,1,136,128]{3,2,1,0:T(8,128)S(1)}, u32[]{:S(2)}, u32[]{:S(2)}) async-start(f32[16,1,136,128]{3,2,1,0:T(8,128)} %bitcast.42), calls=%async_computation | async-start | bytes 2228224 | tf_op jit(solution)/shard_map/all_to_all | solution.py:282
  34.3 17.7 %copy-start.1 = (s32[16,1,2]{0,2,1:T(2,128)S(1)}, s32[16,1,2]{0,2,1:T(2,128)}, u32[]{:S(2)}) copy-start(s32[16,1,2]{0,2,1:T(2,128)} %param.17) | copy-start | bytes 388
  34.3 17.7 %copy-start.2 = (s32[16,1,2]{0,2,1:T(2,128)S(1)}, s32[16,1,2]{0,2,1:T(2,128)}, u32[]{:S(2)}) copy-start(s32[16,1,2]{0,2,1:T(2,128)} %param.18) | copy-start | bytes 388
  46.5 11.1 %all-to-all-start.2 = ((f32[4,8,128]{2,1,0:T(8,128)}), f32[4,8,128]{2,1,0:T(8,128)S(1)}, u32[]{:S(2)}, u32[]{:S(2)}) async-start(f32[4,8,128]{2,1,0:T(8,128)} %broadcast_in_dim.2), calls=%async_computation.2 | async-start | bytes 32768 | tf_op jit(solution)/shard_map/all_to_all | solution.py:336
  52.0 5.6 %copy-start = (f32[8,16384]{1,0:T(8,128)S(1)}, f32[8,16384]{1,0:T(8,128)}, u32[]{:S(2)}) copy-start(f32[8,16384]{1,0:T(8,128)} %param.11) | copy-start | bytes 1572868

commit v2 on v1

--- a/solution.py
+++ b/solution.py
@@ -1,3 +1,4 @@
+import functools
 import math
 
 import jax
@@ -170,72 +171,80 @@
     turned_ref[0, terms * sector :] = jnp.where(row == 0, corr, jnp.where(row == 1, norm, 0.0))
 
 
-def arrive_kernel(terms, came_ref, turned_hbm, parts_hbm, moved_ref, sums_ref, marks, turned_ref, lefts_ref, sems):
+def arrive_kernel(terms, bounds, came_ref, turned_hbm, parts_hbm, *rest):
+    moved_refs, rest = rest[: len(bounds) - 1], rest[len(bounds) - 1 :]
+    rights_ref, sums_ref, marks, turned_ref, lefts_ref, sems = rest
     count, height, sector = came_ref.shape
     get_marks = pltpu.make_async_copy(came_ref.at[:, pl.ds(sector, height - sector)], marks, sems.at[0])
     get_lefts = pltpu.make_async_copy(parts_hbm.at[pl.ds(0, lefts_ref.shape[0])], lefts_ref, sems.at[1])
     get_turned = pltpu.make_async_copy(turned_hbm.at[pl.ds(0, count)], turned_ref, sems.at[2])
+    get_rights = pltpu.make_async_copy(parts_hbm.at[pl.ds(lefts_ref.shape[0], rights_ref.shape[0])], rights_ref, sems.at[3])
     get_marks.start()
     get_lefts.start()
     get_turned.start()
+    get_rights.start()
     get_marks.wait()
     get_lefts.wait()
     get_turned.wait()
 
-    def block(i, total):
+    def block(first, moved_ref, i, total):
         stack = [lefts_ref[marks[i, 0, g].astype(jnp.int32)] for g in range(terms)]
         moved = product(jnp.concatenate(stack, axis=0), doubled(came_ref[i, :sector]))
         for g in range(terms):
             part = slice(g * sector, (g + 1) * sector)
             one = moved[part] * marks[i, 0, terms + g]
-            moved_ref[i, part] = halves(one)
+            moved_ref[i - first, part] = halves(one)
             total += jnp.sum((one * turned_ref[i, part]).reshape(-1, SUB, sector), axis=0)
         return total
 
-    total = lax.fori_loop(0, count, block, jnp.zeros((SUB, sector), F32), unroll=4)
+    total = jnp.zeros((SUB, sector), F32)
+    for first, last, moved_ref in zip(bounds[:-1], bounds[1:], moved_refs):
+        total = lax.fori_loop(first, last, functools.partial(block, first, moved_ref), total, unroll=4)
     corr = jnp.sum(total, axis=0, keepdims=True)
     row = lax.broadcasted_iota(jnp.int32, total.shape, 0)
-    mine = turned_ref[0, terms * sector :] + jnp.where(row == 0, corr, 0.0)
-    for i in range(sums_ref.shape[0]):
-        sums_ref[i] = mine
-
-
-def remote_kernel(sums_hbm, rindex_ref, out_index_ref, moved_ref, turned_hbm, parts_hbm, hpsi_rows, acc, near_ref, rights_ref, sems):
-    slots, terms, _ = rindex_ref.shape
-    senders, height, _ = moved_ref.shape
+    sums_ref[...] = turned_ref[0, terms * sector :] + jnp.where(row == 0, corr, 0.0)
+    get_rights.wait()
+
+
+def remote_kernel(first, final, size, order_hbm, rindex_ref, out_index_ref, moved_ref, rights_ref, *rest):
+    slots, terms, peers = rindex_ref.shape
+    senders = slots * peers
+    height = moved_ref.shape[1]
     sector = height // terms
-    rights = rights_ref.shape[0]
-    get_rights = pltpu.make_async_copy(parts_hbm.at[pl.ds(parts_hbm.shape[0] - rights, rights)], rights_ref, sems.at[0])
-    get_rights.start()
-    slabs = []
-    for k in range(acc.shape[0] // height):
-        near = turned_hbm.at[senders + k, pl.ds(0, height)]
-        slabs.append(pltpu.make_async_copy(near, near_ref.at[pl.ds(k * height, height)], sems.at[1 + k]))
-        slabs[k].start()
-    acc[...] = jnp.zeros_like(acc)
-    get_rights.wait()
-
-    def right_step(i, carry):
+    before, rest = (rest[:1], rest[1:]) if first else ((), rest)
+    if final:
+        turned_hbm, out_ref, acc, near_ref, sems = rest
+        slabs = []
+        for k in range(size // height):
+            near = turned_hbm.at[senders + k, pl.ds(0, height)]
+            slabs.append(pltpu.make_async_copy(near, near_ref.at[pl.ds(k * height, height)], sems.at[k]))
+            slabs[k].start()
+    else:
+        (acc,) = rest
+    acc[...] = before[0][...] if before else jnp.zeros_like(acc)
+
+    def right_step(k, carry):
+        i = first + k
         for g in range(terms):
             right = rights_ref[rindex_ref[i % slots, g, i // slots]]
             spot = pl.multiple_of(out_index_ref[i % slots, g, i // slots] * sector, sector)
-            acc[pl.ds(spot, sector)] += product(moved_ref[i, g * sector : (g + 1) * sector], twice(right))
-        return carry
-
-    lax.fori_loop(0, senders, right_step, 0, unroll=4)
-    for copy in slabs:
-        copy.wait()
-    for b in range(acc.shape[0] // sector):
-        start = (b // SUB) * (SUB * sector) + b % SUB
-        part = slice(b * sector, (b + 1) * sector)
-        hpsi_rows[pl.ds(start, sector, stride=SUB), :] = acc[part] + near_ref[part]
+            acc[pl.ds(spot, sector)] += product(moved_ref[k, g * sector : (g + 1) * sector], twice(right))
+        return carry
+
+    lax.fori_loop(0, moved_ref.shape[0], right_step, 0, unroll=4)
+    if final:
+        for copy in slabs:
+            copy.wait()
+        for b in range(size // sector):
+            start = (b // SUB) * (SUB * sector) + b % SUB
+            part = slice(b * sector, (b + 1) * sector)
+            out_ref[pl.ds(start, sector, stride=SUB), :] = acc[part] + near_ref[part]
 
 
 def residual_kernel(sums_ref, hpsi_rows, psi_rows, hpsi_hbm, out_ref, sem):
     put = pltpu.make_async_copy(hpsi_rows, hpsi_hbm, sem)
     put.start()
-    total = jnp.sum(sums_ref[...], axis=0)
-    whole = jnp.sum(total, axis=1, keepdims=True)
+    whole = jnp.sum(sums_ref[...], axis=1, keepdims=True)
     theta = whole[0:1] / (whole[1:2] + 1e-06)
     out_ref[...] = hpsi_rows[...] - theta * psi_rows[...]
     put.wait()
@@ -302,54 +311,65 @@
         name="prepare",
     )(sent, *by_slot[2:], loc_block, loc_left, loc_right, psi_rows, right_rows, left_rows)
 
-    near_by = math.gcd(peers, 4)
+    rounds = max(peers.bit_length() - 1, 1)
     chunk = math.gcd(count, 16)
-    moved = []
+    share_of = max(rounds * chunk // count, 1)
+    bounds = [chunk * i // share_of for i in range(share_of + 1)]
+    pieces = []
     sums = 0.0
-    for first in range(0, count, chunk):
-        part = slice(first, first + chunk) if count > chunk else slice(None)
-        kept, share = pl.pallas_call(
-            lambda *refs: arrive_kernel(terms, *refs),
+    for base in range(0, count, chunk):
+        part = slice(base, base + chunk)
+        *kept, right_parts, share = pl.pallas_call(
+            lambda *refs: arrive_kernel(terms, bounds, *refs),
             out_shape=(
-                jax.ShapeDtypeStruct((chunk, terms * sector, 2 * sector), BF16),
-                jax.ShapeDtypeStruct((near_by, SUB, sector), F32),
+                *(
+                    jax.ShapeDtypeStruct((last - first, terms * sector, 2 * sector), BF16)
+                    for first, last in zip(bounds[:-1], bounds[1:])
+                ),
+                jax.ShapeDtypeStruct((rights, sector, 2 * sector), BF16),
+                jax.ShapeDtypeStruct((SUB, sector), F32),
             ),
             in_specs=[VMEM] + [HBM] * 2,
-            out_specs=(VMEM,) * 2,
+            out_specs=(VMEM,) * (share_of + 2),
             scratch_shapes=[
                 pltpu.SMEM((chunk, SUB, sector), F32),
                 pltpu.VMEM((chunk, terms * sector + SUB, sector), F32),
                 pltpu.VMEM((lefts, sector, 2 * sector), BF16),
-                pltpu.SemaphoreType.DMA((3,)),
+                pltpu.SemaphoreType.DMA((4,)),
             ],
-            compiler_params=roomy(50),
+            compiler_params=roomy(48),
             name="arrive",
-        )(came[part], turned if count == chunk else turned[part], parts)
-        moved.append(kept)
+        )(came if count == chunk else came[part], turned if count == chunk else turned[part], parts)
+        pieces += [(base + first, moved) for first, moved in zip(bounds, kept)]
         sums = share if count == chunk else sums + share
-    moved = moved[0] if len(moved) == 1 else jnp.concatenate(moved, axis=0)
-    together = [list(range(first, first + near_by)) for first in range(0, peers, near_by)]
-    across = [list(range(first, peers, near_by)) for first in range(near_by)]
-    totals = lax.all_to_all(sums, "renv", split_axis=0, concat_axis=0, tiled=True, axis_index_groups=together)
-    first_sums = jnp.sum(totals, axis=0)
-    totals = jnp.broadcast_to(first_sums[None], (peers // near_by, SUB, sector))
-    totals = lax.all_to_all(totals, "renv", split_axis=0, concat_axis=0, tiled=True, axis_index_groups=across)
-
-    hpsi_rows = pl.pallas_call(
-        remote_kernel,
-        out_shape=rows,
-        in_specs=[HBM] + [SMEM] * 2 + [VMEM] + [HBM] * 2,
-        out_specs=VMEM,
-        scratch_shapes=[
-            pltpu.VMEM(rows.shape, F32),
-            pltpu.VMEM(rows.shape, F32),
-            pltpu.VMEM((rights, sector, 2 * sector), BF16),
-            pltpu.SemaphoreType.DMA((1 + slabs,)),
-        ],
-        compiler_params=roomy(50),
-        cost_estimate=pl.CostEstimate(flops=4 * 10**9, bytes_accessed=6 * MIB, transcendentals=0),
-        name="remote_terms",
-    )(first_sums, *by_slot[2:], moved, turned, parts)
+
+    hpsi_rows = None
+    for number in range(max(rounds, len(pieces))):
+        got = None
+        if number < rounds:
+            step = 1 << number
+            got = lax.ppermute(sums, "renv", [(s, s ^ step) for s in range(peers)])
+        if number < len(pieces):
+            first, moved = pieces[number]
+            final = number == len(pieces) - 1
+            hpsi_rows = pl.pallas_call(
+                lambda *refs, first=first, final=final: remote_kernel(first, final, owned * sector, *refs),
+                out_shape=rows,
+                in_specs=[HBM] + [SMEM] * 2 + [VMEM] * (3 if first else 2) + [HBM] * final,
+                out_specs=VMEM,
+                scratch_shapes=[
+                    pltpu.VMEM(rows.shape, F32),
+                    pltpu.VMEM(rows.shape, F32),
+                    pltpu.SemaphoreType.DMA((slabs,)),
+                ]
+                * final,
+                input_output_aliases={} if final or not first else {5: 0},
+                compiler_params=roomy(50),
+                cost_estimate=pl.CostEstimate(flops=10**9, bytes_accessed=2 * MIB, transcendentals=0),
+                name=f"remote_terms_{number}",
+            )(sums, *by_slot[2:], moved, right_parts, *([hpsi_rows] if first else []), *([turned] if final else []))
+        if got is not None:
+            sums = sums + got
 
     hpsi, residual_rows = pl.pallas_call(
         residual_kernel,
@@ -359,7 +379,7 @@
         scratch_shapes=[pltpu.SemaphoreType.DMA],
         compiler_params=roomy(16),
         name="residual",
-    )(totals, hpsi_rows, psi_rows)
+    )(sums, hpsi_rows, psi_rows)
     return (from_rows(hpsi, owned), from_rows(residual_rows, owned))
 
 

time: 59.6 us -> 55.8 us (0.936)
  blocking collectives: 7.33 us -> 0 us
  starting transfers between devices: 12.9 us -> 17.1 us
  Pallas kernels: 23 us -> 24 us
  waiting for transfers between devices: 14.7 us -> 13.7 us
  local copies, waits for them, and re-layouts: 0.62 us -> 0.01 us
    ppermute x0 -> x4, starting transfers between devices: none -> 9.75 us  [shards(): got = lax.ppermute(sums, 'renv', [(s, s ^ step) for s in range(peers)])]
    all_to_all x1 -> x0, blocking collectives: 7.33 us -> none  [shards(): lax.all_to_all(sums, 'renv', split_axis=0, concat_axis=0, tiled=True, axi...]
    all_to_all x1 -> x0, starting transfers between devices: 5.54 us -> none  [shards(): lax.all_to_all(totals, 'renv', split_axis=0, concat_axis=0, tiled=True, a...]
    all_to_all x1 -> x0, waiting for transfers between devices: 2.33 us -> none  [shards(): lax.all_to_all(totals, 'renv', split_axis=0, concat_axis=0, tiled=True, a...]
    ppermute x0 -> x4, waiting for transfers between devices: none -> 1.3 us  [shards(): got = lax.ppermute(sums, 'renv', [(s, s ^ step) for s in range(peers)])]
    pallas_call x2 -> x5, Pallas kernels: 7.47 us -> 8.47 us  [the longest x4 4.73 us: shards(): pl.pallas_call(lambda *refs, first=first, final=final: remote_kernel(firs...]
    broadcast_in_dim x1 -> x0, local copies, waits for them, and re-layouts: 0.61 us -> none  [shards(): totals = jnp.broadcast_to(first_sums[None], (peers // near_by, SUB, sector))]
  transfers between devices with their start and end apart: 2 -> 5, of which waited for: 2 -> 3; matrix products, arithmetic and copies ran while one was open for 0% -> 0% of each run, Pallas kernels for 25% -> 29%
where the time goes in v2:
time: 55.8 us; the launch traced here: 55.6 us
  Pallas kernels  24 us (43%)
  starting transfers between devices  17.1 us (31%)
  waiting for transfers between devices  13.7 us (25%)
  between operations  0.74 us (1%)
    all_to_all x1, waiting for transfers between devices, shards(): lax.all_to_all(sent.reshape(peers, slots, height, sector), 'renv', split_...  12.4 us
    pallas_call x1, Pallas kernels, shards(): pl.pallas_call(prepare_kernel, out_shape=(jax.ShapeDtypeStruct((count + s...  11.6 us
    ppermute x4, starting transfers between devices, shards(): got = lax.ppermute(sums, 'renv', [(s, s ^ step) for s in range(peers)])  9.75 us
    all_to_all x1, starting transfers between devices, shards(): lax.all_to_all(sent.reshape(peers, slots, height, sector), 'renv', split_...  7.37 us
    pallas_call x4, Pallas kernels, shards(): pl.pallas_call(lambda *refs, first=first, final=final: remote_kernel(firs...  4.73 us
    pallas_call x1, Pallas kernels, shards(): pl.pallas_call(lambda *refs: arrive_kernel(terms, bounds, *refs), out_sha...  3.74 us
    pallas_call x1, Pallas kernels, shards(): pl.pallas_call(gather_kernel, out_shape=blocks, in_specs=[SMEM] * 3 + [VM...  2.28 us
    pallas_call x1, Pallas kernels, shards(): pl.pallas_call(residual_kernel, out_shape=(rows, rows), in_specs=[VMEM] *...  1.6 us
  transfers between devices with their start and end apart: 5, of which 3 were waited for; matrix products, arithmetic and copies ran while one was open for 0% of the time, Pallas kernels for 29%

profile of v2, /device:TPU:0, one launch (start us, length us, event | category | flops | bytes accessed | tf_op | source)
XLA Modules:
  0.0 55.6 jit_solution(18105234090047812782)
XLA Ops:
  0.6 2.3 %gather_blocks.1.sent_hbm = f32[16,136,128]{2,1,0:T(8,128)} custom-call(s32[16]{0:T(128)} %bitcast.53, s32[1,2,16]{2,1,0:T(2,128)} %bitcast.51, s32[1,2,16]{2,1,0:T(2,128)} %bitcast.52, f32[1024,128]{1,0:T(8,128)} %bitcast.34), custom_call_target="tpu_custom_call" | custom-call | tf_op jit(solution)/shard_map/gather_blocks/pallas_call | solution.py:282
  2.9 7.4 %all-to-all-start = ((f32[16,1,136,128]{3,2,1,0:T(8,128)}), f32[16,1,136,128]{3,2,1,0:T(8,128)S(1)}, u32[]{:S(2)}, u32[]{:S(2)}) async-start(f32[16,1,136,128]{3,2,1,0:T(8,128)} %bitcast.48), calls=%async_computation | async-start | bytes 2228224 | tf_op jit(solution)/shard_map/all_to_all | solution.py:291
  10.3 11.6 %prepare.1 = (f32[20,264,128]{2,1,0:T(8,128)}, bf16[80,128,256]{2,1,0:T(8,128)(2,1)}) custom-call(f32[16,136,128]{2,1,0:T(8,128)} %gather_blocks.1.sent_hbm, s32[1,2,16]{2,1,0:T(2,128)} %bitcast.38, s32[1,2,16]{2,1,0:T(2,128)} %bitcast.43, s32[32]{0:T(128)} %block_ref.1, s32[32]{0:T(128)} %left_ref.1, s32[32]{0:T(128)} %right_ref.1, f32[1024,128]{1,0:T(8,128)} %bitcast.35, ...), custom_call_target="tpu_custom_call" | custom-call | flops 1000000 | bytes 65536 | tf_op jit(solution)/shard_map/prepare/pallas_call | solution.py:295
  21.9 12.4 %all-to-all-done = f32[16,1,136,128]{3,2,1,0:T(8,128)S(1)} async-done(((f32[16,1,136,128]{3,2,1,0:T(8,128)}), f32[16,1,136,128]{3,2,1,0:T(8,128)S(1)}, u32[]{:S(2)}, u32[]{:S(2)}) %all-to-all-start) | async-done | bytes 1114144 | tf_op jit(solution)/shard_map/all_to_all | solution.py:291
  34.3 0.0 copy-start.1
  34.3 0.0 copy-start.2
  34.3 3.7 %arrive.1 = (bf16[4,256,256]{2,1,0:T(8,128)(2,1)S(1)}, bf16[4,256,256]{2,1,0:T(8,128)(2,1)S(1)}, bf16[4,256,256]{2,1,0:T(8,128)(2,1)S(1)}, bf16[4,256,256]{2,1,0...) custom-call(f32[16,136,128]{2,1,0:T(8,128)S(1)} %bitcast.37, ...), custom_call_target="tpu_custom_call" | custom-call | tf_op jit(solution)/shard_map/arrive/pallas_call | solution.py:322
  38.1 0.8 %collective-permute-start = (f32[8,128]{1,0:T(8,128)S(1)}, f32[8,128]{1,0:T(8,128)S(1)}, u32[]{:S(2)}, u32[]{:S(2)}) collective-permute-start(f32[8,128]{1,0:T(8,128)S(1)} %get-tuple-element.14.refs_0_), channel_id=1, source_target_pairs={{0,1},{1,0},{2,3},{3,2},{4,5},{5,4},{6,7},{7,6},{8,9},{9,8},{10,11... | collective-permute-start | bytes 12296 | tf_op jit(solution)/shard_map/ppermute | solution.py:351
  38.9 0.0 copy-done.1
  38.9 0.0 copy-done.2
  38.9 0.9 %remote_terms_0.1.refs_5_ = f32[1024,128]{1,0:T(8,128)S(1)} custom-call(f32[8,128]{1,0:T(8,128)S(1)} %get-tuple-element.14.refs_0_, s32[1,2,16]{2,1,0:T(2,128)S(1)} %bitcast.39, s32[1,2,16]{2,1,0:T(2,128)S(1)} %bitcast.44, bf16[4,256,256]{2,1,0:T(8,128)(2,1)S(1)} %get-tuple-element.19.refs_3_, bf16[16,128,256]{2,1,0:T(8,128)(2,1)S(1)} %get-tuple-element.16.refs_4_), custom_call_target="tpu_custom_call" | custom-call | flops 1000000000 | bytes 2097152 | tf_op jit(solution)/shard_map/remote_terms_0/pallas_call | solution.py:355
  39.8 0.0 collective-permute-done
  39.8 2.1 %collective-permute-start.1 = (f32[8,128]{1,0:T(8,128)S(1)}, f32[8,128]{1,0:T(8,128)S(1)}, u32[]{:S(2)}, u32[]{:S(2)}) collective-permute-start(f32[8,128]{1,0:T(8,128)S(1)} %add.12.refs_0_), channel_id=1, source_target_pairs={{0,2},{1,3},{2,0},{3,1},{4,6},{5,7},{6,4},{7,5},{8,10},{9,11},{10,... | collective-permute-start | bytes 12296 | tf_op jit(solution)/shard_map/ppermute | solution.py:351
  41.9 0.9 %remote_terms_1.1.refs_5_ = f32[1024,128]{1,0:T(8,128)S(1)} custom-call(f32[8,128]{1,0:T(8,128)S(1)} %add.12.refs_0_, s32[1,2,16]{2,1,0:T(2,128)S(1)} %bitcast.40, s32[1,2,16]{2,1,0:T(2,128)S(1)} %bitcast.45, bf16[4,256,256]{2,1,0:T(8,128)(2,1)S(1)} %get-tuple-element.18.refs_3_, ...), custom_call_target="tpu_custom_call", output_to_operand_aliasing={{}: (5, {})} | custom-call | flops 1000000000 | bytes 2097152 | tf_op jit(solution)/shard_map/remote_terms_1/pallas_call | solution.py:355
  42.8 0.7 %collective-permute-done.1 = f32[8,128]{1,0:T(8,128)S(1)} collective-permute-done((f32[8,128]{1,0:T(8,128)S(1)}, f32[8,128]{1,0:T(8,128)S(1)}, u32[]{:S(2)}, u32[]{:S(2)}) %collective-permute-start.1) | collective-permute-done | bytes 4128 | tf_op jit(solution)/shard_map/ppermute | solution.py:351
  43.5 3.5 %collective-permute-start.2 = (f32[8,128]{1,0:T(8,128)S(1)}, f32[8,128]{1,0:T(8,128)S(1)}, u32[]{:S(2)}, u32[]{:S(2)}) collective-permute-start(f32[8,128]{1,0:T(8,128)S(1)} %add.13.refs_0_), channel_id=1, source_target_pairs={{0,4},{1,5},{2,6},{3,7},{4,0},{5,1},{6,2},{7,3},{8,12},{9,13},{10,... | collective-permute-start | bytes 12296 | tf_op jit(solution)/shard_map/ppermute | solution.py:351
  47.0 0.9 %remote_terms_2.1.refs_5_ = f32[1024,128]{1,0:T(8,128)S(1)} custom-call(f32[8,128]{1,0:T(8,128)S(1)} %add.13.refs_0_, s32[1,2,16]{2,1,0:T(2,128)S(1)} %bitcast.41, s32[1,2,16]{2,1,0:T(2,128)S(1)} %bitcast.46, bf16[4,256,256]{2,1,0:T(8,128)(2,1)S(1)} %get-tuple-element.17.refs_3_, ...), custom_call_target="tpu_custom_call", output_to_operand_aliasing={{}: (5, {})} | custom-call | flops 1000000000 | bytes 2097152 | tf_op jit(solution)/shard_map/remote_terms_2/pallas_call | solution.py:355
  48.0 0.0 copy-start
  48.0 0.6 %collective-permute-done.2 = f32[8,128]{1,0:T(8,128)S(1)} collective-permute-done((f32[8,128]{1,0:T(8,128)S(1)}, f32[8,128]{1,0:T(8,128)S(1)}, u32[]{:S(2)}, u32[]{:S(2)}) %collective-permute-start.2) | collective-permute-done | bytes 4128 | tf_op jit(solution)/shard_map/ppermute | solution.py:351
  48.6 3.3 %collective-permute-start.3 = (f32[8,128]{1,0:T(8,128)S(1)}, f32[8,128]{1,0:T(8,128)S(1)}, u32[]{:S(2)}, u32[]{:S(2)}) collective-permute-start(f32[8,128]{1,0:T(8,128)S(1)} %add.14.refs_0_), channel_id=1, source_target_pairs={{0,8},{1,9},{2,10},{3,11},{4,12},{5,13},{6,14},{7,15},{8,0},{9,1},... | collective-permute-start | bytes 12296 | tf_op jit(solution)/shard_map/ppermute | solution.py:351
  51.9 2.0 %remote_terms_3.1.hpsi_rows = f32[1024,128]{1,0:T(8,128)S(1)} custom-call(f32[8,128]{1,0:T(8,128)S(1)} %add.14.refs_0_, s32[1,2,16]{2,1,0:T(2,128)S(1)} %bitcast.42, s32[1,2,16]{2,1,0:T(2,128)S(1)} %bitcast.47, bf16[4,256,256]{2,1,0:T(8,128)(2,1)S(1)} %get-tuple-element.15.refs_3_, bf16[16,128,256]{2,1,0:T(8,128)(2,1)S(1)} %get-tuple-element.16.refs_4_, ...), custom_call_target="tpu_custom_call" | custom-call | flops 1000000000 | bytes 2097152 | tf_op jit(solution)/shard_map/remote_terms_3/pallas_call | solution.py:355
  53.9 0.0 collective-permute-done.3
  53.9 0.0 copy-done
  54.0 1.6 %residual.1 = (f32[1024,128]{1,0:T(8,128)}, f32[1024,128]{1,0:T(8,128)}) custom-call(f32[8,128]{1,0:T(8,128)S(1)} %add.15.sums_ref, f32[1024,128]{1,0:T(8,128)S(1)} %remote_terms_3.1.hpsi_rows, f32[1024,128]{1,0:T(8,128)S(1)} %bitcast.36), custom_call_target="tpu_custom_call" | custom-call | tf_op jit(solution)/shard_map/residual/pallas_call | solution.py:374
  (4 shorter events, 0.0 us)
Async XLA Ops:
  2.9 31.4 %all-to-all-start = ((f32[16,1,136,128]{3,2,1,0:T(8,128)}), f32[16,1,136,128]{3,2,1,0:T(8,128)S(1)}, u32[]{:S(2)}, u32[]{:S(2)}) async-start(f32[16,1,136,128]{3,2,1,0:T(8,128)} %bitcast.48), calls=%async_computation | async-start | bytes 2228224 | tf_op jit(solution)/shard_map/all_to_all | solution.py:291
  34.3 4.6 %copy-start.1 = (s32[16,1,2]{0,2,1:T(2,128)S(1)}, s32[16,1,2]{0,2,1:T(2,128)}, u32[]{:S(2)}) copy-start(s32[16,1,2]{0,2,1:T(2,128)} %param.17) | copy-start | bytes 388
  34.3 4.6 %copy-start.2 = (s32[16,1,2]{0,2,1:T(2,128)S(1)}, s32[16,1,2]{0,2,1:T(2,128)}, u32[]{:S(2)}) copy-start(s32[16,1,2]{0,2,1:T(2,128)} %param.18) | copy-start | bytes 388
  38.1 1.7 %collective-permute-start = (f32[8,128]{1,0:T(8,128)S(1)}, f32[8,128]{1,0:T(8,128)S(1)}, u32[]{:S(2)}, u32[]{:S(2)}) collective-permute-start(f32[8,128]{1,0:T(8,128)S(1)} %get-tuple-element.14.refs_0_), channel_id=1, source_target_pairs={{0,1},{1,0},{2,3},{3,2},{4,5},{5,4},{6,7},{7,6},{8,9},{9,8},{10,11... | collective-permute-start | bytes 12296 | tf_op jit(solution)/shard_map/ppermute | solution.py:351
  39.8 3.7 %collective-permute-start.1 = (f32[8,128]{1,0:T(8,128)S(1)}, f32[8,128]{1,0:T(8,128)S(1)}, u32[]{:S(2)}, u32[]{:S(2)}) collective-permute-start(f32[8,128]{1,0:T(8,128)S(1)} %add.12.refs_0_), channel_id=1, source_target_pairs={{0,2},{1,3},{2,0},{3,1},{4,6},{5,7},{6,4},{7,5},{8,10},{9,11},{10,... | collective-permute-start | bytes 12296 | tf_op jit(solution)/shard_map/ppermute | solution.py:351
  43.5 5.1 %collective-permute-start.2 = (f32[8,128]{1,0:T(8,128)S(1)}, f32[8,128]{1,0:T(8,128)S(1)}, u32[]{:S(2)}, u32[]{:S(2)}) collective-permute-start(f32[8,128]{1,0:T(8,128)S(1)} %add.13.refs_0_), channel_id=1, source_target_pairs={{0,4},{1,5},{2,6},{3,7},{4,0},{5,1},{6,2},{7,3},{8,12},{9,13},{10,... | collective-permute-start | bytes 12296 | tf_op jit(solution)/shard_map/ppermute | solution.py:351
  48.0 6.0 %copy-start = (f32[8,16384]{1,0:T(8,128)S(1)}, f32[8,16384]{1,0:T(8,128)}, u32[]{:S(2)}) copy-start(f32[8,16384]{1,0:T(8,128)} %param.11) | copy-start | bytes 1572868
  48.6 5.3 %collective-permute-start.3 = (f32[8,128]{1,0:T(8,128)S(1)}, f32[8,128]{1,0:T(8,128)S(1)}, u32[]{:S(2)}, u32[]{:S(2)}) collective-permute-start(f32[8,128]{1,0:T(8,128)S(1)} %add.14.refs_0_), channel_id=1, source_target_pairs={{0,8},{1,9},{2,10},{3,11},{4,12},{5,13},{6,14},{7,15},{8,0},{9,1},... | collective-permute-start | bytes 12296 | tf_op jit(solution)/shard_map/ppermute | solution.py:351

commit v3 on v1

--- a/solution.py
+++ b/solution.py
@@ -192,15 +192,18 @@
             total += jnp.sum((one * turned_ref[i, part]).reshape(-1, SUB, sector), axis=0)
         return total
 
-    total = lax.fori_loop(0, count, block, jnp.zeros((SUB, sector), F32), unroll=4)
+    total = lax.fori_loop(0, count, block, jnp.zeros((SUB, sector), F32), unroll=16)
     corr = jnp.sum(total, axis=0, keepdims=True)
     row = lax.broadcasted_iota(jnp.int32, total.shape, 0)
     mine = turned_ref[0, terms * sector :] + jnp.where(row == 0, corr, 0.0)
+    folded = mine + pltpu.roll(mine, sector // 2, 1)
+    lane = lax.broadcasted_iota(jnp.int32, (1, sector), 1)
+    shared = jnp.where(lane < sector // 2, folded[0:1], folded[1:2])
     for i in range(sums_ref.shape[0]):
-        sums_ref[i] = mine
-
-
-def remote_kernel(sums_hbm, rindex_ref, out_index_ref, moved_ref, turned_hbm, parts_hbm, hpsi_rows, acc, near_ref, rights_ref, sems):
+        sums_ref[i] = shared
+
+
+def remote_kernel(rindex_ref, out_index_ref, moved_ref, turned_hbm, parts_hbm, hpsi_rows, acc, near_ref, rights_ref, sems):
     slots, terms, _ = rindex_ref.shape
     senders, height, _ = moved_ref.shape
     sector = height // terms
@@ -235,8 +238,11 @@
     put = pltpu.make_async_copy(hpsi_rows, hpsi_hbm, sem)
     put.start()
     total = jnp.sum(sums_ref[...], axis=0)
-    whole = jnp.sum(total, axis=1, keepdims=True)
-    theta = whole[0:1] / (whole[1:2] + 1e-06)
+    lane = lax.broadcasted_iota(jnp.int32, total.shape, 1)
+    first = lane < total.shape[1] // 2
+    corr = jnp.sum(jnp.where(first, total, 0.0), axis=1, keepdims=True)
+    norm = jnp.sum(jnp.where(first, 0.0, total), axis=1, keepdims=True)
+    theta = corr / (norm + 1e-06)
     out_ref[...] = hpsi_rows[...] - theta * psi_rows[...]
     put.wait()
 
@@ -302,7 +308,6 @@
         name="prepare",
     )(sent, *by_slot[2:], loc_block, loc_left, loc_right, psi_rows, right_rows, left_rows)
 
-    near_by = math.gcd(peers, 4)
     chunk = math.gcd(count, 16)
     moved = []
     sums = 0.0
@@ -312,7 +317,7 @@
             lambda *refs: arrive_kernel(terms, *refs),
             out_shape=(
                 jax.ShapeDtypeStruct((chunk, terms * sector, 2 * sector), BF16),
-                jax.ShapeDtypeStruct((near_by, SUB, sector), F32),
+                jax.ShapeDtypeStruct((peers, 1, sector), F32),
             ),
             in_specs=[VMEM] + [HBM] * 2,
             out_specs=(VMEM,) * 2,
@@ -328,17 +333,12 @@
         moved.append(kept)
         sums = share if count == chunk else sums + share
     moved = moved[0] if len(moved) == 1 else jnp.concatenate(moved, axis=0)
-    together = [list(range(first, first + near_by)) for first in range(0, peers, near_by)]
-    across = [list(range(first, peers, near_by)) for first in range(near_by)]
-    totals = lax.all_to_all(sums, "renv", split_axis=0, concat_axis=0, tiled=True, axis_index_groups=together)
-    first_sums = jnp.sum(totals, axis=0)
-    totals = jnp.broadcast_to(first_sums[None], (peers // near_by, SUB, sector))
-    totals = lax.all_to_all(totals, "renv", split_axis=0, concat_axis=0, tiled=True, axis_index_groups=across)
+    totals = lax.all_to_all(sums, "renv", split_axis=0, concat_axis=0, tiled=True)
 
     hpsi_rows = pl.pallas_call(
         remote_kernel,
         out_shape=rows,
-        in_specs=[HBM] + [SMEM] * 2 + [VMEM] + [HBM] * 2,
+        in_specs=[SMEM] * 2 + [VMEM] + [HBM] * 2,
         out_specs=VMEM,
         scratch_shapes=[
             pltpu.VMEM(rows.shape, F32),
@@ -349,7 +349,7 @@
         compiler_params=roomy(50),
         cost_estimate=pl.CostEstimate(flops=4 * 10**9, bytes_accessed=6 * MIB, transcendentals=0),
         name="remote_terms",
-    )(first_sums, *by_slot[2:], moved, turned, parts)
+    )(*by_slot[2:], moved, turned, parts)
 
     hpsi, residual_rows = pl.pallas_call(
         residual_kernel,

time: 59.6 us -> 54.2 us (0.909)
  blocking collectives: 7.33 us -> 0 us
  starting transfers between devices: 12.9 us -> 14.6 us
  waiting for transfers between devices: 14.7 us -> 15.4 us
  local copies, waits for them, and re-layouts: 0.62 us -> 0.01 us
    all_to_all x1 -> x0, blocking collectives: 7.33 us -> none  [shards(): lax.all_to_all(sums, 'renv', split_axis=0, concat_axis=0, tiled=True, axi...]
    all_to_all x1, starting transfers between devices: 5.54 us -> 7.19 us  [shards(): lax.all_to_all(sums, 'renv', split_axis=0, concat_axis=0, tiled=True)]
    all_to_all x1, waiting for transfers between devices: 2.33 us -> 3.03 us  [shards(): lax.all_to_all(sums, 'renv', split_axis=0, concat_axis=0, tiled=True)]
    broadcast_in_dim x1 -> x0, local copies, waits for them, and re-layouts: 0.61 us -> none  [shards(): totals = jnp.broadcast_to(first_sums[None], (peers // near_by, SUB, sector))]
  transfers between devices with their start and end apart: 2 -> 2, of which waited for: 2 -> 2; matrix products, arithmetic and copies ran while one was open for 0% -> 0% of each run, Pallas kernels for 25% -> 28%
where the time goes in v3:
time: 54.2 us; the launch traced here: 53.9 us
  Pallas kernels  23.3 us (43%)
  waiting for transfers between devices  15.4 us (28%)
  starting transfers between devices  14.6 us (27%)
  between operations  0.7 us (1%)
    all_to_all x1, waiting for transfers between devices, shards(): lax.all_to_all(sent.reshape(peers, slots, height, sector), 'renv', split_...  12.4 us
    pallas_call x1, Pallas kernels, shards(): pl.pallas_call(prepare_kernel, out_shape=(jax.ShapeDtypeStruct((count + s...  11.7 us
    all_to_all x1, starting transfers between devices, shards(): lax.all_to_all(sent.reshape(peers, slots, height, sector), 'renv', split_...  7.37 us
    all_to_all x1, starting transfers between devices, shards(): lax.all_to_all(sums, 'renv', split_axis=0, concat_axis=0, tiled=True)  7.19 us
    pallas_call x1, Pallas kernels, shards(): pl.pallas_call(lambda *refs: arrive_kernel(terms, *refs), out_shape=(jax....  4.48 us
    pallas_call x1, Pallas kernels, shards(): pl.pallas_call(remote_kernel, out_shape=rows, in_specs=[SMEM] * 2 + [VMEM...  3.26 us
    all_to_all x1, waiting for transfers between devices, shards(): lax.all_to_all(sums, 'renv', split_axis=0, concat_axis=0, tiled=True)  3.03 us
    pallas_call x1, Pallas kernels, shards(): pl.pallas_call(gather_kernel, out_shape=blocks, in_specs=[SMEM] * 3 + [VM...  2.28 us
  transfers between devices with their start and end apart: 2, of which 2 were waited for; matrix products, arithmetic and copies ran while one was open for 0% of the time, Pallas kernels for 28%

profile of v3, /device:TPU:0, one launch (start us, length us, event | category | flops | bytes accessed | tf_op | source)
XLA Modules:
  0.0 53.9 jit_solution(74251153288393016)
XLA Ops:
  0.6 2.3 %gather_blocks.1.sent_hbm = f32[16,136,128]{2,1,0:T(8,128)} custom-call(s32[16]{0:T(128)} %bitcast.47, s32[1,2,16]{2,1,0:T(2,128)} %bitcast.45, s32[1,2,16]{2,1,0:T(2,128)} %bitcast.46, f32[1024,128]{1,0:T(8,128)} %bitcast.34), custom_call_target="tpu_custom_call" | custom-call | tf_op jit(solution)/shard_map/gather_blocks/pallas_call | solution.py:279
  2.9 7.4 %all-to-all-start = ((f32[16,1,136,128]{3,2,1,0:T(8,128)}), f32[16,1,136,128]{3,2,1,0:T(8,128)S(1)}, u32[]{:S(2)}, u32[]{:S(2)}) async-start(f32[16,1,136,128]{3,2,1,0:T(8,128)} %bitcast.42), calls=%async_computation | async-start | bytes 2228224 | tf_op jit(solution)/shard_map/all_to_all | solution.py:288
  10.3 11.7 %prepare.1 = (f32[20,264,128]{2,1,0:T(8,128)}, bf16[80,128,256]{2,1,0:T(8,128)(2,1)}) custom-call(f32[16,136,128]{2,1,0:T(8,128)} %gather_blocks.1.sent_hbm, s32[1,2,16]{2,1,0:T(2,128)} %bitcast.38, s32[1,2,16]{2,1,0:T(2,128)} %bitcast.40, s32[32]{0:T(128)} %block_ref.1, s32[32]{0:T(128)} %left_ref.1, s32[32]{0:T(128)} %right_ref.1, f32[1024,128]{1,0:T(8,128)} %bitcast.35, ...), custom_call_target="tpu_custom_call" | custom-call | flops 1000000 | bytes 65536 | tf_op jit(solution)/shard_map/prepare/pallas_call | solution.py:292
  21.9 12.4 %all-to-all-done = f32[16,1,136,128]{3,2,1,0:T(8,128)S(1)} async-done(((f32[16,1,136,128]{3,2,1,0:T(8,128)}), f32[16,1,136,128]{3,2,1,0:T(8,128)S(1)}, u32[]{:S(2)}, u32[]{:S(2)}) %all-to-all-start) | async-done | bytes 1114144 | tf_op jit(solution)/shard_map/all_to_all | solution.py:288
  34.3 0.0 copy-start.1
  34.3 0.0 copy-start.2
  34.3 4.5 %arrive.1 = (bf16[16,256,256]{2,1,0:T(8,128)(2,1)S(1)}, f32[16,1,128]{2,1,0:T(1,128)}) custom-call(f32[16,136,128]{2,1,0:T(8,128)S(1)} %bitcast.37, f32[20,264,128]{2,1,0:T(8,128)} %get-tuple-element.8.refs_1_.turned_hbm, bf16[80,128,256]{2,1,0:T(8,128)(2,1)} %get-tuple-element.9.refs_2_.parts_hbm), custom_call_target="tpu_custom_call" | custom-call | tf_op jit(solution)/shard_map/arrive/pallas_call | solution.py:316
  38.8 7.2 %all-to-all-start.1 = ((f32[16,1,128]{2,1,0:T(1,128)}), f32[16,1,128]{2,1,0:T(1,128)S(1)}, u32[]{:S(2)}, u32[]{:S(2)}) async-start(f32[16,1,128]{2,1,0:T(1,128)} %get-tuple-element.10), calls=%async_computation.1 | async-start | bytes 16384 | tf_op jit(solution)/shard_map/all_to_all | solution.py:336
  46.0 0.0 copy-done.1
  46.0 0.0 copy-done.2
  46.0 0.0 copy-start
  46.0 3.3 %remote_terms.1.hpsi_rows = f32[1024,128]{1,0:T(8,128)S(1)} custom-call(s32[1,2,16]{2,1,0:T(2,128)S(1)} %bitcast.39, s32[1,2,16]{2,1,0:T(2,128)S(1)} %bitcast.41, bf16[16,256,256]{2,1,0:T(8,128)(2,1)S(1)} %get-tuple-element.11.moved_ref, f32[20,264,128]{2,1,0:T(8,128)} %get-tuple-element.8.refs_1_.turned_hbm, ...), custom_call_target="tpu_custom_call" | custom-call | flops 4000000000 | bytes 6291456 | tf_op jit(solution)/shard_map/remote_terms/pallas_call | solution.py:338
  49.3 3.0 %all-to-all-done.1.sums_ref = f32[16,1,128]{2,1,0:T(1,128)S(1)} async-done(((f32[16,1,128]{2,1,0:T(1,128)}), f32[16,1,128]{2,1,0:T(1,128)S(1)}, u32[]{:S(2)}, u32[]{:S(2)}) %all-to-all-start.1) | async-done | bytes 8224 | tf_op jit(solution)/shard_map/all_to_all | solution.py:336
  52.3 0.0 copy-done
  52.3 1.6 %residual.1 = (f32[1024,128]{1,0:T(8,128)}, f32[1024,128]{1,0:T(8,128)}) custom-call(f32[16,1,128]{2,1,0:T(1,128)S(1)} %all-to-all-done.1.sums_ref, f32[1024,128]{1,0:T(8,128)S(1)} %remote_terms.1.hpsi_rows, f32[1024,128]{1,0:T(8,128)S(1)} %bitcast.36), custom_call_target="tpu_custom_call" | custom-call | tf_op jit(solution)/shard_map/residual/pallas_call | solution.py:354
Async XLA Ops:
  2.9 31.4 %all-to-all-start = ((f32[16,1,136,128]{3,2,1,0:T(8,128)}), f32[16,1,136,128]{3,2,1,0:T(8,128)S(1)}, u32[]{:S(2)}, u32[]{:S(2)}) async-start(f32[16,1,136,128]{3,2,1,0:T(8,128)} %bitcast.42), calls=%async_computation | async-start | bytes 2228224 | tf_op jit(solution)/shard_map/all_to_all | solution.py:288
  34.3 11.7 %copy-start.1 = (s32[16,1,2]{0,2,1:T(2,128)S(1)}, s32[16,1,2]{0,2,1:T(2,128)}, u32[]{:S(2)}) copy-start(s32[16,1,2]{0,2,1:T(2,128)} %param.17) | copy-start | bytes 388
  34.3 11.7 %copy-start.2 = (s32[16,1,2]{0,2,1:T(2,128)S(1)}, s32[16,1,2]{0,2,1:T(2,128)}, u32[]{:S(2)}) copy-start(s32[16,1,2]{0,2,1:T(2,128)} %param.18) | copy-start | bytes 388
  38.8 13.5 %all-to-all-start.1 = ((f32[16,1,128]{2,1,0:T(1,128)}), f32[16,1,128]{2,1,0:T(1,128)S(1)}, u32[]{:S(2)}, u32[]{:S(2)}) async-start(f32[16,1,128]{2,1,0:T(1,128)} %get-tuple-element.10), calls=%async_computation.1 | async-start | bytes 16384 | tf_op jit(solution)/shard_map/all_to_all | solution.py:336
  46.0 6.3 %copy-start = (f32[8,16384]{1,0:T(8,128)S(1)}, f32[8,16384]{1,0:T(8,128)}, u32[]{:S(2)}) copy-start(f32[8,16384]{1,0:T(8,128)} %param.11) | copy-start | bytes 1572868

commit v4 on v3

--- a/solution.py
+++ b/solution.py
@@ -170,21 +170,29 @@
     turned_ref[0, terms * sector :] = jnp.where(row == 0, corr, jnp.where(row == 1, norm, 0.0))
 
 
-def arrive_kernel(terms, came_ref, turned_hbm, parts_hbm, moved_ref, sums_ref, marks, turned_ref, lefts_ref, sems):
+def arrive_kernel(terms, came_ref, turned_hbm, parts_hbm, moved_ref, sums_ref, marks, turned_ref, lefts_ref, weights_ref, sems):
     count, height, sector = came_ref.shape
     get_marks = pltpu.make_async_copy(came_ref.at[:, pl.ds(sector, height - sector)], marks, sems.at[0])
     get_lefts = pltpu.make_async_copy(parts_hbm.at[pl.ds(0, lefts_ref.shape[0])], lefts_ref, sems.at[1])
-    get_turned = pltpu.make_async_copy(turned_hbm.at[pl.ds(0, count)], turned_ref, sems.at[2])
-    get_marks.start()
-    get_lefts.start()
-    get_turned.start()
+    quarter = count // math.gcd(count, 4)
+    spans = [pl.ds(first, quarter) for first in range(0, count, quarter)]
+    get_turned = [
+        pltpu.make_async_copy(turned_hbm.at[span], turned_ref.at[span], sems.at[2 + k]) for k, span in enumerate(spans)
+    ]
+    for copy in (get_marks, get_lefts, *get_turned):
+        copy.start()
+
+    def split(i, carry):
+        weights_ref[i] = doubled(came_ref[i, :sector])
+        return carry
+
+    lax.fori_loop(0, count, split, 0, unroll=4)
     get_marks.wait()
     get_lefts.wait()
-    get_turned.wait()
 
     def block(i, total):
         stack = [lefts_ref[marks[i, 0, g].astype(jnp.int32)] for g in range(terms)]
-        moved = product(jnp.concatenate(stack, axis=0), doubled(came_ref[i, :sector]))
+        moved = product(jnp.concatenate(stack, axis=0), weights_ref[i])
         for g in range(terms):
             part = slice(g * sector, (g + 1) * sector)
             one = moved[part] * marks[i, 0, terms + g]
@@ -192,7 +200,10 @@
             total += jnp.sum((one * turned_ref[i, part]).reshape(-1, SUB, sector), axis=0)
         return total
 
-    total = lax.fori_loop(0, count, block, jnp.zeros((SUB, sector), F32), unroll=16)
+    total = jnp.zeros((SUB, sector), F32)
+    for k, copy in enumerate(get_turned):
+        copy.wait()
+        total = lax.fori_loop(k * quarter, (k + 1) * quarter, block, total, unroll=4)
     corr = jnp.sum(total, axis=0, keepdims=True)
     row = lax.broadcasted_iota(jnp.int32, total.shape, 0)
     mine = turned_ref[0, terms * sector :] + jnp.where(row == 0, corr, 0.0)
@@ -203,7 +214,7 @@
         sums_ref[i] = shared
 
 
-def remote_kernel(rindex_ref, out_index_ref, moved_ref, turned_hbm, parts_hbm, hpsi_rows, acc, near_ref, rights_ref, sems):
+def remote_kernel(rindex_ref, out_index_ref, moved_ref, turned_hbm, parts_hbm, hpsi_rows, hpsi_hbm, acc, near_ref, rights_ref, sems):
     slots, terms, _ = rindex_ref.shape
     senders, height, _ = moved_ref.shape
     sector = height // terms
@@ -232,11 +243,12 @@
         start = (b // SUB) * (SUB * sector) + b % SUB
         part = slice(b * sector, (b + 1) * sector)
         hpsi_rows[pl.ds(start, sector, stride=SUB), :] = acc[part] + near_ref[part]
-
-
-def residual_kernel(sums_ref, hpsi_rows, psi_rows, hpsi_hbm, out_ref, sem):
-    put = pltpu.make_async_copy(hpsi_rows, hpsi_hbm, sem)
+    put = pltpu.make_async_copy(hpsi_rows, hpsi_hbm, sems.at[0])
     put.start()
+    put.wait()
+
+
+def residual_kernel(sums_ref, hpsi_rows, psi_rows, out_ref):
     total = jnp.sum(sums_ref[...], axis=0)
     lane = lax.broadcasted_iota(jnp.int32, total.shape, 1)
     first = lane < total.shape[1] // 2
@@ -244,7 +256,6 @@
     norm = jnp.sum(jnp.where(first, 0.0, total), axis=1, keepdims=True)
     theta = corr / (norm + 1e-06)
     out_ref[...] = hpsi_rows[...] - theta * psi_rows[...]
-    put.wait()
 
 
 def shards(
@@ -325,7 +336,8 @@
                 pltpu.SMEM((chunk, SUB, sector), F32),
                 pltpu.VMEM((chunk, terms * sector + SUB, sector), F32),
                 pltpu.VMEM((lefts, sector, 2 * sector), BF16),
-                pltpu.SemaphoreType.DMA((3,)),
+                pltpu.VMEM((chunk, 2 * sector, 2 * sector), BF16),
+                pltpu.SemaphoreType.DMA((6,)),
             ],
             compiler_params=roomy(50),
             name="arrive",
@@ -335,11 +347,11 @@
     moved = moved[0] if len(moved) == 1 else jnp.concatenate(moved, axis=0)
     totals = lax.all_to_all(sums, "renv", split_axis=0, concat_axis=0, tiled=True)
 
-    hpsi_rows = pl.pallas_call(
+    hpsi_rows, hpsi = pl.pallas_call(
         remote_kernel,
-        out_shape=rows,
+        out_shape=(rows, rows),
         in_specs=[SMEM] * 2 + [VMEM] + [HBM] * 2,
-        out_specs=VMEM,
+        out_specs=(VMEM, HBM),
         scratch_shapes=[
             pltpu.VMEM(rows.shape, F32),
             pltpu.VMEM(rows.shape, F32),
@@ -351,12 +363,11 @@
         name="remote_terms",
     )(*by_slot[2:], moved, turned, parts)
 
-    hpsi, residual_rows = pl.pallas_call(
+    residual_rows = pl.pallas_call(
         residual_kernel,
-        out_shape=(rows, rows),
+        out_shape=rows,
         in_specs=[VMEM] * 3,
-        out_specs=(HBM, VMEM),
-        scratch_shapes=[pltpu.SemaphoreType.DMA],
+        out_specs=VMEM,
         compiler_params=roomy(16),
         name="residual",
     )(totals, hpsi_rows, psi_rows)

time: 54.2 us -> 53.5 us (0.987)
  waiting for transfers between devices: 15.4 us -> 14.6 us
    all_to_all x1, waiting for transfers between devices: 3.03 us -> 2.25 us  [shards(): lax.all_to_all(sums, 'renv', split_axis=0, concat_axis=0, tiled=True)]
  transfers between devices with their start and end apart: 2 -> 2, of which waited for: 2 -> 2; matrix products, arithmetic and copies ran while one was open for 0% -> 0% of each run, Pallas kernels for 28% -> 29%
where the time goes in v4:
time: 53.5 us; the launch traced here: 53.2 us
  Pallas kernels  23.3 us (44%)
  starting transfers between devices  14.6 us (27%)
  waiting for transfers between devices  14.6 us (27%)
  between operations  0.7 us (1%)
    all_to_all x1, waiting for transfers between devices, shards(): lax.all_to_all(sent.reshape(peers, slots, height, sector), 'renv', split_...  12.4 us
    pallas_call x1, Pallas kernels, shards(): pl.pallas_call(prepare_kernel, out_shape=(jax.ShapeDtypeStruct((count + s...  11.6 us
    all_to_all x1, starting transfers between devices, shards(): lax.all_to_all(sent.reshape(peers, slots, height, sector), 'renv', split_...  7.37 us
    all_to_all x1, starting transfers between devices, shards(): lax.all_to_all(sums, 'renv', split_axis=0, concat_axis=0, tiled=True)  7.2 us
    pallas_call x1, Pallas kernels, shards(): pl.pallas_call(lambda *refs: arrive_kernel(terms, *refs), out_shape=(jax....  4.31 us
    pallas_call x1, Pallas kernels, shards(): pl.pallas_call(remote_kernel, out_shape=(rows, rows), in_specs=[SMEM] * 2...  4.04 us
    pallas_call x1, Pallas kernels, shards(): pl.pallas_call(gather_kernel, out_shape=blocks, in_specs=[SMEM] * 3 + [VM...  2.28 us
    all_to_all x1, waiting for transfers between devices, shards(): lax.all_to_all(sums, 'renv', split_axis=0, concat_axis=0, tiled=True)  2.25 us
  transfers between devices with their start and end apart: 2, of which 2 were waited for; matrix products, arithmetic and copies ran while one was open for 0% of the time, Pallas kernels for 29%

profile of v4, /device:TPU:0, one launch (start us, length us, event | category | flops | bytes accessed | tf_op | source)
XLA Modules:
  0.0 53.2 jit_solution(10093218952220831987)
XLA Ops:
  0.6 2.3 %gather_blocks.1.sent_hbm = f32[16,136,128]{2,1,0:T(8,128)} custom-call(s32[16]{0:T(128)} %bitcast.48, s32[1,2,16]{2,1,0:T(2,128)} %bitcast.46, s32[1,2,16]{2,1,0:T(2,128)} %bitcast.47, f32[1024,128]{1,0:T(8,128)} %bitcast.34), custom_call_target="tpu_custom_call" | custom-call | tf_op jit(solution)/shard_map/gather_blocks/pallas_call | solution.py:290
  2.9 7.4 %all-to-all-start = ((f32[16,1,136,128]{3,2,1,0:T(8,128)}), f32[16,1,136,128]{3,2,1,0:T(8,128)S(1)}, u32[]{:S(2)}, u32[]{:S(2)}) async-start(f32[16,1,136,128]{3,2,1,0:T(8,128)} %bitcast.42), calls=%async_computation | async-start | bytes 2228224 | tf_op jit(solution)/shard_map/all_to_all | solution.py:299
  10.3 11.6 %prepare.1 = (f32[20,264,128]{2,1,0:T(8,128)}, bf16[80,128,256]{2,1,0:T(8,128)(2,1)}) custom-call(f32[16,136,128]{2,1,0:T(8,128)} %gather_blocks.1.sent_hbm, s32[1,2,16]{2,1,0:T(2,128)} %bitcast.38, s32[1,2,16]{2,1,0:T(2,128)} %bitcast.40, s32[32]{0:T(128)} %block_ref.1, s32[32]{0:T(128)} %left_ref.1, s32[32]{0:T(128)} %right_ref.1, f32[1024,128]{1,0:T(8,128)} %bitcast.35, ...), custom_call_target="tpu_custom_call" | custom-call | flops 1000000 | bytes 65536 | tf_op jit(solution)/shard_map/prepare/pallas_call | solution.py:303
  21.9 12.4 %all-to-all-done = f32[16,1,136,128]{3,2,1,0:T(8,128)S(1)} async-done(((f32[16,1,136,128]{3,2,1,0:T(8,128)}), f32[16,1,136,128]{3,2,1,0:T(8,128)S(1)}, u32[]{:S(2)}, u32[]{:S(2)}) %all-to-all-start) | async-done | bytes 1114144 | tf_op jit(solution)/shard_map/all_to_all | solution.py:299
  34.3 0.0 copy-start.1
  34.3 0.0 copy-start.2
  34.3 4.3 %arrive.1 = (bf16[16,256,256]{2,1,0:T(8,128)(2,1)S(1)}, f32[16,1,128]{2,1,0:T(1,128)}) custom-call(f32[16,136,128]{2,1,0:T(8,128)S(1)} %bitcast.37, f32[20,264,128]{2,1,0:T(8,128)} %get-tuple-element.8.refs_1_.turned_hbm, bf16[80,128,256]{2,1,0:T(8,128)(2,1)} %get-tuple-element.9.refs_2_.parts_hbm), custom_call_target="tpu_custom_call" | custom-call | tf_op jit(solution)/shard_map/arrive/pallas_call | solution.py:327
  38.6 7.2 %all-to-all-start.1 = ((f32[16,1,128]{2,1,0:T(1,128)}), f32[16,1,128]{2,1,0:T(1,128)S(1)}, u32[]{:S(2)}, u32[]{:S(2)}) async-start(f32[16,1,128]{2,1,0:T(1,128)} %get-tuple-element.12), calls=%async_computation.1 | async-start | bytes 16384 | tf_op jit(solution)/shard_map/all_to_all | solution.py:348
  45.8 0.0 copy-done.1
  45.9 0.0 copy-done.2
  45.9 0.0 copy-start
  45.9 4.0 %remote_terms.1 = (f32[1024,128]{1,0:T(8,128)S(1)}, f32[1024,128]{1,0:T(8,128)}) custom-call(s32[1,2,16]{2,1,0:T(2,128)S(1)} %bitcast.39, s32[1,2,16]{2,1,0:T(2,128)S(1)} %bitcast.41, bf16[16,256,256]{2,1,0:T(8,128)(2,1)S(1)} %get-tuple-element.10.moved_ref, f32[20,264,128]{2,1,0:T(8,128)} %get-tuple-element.8.refs_1_.turned_hbm, ...), custom_call_target="tpu_custom_call" | custom-call | flops 4000000000 | bytes 6291456 | tf_op jit(solution)/shard_map/remote_terms/pallas_call | solution.py:350
  49.9 2.2 %all-to-all-done.1.sums_ref = f32[16,1,128]{2,1,0:T(1,128)S(1)} async-done(((f32[16,1,128]{2,1,0:T(1,128)}), f32[16,1,128]{2,1,0:T(1,128)S(1)}, u32[]{:S(2)}, u32[]{:S(2)}) %all-to-all-start.1) | async-done | bytes 8224 | tf_op jit(solution)/shard_map/all_to_all | solution.py:348
  52.2 0.0 copy-done
  52.2 1.0 %residual.1 = f32[1024,128]{1,0:T(8,128)} custom-call(f32[16,1,128]{2,1,0:T(1,128)S(1)} %all-to-all-done.1.sums_ref, f32[1024,128]{1,0:T(8,128)S(1)} %get-tuple-element.13.hpsi_rows, f32[1024,128]{1,0:T(8,128)S(1)} %bitcast.36), custom_call_target="tpu_custom_call" | custom-call | tf_op jit(solution)/shard_map/residual/pallas_call | solution.py:366
Async XLA Ops:
  2.9 31.4 %all-to-all-start = ((f32[16,1,136,128]{3,2,1,0:T(8,128)}), f32[16,1,136,128]{3,2,1,0:T(8,128)S(1)}, u32[]{:S(2)}, u32[]{:S(2)}) async-start(f32[16,1,136,128]{3,2,1,0:T(8,128)} %bitcast.42), calls=%async_computation | async-start | bytes 2228224 | tf_op jit(solution)/shard_map/all_to_all | solution.py:299
  34.3 11.5 %copy-start.1 = (s32[16,1,2]{0,2,1:T(2,128)S(1)}, s32[16,1,2]{0,2,1:T(2,128)}, u32[]{:S(2)}) copy-start(s32[16,1,2]{0,2,1:T(2,128)} %param.17) | copy-start | bytes 388
  34.3 11.5 %copy-start.2 = (s32[16,1,2]{0,2,1:T(2,128)S(1)}, s32[16,1,2]{0,2,1:T(2,128)}, u32[]{:S(2)}) copy-start(s32[16,1,2]{0,2,1:T(2,128)} %param.18) | copy-start | bytes 388
  38.6 13.5 %all-to-all-start.1 = ((f32[16,1,128]{2,1,0:T(1,128)}), f32[16,1,128]{2,1,0:T(1,128)S(1)}, u32[]{:S(2)}, u32[]{:S(2)}) async-start(f32[16,1,128]{2,1,0:T(1,128)} %get-tuple-element.12), calls=%async_computation.1 | async-start | bytes 16384 | tf_op jit(solution)/shard_map/all_to_all | solution.py:348
  45.9 6.3 %copy-start = (f32[8,16384]{1,0:T(8,128)S(1)}, f32[8,16384]{1,0:T(8,128)}, u32[]{:S(2)}) copy-start(f32[8,16384]{1,0:T(8,128)} %param.11) | copy-start | bytes 1572868

commit v5 on v4

--- a/solution.py
+++ b/solution.py
@@ -73,17 +73,25 @@
     return pltpu.CompilerParams(vmem_limit_bytes=mib * MIB)
 
 
+def member(position, peers):
+    bits = peers.bit_length() - 1
+    if peers != 1 << bits:
+        return position
+    return sum(((position >> k) & 1) << (bits - 1 - k) for k in range(bits))
+
+
 def gather_kernel(block_ref, left_ref, live_ref, psi_rows, out_hbm, stage, sems):
-    slots, terms, _ = left_ref.shape
+    slots, terms, peers = left_ref.shape
     sector = psi_rows.shape[1]
     lane = lax.broadcasted_iota(jnp.int32, (SUB, sector), 1)
     puts = []
     for i in range(stage.shape[0]):
-        stage[i, :sector] = pick(psi_rows, block_ref[i])
+        slot, peer = i % slots, member(i // slots, peers)
+        stage[i, :sector] = pick(psi_rows, block_ref[peer * slots + slot])
         values = jnp.zeros(lane.shape, jnp.int32)
         for g in range(terms):
-            values = jnp.where(lane == g, left_ref[i % slots, g, i // slots], values)
-            values = jnp.where(lane == terms + g, live_ref[i % slots, g, i // slots], values)
+            values = jnp.where(lane == g, left_ref[slot, g, peer], values)
+            values = jnp.where(lane == terms + g, live_ref[slot, g, peer], values)
         stage[i, sector:] = values.astype(F32)
         put = pltpu.make_async_copy(stage.at[i], out_hbm.at[i], sems.at[i])
         put.start()
@@ -109,7 +117,7 @@
     stacks_ref,
     moved_ref,
 ):
-    slots, terms, _ = rindex_ref.shape
+    slots, terms, peers = rindex_ref.shape
     sector = psi_rows.shape[1]
 
     rights = right_rows.shape[0] // sector
@@ -130,9 +138,10 @@
     lax.fori_loop(0, psis_ref.shape[0], split_psi, 0, unroll=4)
 
     def turn(i, carry):
+        slot, peer = i % slots, member(i // slots, peers)
         for g in range(terms):
-            right = stacks_ref[rindex_ref[i % slots, g, i // slots]]
-            psi = psis_ref[out_index_ref[i % slots, g, i // slots]]
+            right = stacks_ref[rindex_ref[slot, g, peer]]
+            psi = psis_ref[out_index_ref[slot, g, peer]]
             turned_ref[i, g * sector : (g + 1) * sector] = product_t(psi, right)
         turned_ref[i, terms * sector :] = jnp.zeros((SUB, sector), F32)
         return carry
@@ -215,7 +224,7 @@
 
 
 def remote_kernel(rindex_ref, out_index_ref, moved_ref, turned_hbm, parts_hbm, hpsi_rows, hpsi_hbm, acc, near_ref, rights_ref, sems):
-    slots, terms, _ = rindex_ref.shape
+    slots, terms, peers = rindex_ref.shape
     senders, height, _ = moved_ref.shape
     sector = height // terms
     rights = rights_ref.shape[0]
@@ -230,9 +239,10 @@
     get_rights.wait()
 
     def right_step(i, carry):
+        slot, peer = i % slots, member(i // slots, peers)
         for g in range(terms):
-            right = rights_ref[rindex_ref[i % slots, g, i // slots]]
-            spot = pl.multiple_of(out_index_ref[i % slots, g, i // slots] * sector, sector)
+            right = rights_ref[rindex_ref[slot, g, peer]]
+            spot = pl.multiple_of(out_index_ref[slot, g, peer] * sector, sector)
             acc[pl.ds(spot, sector)] += product(moved_ref[i, g * sector : (g + 1) * sector], twice(right))
         return carry
 
@@ -296,7 +306,14 @@
         compiler_params=roomy(56),
         name="gather_blocks",
     )(send_block.reshape(-1), *by_slot[:2], psi_rows)
-    came = lax.all_to_all(sent.reshape(peers, slots, height, sector), "renv", split_axis=0, concat_axis=0, tiled=True)
+    came = lax.all_to_all(
+        sent.reshape(peers, slots, height, sector),
+        "renv",
+        split_axis=0,
+        concat_axis=0,
+        tiled=True,
+        axis_index_groups=[[member(position, peers) for position in range(peers)]],
+    )
     came = came.reshape(count, height, sector)
 
     slabs = owned // terms

time: 53.5 us -> 53.6 us (level)
  waiting for transfers between devices: 14.6 us -> 18.5 us
  starting transfers between devices: 14.6 us -> 10.9 us
    all_to_all x1, waiting for transfers between devices: 12.4 us -> 16.3 us  [shards(): lax.all_to_all(sent.reshape(peers, slots, height, sector), 'renv', split_...]
    all_to_all x1, starting transfers between devices: 7.2 us -> 3.48 us  [shards(): lax.all_to_all(sums, 'renv', split_axis=0, concat_axis=0, tiled=True)]
where the time goes in v5:
time: 53.6 us; the launch traced here: 53.3 us
  Pallas kernels  23.3 us (43%)
  waiting for transfers between devices  18.5 us (35%)
  starting transfers between devices  10.9 us (20%)
  between operations  0.7 us (1%)
    all_to_all x1, waiting for transfers between devices, shards(): lax.all_to_all(sent.reshape(peers, slots, height, sector), 'renv', split_...  16.3 us
    pallas_call x1, Pallas kernels, shards(): pl.pallas_call(prepare_kernel, out_shape=(jax.ShapeDtypeStruct((count + s...  11.6 us
    all_to_all x1, starting transfers between devices, shards(): lax.all_to_all(sent.reshape(peers, slots, height, sector), 'renv', split_...  7.37 us
    pallas_call x1, Pallas kernels, shards(): pl.pallas_call(lambda *refs: arrive_kernel(terms, *refs), out_shape=(jax....  4.31 us
    pallas_call x1, Pallas kernels, shards(): pl.pallas_call(remote_kernel, out_shape=(rows, rows), in_specs=[SMEM] * 2...  4.04 us
    all_to_all x1, starting transfers between devices, shards(): lax.all_to_all(sums, 'renv', split_axis=0, concat_axis=0, tiled=True)  3.48 us
    pallas_call x1, Pallas kernels, shards(): pl.pallas_call(gather_kernel, out_shape=blocks, in_specs=[SMEM] * 3 + [VM...  2.28 us
    all_to_all x1, waiting for transfers between devices, shards(): lax.all_to_all(sums, 'renv', split_axis=0, concat_axis=0, tiled=True)  2.21 us
  transfers between devices with their start and end apart: 2, of which 2 were waited for; matrix products, arithmetic and copies ran while one was open for 0% of the time, Pallas kernels for 29%

profile of v5, /device:TPU:0, one launch (start us, length us, event | category | flops | bytes accessed | tf_op | source)
XLA Modules:
  0.0 53.3 jit_solution(2498579485947497063)
XLA Ops:
  0.6 2.3 %gather_blocks.1.sent_hbm = f32[16,136,128]{2,1,0:T(8,128)} custom-call(s32[16]{0:T(128)} %bitcast.48, s32[1,2,16]{2,1,0:T(2,128)} %bitcast.46, s32[1,2,16]{2,1,0:T(2,128)} %bitcast.47, f32[1024,128]{1,0:T(8,128)} %bitcast.34), custom_call_target="tpu_custom_call" | custom-call | tf_op jit(solution)/shard_map/gather_blocks/pallas_call | solution.py:300
  2.9 7.4 %all-to-all-start = ((f32[16,1,136,128]{3,2,1,0:T(8,128)}), f32[16,1,136,128]{3,2,1,0:T(8,128)S(1)}, u32[]{:S(2)}, u32[]{:S(2)}) async-start(f32[16,1,136,128]{3,2,1,0:T(8,128)} %bitcast.42), calls=%async_computation | async-start | bytes 2228224 | tf_op jit(solution)/shard_map/all_to_all | solution.py:309
  10.3 11.6 %prepare.1 = (f32[20,264,128]{2,1,0:T(8,128)}, bf16[80,128,256]{2,1,0:T(8,128)(2,1)}) custom-call(f32[16,136,128]{2,1,0:T(8,128)} %gather_blocks.1.sent_hbm, s32[1,2,16]{2,1,0:T(2,128)} %bitcast.38, s32[1,2,16]{2,1,0:T(2,128)} %bitcast.40, s32[32]{0:T(128)} %block_ref.1, s32[32]{0:T(128)} %left_ref.1, s32[32]{0:T(128)} %right_ref.1, f32[1024,128]{1,0:T(8,128)} %bitcast.35, ...), custom_call_target="tpu_custom_call" | custom-call | flops 1000000 | bytes 65536 | tf_op jit(solution)/shard_map/prepare/pallas_call | solution.py:320
  21.9 16.3 %all-to-all-done = f32[16,1,136,128]{3,2,1,0:T(8,128)S(1)} async-done(((f32[16,1,136,128]{3,2,1,0:T(8,128)}), f32[16,1,136,128]{3,2,1,0:T(8,128)S(1)}, u32[]{:S(2)}, u32[]{:S(2)}) %all-to-all-start) | async-done | bytes 1114144 | tf_op jit(solution)/shard_map/all_to_all | solution.py:309
  38.2 0.0 copy-start.1
  38.2 0.0 copy-start.2
  38.2 4.3 %arrive.1 = (bf16[16,256,256]{2,1,0:T(8,128)(2,1)S(1)}, f32[16,1,128]{2,1,0:T(1,128)}) custom-call(f32[16,136,128]{2,1,0:T(8,128)S(1)} %bitcast.37, f32[20,264,128]{2,1,0:T(8,128)} %get-tuple-element.8.refs_1_.turned_hbm, bf16[80,128,256]{2,1,0:T(8,128)(2,1)} %get-tuple-element.9.refs_2_.parts_hbm), custom_call_target="tpu_custom_call" | custom-call | tf_op jit(solution)/shard_map/arrive/pallas_call | solution.py:344
  42.5 3.5 %all-to-all-start.1 = ((f32[16,1,128]{2,1,0:T(1,128)}), f32[16,1,128]{2,1,0:T(1,128)S(1)}, u32[]{:S(2)}, u32[]{:S(2)}) async-start(f32[16,1,128]{2,1,0:T(1,128)} %get-tuple-element.12), calls=%async_computation.1 | async-start | bytes 16384 | tf_op jit(solution)/shard_map/all_to_all | solution.py:365
  46.0 0.0 copy-done.1
  46.0 0.0 copy-done.2
  46.1 0.0 copy-start
  46.1 4.0 %remote_terms.1 = (f32[1024,128]{1,0:T(8,128)S(1)}, f32[1024,128]{1,0:T(8,128)}) custom-call(s32[1,2,16]{2,1,0:T(2,128)S(1)} %bitcast.39, s32[1,2,16]{2,1,0:T(2,128)S(1)} %bitcast.41, bf16[16,256,256]{2,1,0:T(8,128)(2,1)S(1)} %get-tuple-element.10.moved_ref, f32[20,264,128]{2,1,0:T(8,128)} %get-tuple-element.8.refs_1_.turned_hbm, ...), custom_call_target="tpu_custom_call" | custom-call | flops 4000000000 | bytes 6291456 | tf_op jit(solution)/shard_map/remote_terms/pallas_call | solution.py:367
  50.1 2.2 %all-to-all-done.1.sums_ref = f32[16,1,128]{2,1,0:T(1,128)S(1)} async-done(((f32[16,1,128]{2,1,0:T(1,128)}), f32[16,1,128]{2,1,0:T(1,128)S(1)}, u32[]{:S(2)}, u32[]{:S(2)}) %all-to-all-start.1) | async-done | bytes 8224 | tf_op jit(solution)/shard_map/all_to_all | solution.py:365
  52.3 0.0 copy-done
  52.3 1.0 %residual.1 = f32[1024,128]{1,0:T(8,128)} custom-call(f32[16,1,128]{2,1,0:T(1,128)S(1)} %all-to-all-done.1.sums_ref, f32[1024,128]{1,0:T(8,128)S(1)} %get-tuple-element.13.hpsi_rows, f32[1024,128]{1,0:T(8,128)S(1)} %bitcast.36), custom_call_target="tpu_custom_call" | custom-call | tf_op jit(solution)/shard_map/residual/pallas_call | solution.py:383
Async XLA Ops:
  2.9 35.3 %all-to-all-start = ((f32[16,1,136,128]{3,2,1,0:T(8,128)}), f32[16,1,136,128]{3,2,1,0:T(8,128)S(1)}, u32[]{:S(2)}, u32[]{:S(2)}) async-start(f32[16,1,136,128]{3,2,1,0:T(8,128)} %bitcast.42), calls=%async_computation | async-start | bytes 2228224 | tf_op jit(solution)/shard_map/all_to_all | solution.py:309
  38.2 7.8 %copy-start.1 = (s32[16,1,2]{0,2,1:T(2,128)S(1)}, s32[16,1,2]{0,2,1:T(2,128)}, u32[]{:S(2)}) copy-start(s32[16,1,2]{0,2,1:T(2,128)} %param.17) | copy-start | bytes 388
  38.2 7.8 %copy-start.2 = (s32[16,1,2]{0,2,1:T(2,128)S(1)}, s32[16,1,2]{0,2,1:T(2,128)}, u32[]{:S(2)}) copy-start(s32[16,1,2]{0,2,1:T(2,128)} %param.18) | copy-start | bytes 388
  42.5 9.8 %all-to-all-start.1 = ((f32[16,1,128]{2,1,0:T(1,128)}), f32[16,1,128]{2,1,0:T(1,128)S(1)}, u32[]{:S(2)}, u32[]{:S(2)}) async-start(f32[16,1,128]{2,1,0:T(1,128)} %get-tuple-element.12), calls=%async_computation.1 | async-start | bytes 16384 | tf_op jit(solution)/shard_map/all_to_all | solution.py:365
  46.1 6.3 %copy-start = (f32[8,16384]{1,0:T(8,128)S(1)}, f32[8,16384]{1,0:T(8,128)}, u32[]{:S(2)}) copy-start(f32[8,16384]{1,0:T(8,128)} %param.11) | copy-start | bytes 1572868

commit v6 on v5

--- a/solution.py
+++ b/solution.py
@@ -74,10 +74,11 @@
 
 
 def member(position, peers):
-    bits = peers.bit_length() - 1
-    if peers != 1 << bits:
+    quarter = peers // 4
+    if peers % 4:
         return position
-    return sum(((position >> k) & 1) << (bits - 1 - k) for k in range(bits))
+    part = position // quarter
+    return position + quarter * (2 * (part == 1) - (part == 2) - (part == 3))
 
 
 def gather_kernel(block_ref, left_ref, live_ref, psi_rows, out_hbm, stage, sems):

time: 53.6 us -> 54.5 us (1.017)
  waiting for transfers between devices: 18.5 us -> 19.3 us
    all_to_all x1, waiting for transfers between devices: 16.3 us -> 17.1 us  [shards(): lax.all_to_all(sent.reshape(peers, slots, height, sector), 'renv', split_...]
where the time goes in v6:
time: 54.5 us; the launch traced here: 54.2 us
  Pallas kernels  23.3 us (43%)
  waiting for transfers between devices  19.3 us (35%)
  starting transfers between devices  10.9 us (20%)
  between operations  0.7 us (1%)
    all_to_all x1, waiting for transfers between devices, shards(): lax.all_to_all(sent.reshape(peers, slots, height, sector), 'renv', split_...  17.1 us
    pallas_call x1, Pallas kernels, shards(): pl.pallas_call(prepare_kernel, out_shape=(jax.ShapeDtypeStruct((count + s...  11.7 us
    all_to_all x1, starting transfers between devices, shards(): lax.all_to_all(sent.reshape(peers, slots, height, sector), 'renv', split_...  7.37 us
    pallas_call x1, Pallas kernels, shards(): pl.pallas_call(lambda *refs: arrive_kernel(terms, *refs), out_shape=(jax....  4.31 us
    pallas_call x1, Pallas kernels, shards(): pl.pallas_call(remote_kernel, out_shape=(rows, rows), in_specs=[SMEM] * 2...  4.07 us
    all_to_all x1, starting transfers between devices, shards(): lax.all_to_all(sums, 'renv', split_axis=0, concat_axis=0, tiled=True)  3.48 us
    pallas_call x1, Pallas kernels, shards(): pl.pallas_call(gather_kernel, out_shape=blocks, in_specs=[SMEM] * 3 + [VM...  2.28 us
    all_to_all x1, waiting for transfers between devices, shards(): lax.all_to_all(sums, 'renv', split_axis=0, concat_axis=0, tiled=True)  2.19 us
  transfers between devices with their start and end apart: 2, of which 2 were waited for; matrix products, arithmetic and copies ran while one was open for 0% of the time, Pallas kernels for 29%

profile of v6, /device:TPU:0, one launch (start us, length us, event | category | flops | bytes accessed | tf_op | source)
XLA Modules:
  0.0 54.2 jit_solution(10006444852936111975)
XLA Ops:
  0.6 2.3 %gather_blocks.1.sent_hbm = f32[16,136,128]{2,1,0:T(8,128)} custom-call(s32[16]{0:T(128)} %bitcast.48, s32[1,2,16]{2,1,0:T(2,128)} %bitcast.46, s32[1,2,16]{2,1,0:T(2,128)} %bitcast.47, f32[1024,128]{1,0:T(8,128)} %bitcast.34), custom_call_target="tpu_custom_call" | custom-call | tf_op jit(solution)/shard_map/gather_blocks/pallas_call | solution.py:301
  2.9 7.4 %all-to-all-start = ((f32[16,1,136,128]{3,2,1,0:T(8,128)}), f32[16,1,136,128]{3,2,1,0:T(8,128)S(1)}, u32[]{:S(2)}, u32[]{:S(2)}) async-start(f32[16,1,136,128]{3,2,1,0:T(8,128)} %bitcast.42), calls=%async_computation | async-start | bytes 2228224 | tf_op jit(solution)/shard_map/all_to_all | solution.py:310
  10.3 11.7 %prepare.1 = (f32[20,264,128]{2,1,0:T(8,128)}, bf16[80,128,256]{2,1,0:T(8,128)(2,1)}) custom-call(f32[16,136,128]{2,1,0:T(8,128)} %gather_blocks.1.sent_hbm, s32[1,2,16]{2,1,0:T(2,128)} %bitcast.38, s32[1,2,16]{2,1,0:T(2,128)} %bitcast.40, s32[32]{0:T(128)} %block_ref.1, s32[32]{0:T(128)} %left_ref.1, s32[32]{0:T(128)} %right_ref.1, f32[1024,128]{1,0:T(8,128)} %bitcast.35, ...), custom_call_target="tpu_custom_call" | custom-call | flops 1000000 | bytes 65536 | tf_op jit(solution)/shard_map/prepare/pallas_call | solution.py:321
  22.0 17.1 %all-to-all-done = f32[16,1,136,128]{3,2,1,0:T(8,128)S(1)} async-done(((f32[16,1,136,128]{3,2,1,0:T(8,128)}), f32[16,1,136,128]{3,2,1,0:T(8,128)S(1)}, u32[]{:S(2)}, u32[]{:S(2)}) %all-to-all-start) | async-done | bytes 1114144 | tf_op jit(solution)/shard_map/all_to_all | solution.py:310
  39.1 0.0 copy-start.1
  39.1 0.0 copy-start.2
  39.1 4.3 %arrive.1 = (bf16[16,256,256]{2,1,0:T(8,128)(2,1)S(1)}, f32[16,1,128]{2,1,0:T(1,128)}) custom-call(f32[16,136,128]{2,1,0:T(8,128)S(1)} %bitcast.37, f32[20,264,128]{2,1,0:T(8,128)} %get-tuple-element.8.refs_1_.turned_hbm, bf16[80,128,256]{2,1,0:T(8,128)(2,1)} %get-tuple-element.9.refs_2_.parts_hbm), custom_call_target="tpu_custom_call" | custom-call | tf_op jit(solution)/shard_map/arrive/pallas_call | solution.py:345
  43.4 3.5 %all-to-all-start.1 = ((f32[16,1,128]{2,1,0:T(1,128)}), f32[16,1,128]{2,1,0:T(1,128)S(1)}, u32[]{:S(2)}, u32[]{:S(2)}) async-start(f32[16,1,128]{2,1,0:T(1,128)} %get-tuple-element.12), calls=%async_computation.1 | async-start | bytes 16384 | tf_op jit(solution)/shard_map/all_to_all | solution.py:366
  46.9 0.0 copy-done.1
  46.9 0.0 copy-done.2
  46.9 0.0 copy-start
  46.9 4.1 %remote_terms.1 = (f32[1024,128]{1,0:T(8,128)S(1)}, f32[1024,128]{1,0:T(8,128)}) custom-call(s32[1,2,16]{2,1,0:T(2,128)S(1)} %bitcast.39, s32[1,2,16]{2,1,0:T(2,128)S(1)} %bitcast.41, bf16[16,256,256]{2,1,0:T(8,128)(2,1)S(1)} %get-tuple-element.10.moved_ref, f32[20,264,128]{2,1,0:T(8,128)} %get-tuple-element.8.refs_1_.turned_hbm, ...), custom_call_target="tpu_custom_call" | custom-call | flops 4000000000 | bytes 6291456 | tf_op jit(solution)/shard_map/remote_terms/pallas_call | solution.py:368
  51.0 2.2 %all-to-all-done.1.sums_ref = f32[16,1,128]{2,1,0:T(1,128)S(1)} async-done(((f32[16,1,128]{2,1,0:T(1,128)}), f32[16,1,128]{2,1,0:T(1,128)S(1)}, u32[]{:S(2)}, u32[]{:S(2)}) %all-to-all-start.1) | async-done | bytes 8224 | tf_op jit(solution)/shard_map/all_to_all | solution.py:366
  53.2 0.0 copy-done
  53.2 1.0 %residual.1 = f32[1024,128]{1,0:T(8,128)} custom-call(f32[16,1,128]{2,1,0:T(1,128)S(1)} %all-to-all-done.1.sums_ref, f32[1024,128]{1,0:T(8,128)S(1)} %get-tuple-element.13.hpsi_rows, f32[1024,128]{1,0:T(8,128)S(1)} %bitcast.36), custom_call_target="tpu_custom_call" | custom-call | tf_op jit(solution)/shard_map/residual/pallas_call | solution.py:384
Async XLA Ops:
  2.9 36.2 %all-to-all-start = ((f32[16,1,136,128]{3,2,1,0:T(8,128)}), f32[16,1,136,128]{3,2,1,0:T(8,128)S(1)}, u32[]{:S(2)}, u32[]{:S(2)}) async-start(f32[16,1,136,128]{3,2,1,0:T(8,128)} %bitcast.42), calls=%async_computation | async-start | bytes 2228224 | tf_op jit(solution)/shard_map/all_to_all | solution.py:310
  39.1 7.8 %copy-start.1 = (s32[16,1,2]{0,2,1:T(2,128)S(1)}, s32[16,1,2]{0,2,1:T(2,128)}, u32[]{:S(2)}) copy-start(s32[16,1,2]{0,2,1:T(2,128)} %param.17) | copy-start | bytes 388
  39.1 7.8 %copy-start.2 = (s32[16,1,2]{0,2,1:T(2,128)S(1)}, s32[16,1,2]{0,2,1:T(2,128)}, u32[]{:S(2)}) copy-start(s32[16,1,2]{0,2,1:T(2,128)} %param.18) | copy-start | bytes 388
  43.4 9.8 %all-to-all-start.1 = ((f32[16,1,128]{2,1,0:T(1,128)}), f32[16,1,128]{2,1,0:T(1,128)S(1)}, u32[]{:S(2)}, u32[]{:S(2)}) async-start(f32[16,1,128]{2,1,0:T(1,128)} %get-tuple-element.12), calls=%async_computation.1 | async-start | bytes 16384 | tf_op jit(solution)/shard_map/all_to_all | solution.py:366
  46.9 6.3 %copy-start = (f32[8,16384]{1,0:T(8,128)S(1)}, f32[8,16384]{1,0:T(8,128)}, u32[]{:S(2)}) copy-start(f32[8,16384]{1,0:T(8,128)} %param.11) | copy-start | bytes 1572868

commit v7 on v4

--- a/solution.py
+++ b/solution.py
@@ -345,7 +345,9 @@
         moved.append(kept)
         sums = share if count == chunk else sums + share
     moved = moved[0] if len(moved) == 1 else jnp.concatenate(moved, axis=0)
-    totals = lax.all_to_all(sums, "renv", split_axis=0, concat_axis=0, tiled=True)
+    totals = lax.all_to_all(
+        sums, "renv", split_axis=0, concat_axis=0, tiled=True, axis_index_groups=[list(reversed(range(peers)))]
+    )
 
     hpsi_rows, hpsi = pl.pallas_call(
         remote_kernel,

time: 53.5 us -> 53.1 us (level)
  waiting for transfers between devices: 14.6 us -> 12.4 us
  starting transfers between devices: 14.6 us -> 16.5 us
    all_to_all x1, waiting for transfers between devices: 2.25 us -> 0.01 us  [shards(): lax.all_to_all(sums, 'renv', split_axis=0, concat_axis=0, tiled=True, axi...]
    all_to_all x1, starting transfers between devices: 7.2 us -> 9.1 us  [shards(): lax.all_to_all(sums, 'renv', split_axis=0, concat_axis=0, tiled=True, axi...]
  transfers between devices with their start and end apart: 2 -> 2, of which waited for: 2 -> 1; matrix products, arithmetic and copies ran while one was open for 0% -> 0% of each run, Pallas kernels for 29% -> 30%
where the time goes in v7:
time: 53.1 us; the launch traced here: 52.8 us
  Pallas kernels  23.3 us (44%)
  starting transfers between devices  16.5 us (31%)
  waiting for transfers between devices  12.4 us (23%)
  between operations  0.7 us (1%)
    all_to_all x1, waiting for transfers between devices, shards(): lax.all_to_all(sent.reshape(peers, slots, height, sector), 'renv', split_...  12.4 us
    pallas_call x1, Pallas kernels, shards(): pl.pallas_call(prepare_kernel, out_shape=(jax.ShapeDtypeStruct((count + s...  11.6 us
    all_to_all x1, starting transfers between devices, shards(): lax.all_to_all(sums, 'renv', split_axis=0, concat_axis=0, tiled=True, axi...  9.1 us
    all_to_all x1, starting transfers between devices, shards(): lax.all_to_all(sent.reshape(peers, slots, height, sector), 'renv', split_...  7.37 us
    pallas_call x1, Pallas kernels, shards(): pl.pallas_call(lambda *refs: arrive_kernel(terms, *refs), out_shape=(jax....  4.31 us
    pallas_call x1, Pallas kernels, shards(): pl.pallas_call(remote_kernel, out_shape=(rows, rows), in_specs=[SMEM] * 2...  4.04 us
    pallas_call x1, Pallas kernels, shards(): pl.pallas_call(gather_kernel, out_shape=blocks, in_specs=[SMEM] * 3 + [VM...  2.28 us
  transfers between devices with their start and end apart: 2, of which 1 were waited for; matrix products, arithmetic and copies ran while one was open for 0% of the time, Pallas kernels for 30%

profile of v7, /device:TPU:0, one launch (start us, length us, event | category | flops | bytes accessed | tf_op | source)
XLA Modules:
  0.0 52.8 jit_solution(18229795879254761881)
XLA Ops:
  0.6 2.3 %gather_blocks.1.sent_hbm = f32[16,136,128]{2,1,0:T(8,128)} custom-call(s32[16]{0:T(128)} %bitcast.48, s32[1,2,16]{2,1,0:T(2,128)} %bitcast.46, s32[1,2,16]{2,1,0:T(2,128)} %bitcast.47, f32[1024,128]{1,0:T(8,128)} %bitcast.34), custom_call_target="tpu_custom_call" | custom-call | tf_op jit(solution)/shard_map/gather_blocks/pallas_call | solution.py:290
  2.9 7.4 %all-to-all-start = ((f32[16,1,136,128]{3,2,1,0:T(8,128)}), f32[16,1,136,128]{3,2,1,0:T(8,128)S(1)}, u32[]{:S(2)}, u32[]{:S(2)}) async-start(f32[16,1,136,128]{3,2,1,0:T(8,128)} %bitcast.42), calls=%async_computation | async-start | bytes 2228224 | tf_op jit(solution)/shard_map/all_to_all | solution.py:299
  10.3 11.6 %prepare.1 = (f32[20,264,128]{2,1,0:T(8,128)}, bf16[80,128,256]{2,1,0:T(8,128)(2,1)}) custom-call(f32[16,136,128]{2,1,0:T(8,128)} %gather_blocks.1.sent_hbm, s32[1,2,16]{2,1,0:T(2,128)} %bitcast.38, s32[1,2,16]{2,1,0:T(2,128)} %bitcast.40, s32[32]{0:T(128)} %block_ref.1, s32[32]{0:T(128)} %left_ref.1, s32[32]{0:T(128)} %right_ref.1, f32[1024,128]{1,0:T(8,128)} %bitcast.35, ...), custom_call_target="tpu_custom_call" | custom-call | flops 1000000 | bytes 65536 | tf_op jit(solution)/shard_map/prepare/pallas_call | solution.py:303
  21.9 12.4 %all-to-all-done = f32[16,1,136,128]{3,2,1,0:T(8,128)S(1)} async-done(((f32[16,1,136,128]{3,2,1,0:T(8,128)}), f32[16,1,136,128]{3,2,1,0:T(8,128)S(1)}, u32[]{:S(2)}, u32[]{:S(2)}) %all-to-all-start) | async-done | bytes 1114144 | tf_op jit(solution)/shard_map/all_to_all | solution.py:299
  34.3 0.0 copy-start.1
  34.3 0.0 copy-start.2
  34.3 4.3 %arrive.1 = (bf16[16,256,256]{2,1,0:T(8,128)(2,1)S(1)}, f32[16,1,128]{2,1,0:T(1,128)}) custom-call(f32[16,136,128]{2,1,0:T(8,128)S(1)} %bitcast.37, f32[20,264,128]{2,1,0:T(8,128)} %get-tuple-element.8.refs_1_.turned_hbm, bf16[80,128,256]{2,1,0:T(8,128)(2,1)} %get-tuple-element.9.refs_2_.parts_hbm), custom_call_target="tpu_custom_call" | custom-call | tf_op jit(solution)/shard_map/arrive/pallas_call | solution.py:327
  38.6 9.1 %all-to-all-start.1 = ((f32[16,1,128]{2,1,0:T(1,128)}), f32[16,1,128]{2,1,0:T(1,128)S(1)}, u32[]{:S(2)}, u32[]{:S(2)}) async-start(f32[16,1,128]{2,1,0:T(1,128)} %get-tuple-element.12), calls=%async_computation.1 | async-start | bytes 16384 | tf_op jit(solution)/shard_map/all_to_all | solution.py:348
  47.7 0.0 copy-done.1
  47.8 0.0 copy-done.2
  47.8 0.0 copy-start
  47.8 4.0 %remote_terms.1 = (f32[1024,128]{1,0:T(8,128)S(1)}, f32[1024,128]{1,0:T(8,128)}) custom-call(s32[1,2,16]{2,1,0:T(2,128)S(1)} %bitcast.39, s32[1,2,16]{2,1,0:T(2,128)S(1)} %bitcast.41, bf16[16,256,256]{2,1,0:T(8,128)(2,1)S(1)} %get-tuple-element.10.moved_ref, f32[20,264,128]{2,1,0:T(8,128)} %get-tuple-element.8.refs_1_.turned_hbm, ...), custom_call_target="tpu_custom_call" | custom-call | flops 4000000000 | bytes 6291456 | tf_op jit(solution)/shard_map/remote_terms/pallas_call | solution.py:352
  51.8 0.0 all-to-all-done.1.sums_ref
  51.8 0.0 copy-done
  51.8 1.0 %residual.1 = f32[1024,128]{1,0:T(8,128)} custom-call(f32[16,1,128]{2,1,0:T(1,128)S(1)} %all-to-all-done.1.sums_ref, f32[1024,128]{1,0:T(8,128)S(1)} %get-tuple-element.13.hpsi_rows, f32[1024,128]{1,0:T(8,128)S(1)} %bitcast.36), custom_call_target="tpu_custom_call" | custom-call | tf_op jit(solution)/shard_map/residual/pallas_call | solution.py:368
Async XLA Ops:
  2.9 31.4 %all-to-all-start = ((f32[16,1,136,128]{3,2,1,0:T(8,128)}), f32[16,1,136,128]{3,2,1,0:T(8,128)S(1)}, u32[]{:S(2)}, u32[]{:S(2)}) async-start(f32[16,1,136,128]{3,2,1,0:T(8,128)} %bitcast.42), calls=%async_computation | async-start | bytes 2228224 | tf_op jit(solution)/shard_map/all_to_all | solution.py:299
  34.3 13.4 %copy-start.1 = (s32[16,1,2]{0,2,1:T(2,128)S(1)}, s32[16,1,2]{0,2,1:T(2,128)}, u32[]{:S(2)}) copy-start(s32[16,1,2]{0,2,1:T(2,128)} %param.17) | copy-start | bytes 388
  34.3 13.4 %copy-start.2 = (s32[16,1,2]{0,2,1:T(2,128)S(1)}, s32[16,1,2]{0,2,1:T(2,128)}, u32[]{:S(2)}) copy-start(s32[16,1,2]{0,2,1:T(2,128)} %param.18) | copy-start | bytes 388
  38.6 13.2 %all-to-all-start.1 = ((f32[16,1,128]{2,1,0:T(1,128)}), f32[16,1,128]{2,1,0:T(1,128)S(1)}, u32[]{:S(2)}, u32[]{:S(2)}) async-start(f32[16,1,128]{2,1,0:T(1,128)} %get-tuple-element.12), calls=%async_computation.1 | async-start | bytes 16384 | tf_op jit(solution)/shard_map/all_to_all | solution.py:348
  47.8 4.1 %copy-start = (f32[8,16384]{1,0:T(8,128)S(1)}, f32[8,16384]{1,0:T(8,128)}, u32[]{:S(2)}) copy-start(f32[8,16384]{1,0:T(8,128)} %param.11) | copy-start | bytes 1572868

commit v8 on v7

--- a/solution.py
+++ b/solution.py
@@ -246,6 +246,14 @@
     put = pltpu.make_async_copy(hpsi_rows, hpsi_hbm, sems.at[0])
     put.start()
     put.wait()
+
+
+def scalar_order(peers):
+    quarter = peers // 4
+    if peers % 4:
+        return list(range(peers))
+    order = list(range(peers - 1, 3 * quarter - 1, -1)) + list(range(quarter))
+    return order + list(range(3 * quarter - 1, quarter - 1, -1))
 
 
 def residual_kernel(sums_ref, hpsi_rows, psi_rows, out_ref):
@@ -346,7 +354,7 @@
         sums = share if count == chunk else sums + share
     moved = moved[0] if len(moved) == 1 else jnp.concatenate(moved, axis=0)
     totals = lax.all_to_all(
-        sums, "renv", split_axis=0, concat_axis=0, tiled=True, axis_index_groups=[list(reversed(range(peers)))]
+        sums, "renv", split_axis=0, concat_axis=0, tiled=True, axis_index_groups=[scalar_order(peers)]
     )
 
     hpsi_rows, hpsi = pl.pallas_call(

time: 53.1 us -> 53 us (level)
  no operation moved by 1% of the time
where the time goes in v8:
time: 53 us; the launch traced here: 52.7 us
  Pallas kernels  23.3 us (44%)
  starting transfers between devices  16.4 us (31%)
  waiting for transfers between devices  12.4 us (23%)
  between operations  0.7 us (1%)
    all_to_all x1, waiting for transfers between devices, shards(): lax.all_to_all(sent.reshape(peers, slots, height, sector), 'renv', split_...  12.4 us
    pallas_call x1, Pallas kernels, shards(): pl.pallas_call(prepare_kernel, out_shape=(jax.ShapeDtypeStruct((count + s...  11.6 us
    all_to_all x1, starting transfers between devices, shards(): lax.all_to_all(sums, 'renv', split_axis=0, concat_axis=0, tiled=True, axi...  9 us
    all_to_all x1, starting transfers between devices, shards(): lax.all_to_all(sent.reshape(peers, slots, height, sector), 'renv', split_...  7.37 us
    pallas_call x1, Pallas kernels, shards(): pl.pallas_call(lambda *refs: arrive_kernel(terms, *refs), out_shape=(jax....  4.31 us
    pallas_call x1, Pallas kernels, shards(): pl.pallas_call(remote_kernel, out_shape=(rows, rows), in_specs=[SMEM] * 2...  4.04 us
    pallas_call x1, Pallas kernels, shards(): pl.pallas_call(gather_kernel, out_shape=blocks, in_specs=[SMEM] * 3 + [VM...  2.28 us
  transfers between devices with their start and end apart: 2, of which 1 were waited for; matrix products, arithmetic and copies ran while one was open for 0% of the time, Pallas kernels for 30%

profile of v8, /device:TPU:0, one launch (start us, length us, event | category | flops | bytes accessed | tf_op | source)
XLA Modules:
  0.0 52.7 jit_solution(7888686037886530977)
XLA Ops:
  0.6 2.3 %gather_blocks.1.sent_hbm = f32[16,136,128]{2,1,0:T(8,128)} custom-call(s32[16]{0:T(128)} %bitcast.48, s32[1,2,16]{2,1,0:T(2,128)} %bitcast.46, s32[1,2,16]{2,1,0:T(2,128)} %bitcast.47, f32[1024,128]{1,0:T(8,128)} %bitcast.34), custom_call_target="tpu_custom_call" | custom-call | tf_op jit(solution)/shard_map/gather_blocks/pallas_call | solution.py:298
  2.9 7.4 %all-to-all-start = ((f32[16,1,136,128]{3,2,1,0:T(8,128)}), f32[16,1,136,128]{3,2,1,0:T(8,128)S(1)}, u32[]{:S(2)}, u32[]{:S(2)}) async-start(f32[16,1,136,128]{3,2,1,0:T(8,128)} %bitcast.42), calls=%async_computation | async-start | bytes 2228224 | tf_op jit(solution)/shard_map/all_to_all | solution.py:307
  10.3 11.6 %prepare.1 = (f32[20,264,128]{2,1,0:T(8,128)}, bf16[80,128,256]{2,1,0:T(8,128)(2,1)}) custom-call(f32[16,136,128]{2,1,0:T(8,128)} %gather_blocks.1.sent_hbm, s32[1,2,16]{2,1,0:T(2,128)} %bitcast.38, s32[1,2,16]{2,1,0:T(2,128)} %bitcast.40, s32[32]{0:T(128)} %block_ref.1, s32[32]{0:T(128)} %left_ref.1, s32[32]{0:T(128)} %right_ref.1, f32[1024,128]{1,0:T(8,128)} %bitcast.35, ...), custom_call_target="tpu_custom_call" | custom-call | flops 1000000 | bytes 65536 | tf_op jit(solution)/shard_map/prepare/pallas_call | solution.py:311
  21.9 12.4 %all-to-all-done = f32[16,1,136,128]{3,2,1,0:T(8,128)S(1)} async-done(((f32[16,1,136,128]{3,2,1,0:T(8,128)}), f32[16,1,136,128]{3,2,1,0:T(8,128)S(1)}, u32[]{:S(2)}, u32[]{:S(2)}) %all-to-all-start) | async-done | bytes 1114144 | tf_op jit(solution)/shard_map/all_to_all | solution.py:307
  34.3 0.0 copy-start.1
  34.3 0.0 copy-start.2
  34.3 4.3 %arrive.1 = (bf16[16,256,256]{2,1,0:T(8,128)(2,1)S(1)}, f32[16,1,128]{2,1,0:T(1,128)}) custom-call(f32[16,136,128]{2,1,0:T(8,128)S(1)} %bitcast.37, f32[20,264,128]{2,1,0:T(8,128)} %get-tuple-element.8.refs_1_.turned_hbm, bf16[80,128,256]{2,1,0:T(8,128)(2,1)} %get-tuple-element.9.refs_2_.parts_hbm), custom_call_target="tpu_custom_call" | custom-call | tf_op jit(solution)/shard_map/arrive/pallas_call | solution.py:335
  38.6 9.0 %all-to-all-start.1 = ((f32[16,1,128]{2,1,0:T(1,128)}), f32[16,1,128]{2,1,0:T(1,128)S(1)}, u32[]{:S(2)}, u32[]{:S(2)}) async-start(f32[16,1,128]{2,1,0:T(1,128)} %get-tuple-element.12), calls=%async_computation.1 | async-start | bytes 16384 | tf_op jit(solution)/shard_map/all_to_all | solution.py:356
  47.6 0.0 copy-done.1
  47.6 0.0 copy-done.2
  47.7 0.0 copy-start
  47.7 4.0 %remote_terms.1 = (f32[1024,128]{1,0:T(8,128)S(1)}, f32[1024,128]{1,0:T(8,128)}) custom-call(s32[1,2,16]{2,1,0:T(2,128)S(1)} %bitcast.39, s32[1,2,16]{2,1,0:T(2,128)S(1)} %bitcast.41, bf16[16,256,256]{2,1,0:T(8,128)(2,1)S(1)} %get-tuple-element.10.moved_ref, f32[20,264,128]{2,1,0:T(8,128)} %get-tuple-element.8.refs_1_.turned_hbm, ...), custom_call_target="tpu_custom_call" | custom-call | flops 4000000000 | bytes 6291456 | tf_op jit(solution)/shard_map/remote_terms/pallas_call | solution.py:360
  51.7 0.0 all-to-all-done.1.sums_ref
  51.7 0.0 copy-done
  51.7 1.0 %residual.1 = f32[1024,128]{1,0:T(8,128)} custom-call(f32[16,1,128]{2,1,0:T(1,128)S(1)} %all-to-all-done.1.sums_ref, f32[1024,128]{1,0:T(8,128)S(1)} %get-tuple-element.13.hpsi_rows, f32[1024,128]{1,0:T(8,128)S(1)} %bitcast.36), custom_call_target="tpu_custom_call" | custom-call | tf_op jit(solution)/shard_map/residual/pallas_call | solution.py:376
Async XLA Ops:
  2.9 31.4 %all-to-all-start = ((f32[16,1,136,128]{3,2,1,0:T(8,128)}), f32[16,1,136,128]{3,2,1,0:T(8,128)S(1)}, u32[]{:S(2)}, u32[]{:S(2)}) async-start(f32[16,1,136,128]{3,2,1,0:T(8,128)} %bitcast.42), calls=%async_computation | async-start | bytes 2228224 | tf_op jit(solution)/shard_map/all_to_all | solution.py:307
  34.3 13.3 %copy-start.1 = (s32[16,1,2]{0,2,1:T(2,128)S(1)}, s32[16,1,2]{0,2,1:T(2,128)}, u32[]{:S(2)}) copy-start(s32[16,1,2]{0,2,1:T(2,128)} %param.17) | copy-start | bytes 388
  34.3 13.3 %copy-start.2 = (s32[16,1,2]{0,2,1:T(2,128)S(1)}, s32[16,1,2]{0,2,1:T(2,128)}, u32[]{:S(2)}) copy-start(s32[16,1,2]{0,2,1:T(2,128)} %param.18) | copy-start | bytes 388
  38.6 13.1 %all-to-all-start.1 = ((f32[16,1,128]{2,1,0:T(1,128)}), f32[16,1,128]{2,1,0:T(1,128)S(1)}, u32[]{:S(2)}, u32[]{:S(2)}) async-start(f32[16,1,128]{2,1,0:T(1,128)} %get-tuple-element.12), calls=%async_computation.1 | async-start | bytes 16384 | tf_op jit(solution)/shard_map/all_to_all | solution.py:356
  47.7 4.1 %copy-start = (f32[8,16384]{1,0:T(8,128)S(1)}, f32[8,16384]{1,0:T(8,128)}, u32[]{:S(2)}) copy-start(f32[8,16384]{1,0:T(8,128)} %param.11) | copy-start | bytes 1572868

commit v9 on v5

--- a/solution.py
+++ b/solution.py
@@ -74,10 +74,10 @@
 
 
 def member(position, peers):
-    bits = peers.bit_length() - 1
-    if peers != 1 << bits:
+    if peers % 2:
         return position
-    return sum(((position >> k) & 1) << (bits - 1 - k) for k in range(bits))
+    middle = peers // 2 + 1
+    return position + middle * (1 * (position == 0) - 1 * (position == middle))
 
 
 def gather_kernel(block_ref, left_ref, live_ref, psi_rows, out_hbm, stage, sems):
@@ -362,7 +362,8 @@
         moved.append(kept)
         sums = share if count == chunk else sums + share
     moved = moved[0] if len(moved) == 1 else jnp.concatenate(moved, axis=0)
-    totals = lax.all_to_all(sums, "renv", split_axis=0, concat_axis=0, tiled=True)
+    order = [member(position, peers) for position in range(peers)]
+    totals = lax.all_to_all(sums, "renv", split_axis=0, concat_axis=0, tiled=True, axis_index_groups=[order])
 
     hpsi_rows, hpsi = pl.pallas_call(
         remote_kernel,

time: 53.6 us -> 50.8 us (0.948)
  waiting for transfers between devices: 18.5 us -> 15 us
  starting transfers between devices: 10.9 us -> 11.6 us
    all_to_all x1, waiting for transfers between devices: 2.21 us -> 0.01 us  [shards(): lax.all_to_all(sums, 'renv', split_axis=0, concat_axis=0, tiled=True, axi...]
    all_to_all x1, waiting for transfers between devices: 16.3 us -> 14.9 us  [shards(): lax.all_to_all(sent.reshape(peers, slots, height, sector), 'renv', split_...]
  transfers between devices with their start and end apart: 2 -> 2, of which waited for: 2 -> 1; matrix products, arithmetic and copies ran while one was open for 0% -> 0% of each run, Pallas kernels for 29% -> 31%
where the time goes in v9:
time: 50.8 us; the launch traced here: 50.5 us
  Pallas kernels  23.3 us (46%)
  waiting for transfers between devices  15 us (30%)
  starting transfers between devices  11.6 us (23%)
  between operations  0.69 us (1%)
    all_to_all x1, waiting for transfers between devices, shards(): lax.all_to_all(sent.reshape(peers, slots, height, sector), 'renv', split_...  14.9 us
    pallas_call x1, Pallas kernels, shards(): pl.pallas_call(prepare_kernel, out_shape=(jax.ShapeDtypeStruct((count + s...  11.6 us
    all_to_all x1, starting transfers between devices, shards(): lax.all_to_all(sent.reshape(peers, slots, height, sector), 'renv', split_...  7.59 us
    pallas_call x1, Pallas kernels, shards(): pl.pallas_call(lambda *refs: arrive_kernel(terms, *refs), out_shape=(jax....  4.31 us
    pallas_call x1, Pallas kernels, shards(): pl.pallas_call(remote_kernel, out_shape=(rows, rows), in_specs=[SMEM] * 2...  4.05 us
    all_to_all x1, starting transfers between devices, shards(): lax.all_to_all(sums, 'renv', split_axis=0, concat_axis=0, tiled=True, axi...  4 us
    pallas_call x1, Pallas kernels, shards(): pl.pallas_call(gather_kernel, out_shape=blocks, in_specs=[SMEM] * 3 + [VM...  2.28 us
  transfers between devices with their start and end apart: 2, of which 1 were waited for; matrix products, arithmetic and copies ran while one was open for 0% of the time, Pallas kernels for 31%

profile of v9, /device:TPU:0, one launch (start us, length us, event | category | flops | bytes accessed | tf_op | source)
XLA Modules:
  0.0 50.5 jit_solution(873813109896562124)
XLA Ops:
  0.6 2.3 %gather_blocks.1.sent_hbm = f32[16,136,128]{2,1,0:T(8,128)} custom-call(s32[16]{0:T(128)} %bitcast.48, s32[1,2,16]{2,1,0:T(2,128)} %bitcast.46, s32[1,2,16]{2,1,0:T(2,128)} %bitcast.47, f32[1024,128]{1,0:T(8,128)} %bitcast.34), custom_call_target="tpu_custom_call" | custom-call | tf_op jit(solution)/shard_map/gather_blocks/pallas_call | solution.py:300
  2.9 7.6 %all-to-all-start = ((f32[16,1,136,128]{3,2,1,0:T(8,128)}), f32[16,1,136,128]{3,2,1,0:T(8,128)S(1)}, u32[]{:S(2)}, u32[]{:S(2)}) async-start(f32[16,1,136,128]{3,2,1,0:T(8,128)} %bitcast.42), calls=%async_computation | async-start | bytes 2228224 | tf_op jit(solution)/shard_map/all_to_all | solution.py:309
  10.5 11.6 %prepare.1 = (f32[20,264,128]{2,1,0:T(8,128)}, bf16[80,128,256]{2,1,0:T(8,128)(2,1)}) custom-call(f32[16,136,128]{2,1,0:T(8,128)} %gather_blocks.1.sent_hbm, s32[1,2,16]{2,1,0:T(2,128)} %bitcast.38, s32[1,2,16]{2,1,0:T(2,128)} %bitcast.40, s32[32]{0:T(128)} %block_ref.1, s32[32]{0:T(128)} %left_ref.1, s32[32]{0:T(128)} %right_ref.1, f32[1024,128]{1,0:T(8,128)} %bitcast.35, ...), custom_call_target="tpu_custom_call" | custom-call | flops 1000000 | bytes 65536 | tf_op jit(solution)/shard_map/prepare/pallas_call | solution.py:320
  22.2 14.9 %all-to-all-done = f32[16,1,136,128]{3,2,1,0:T(8,128)S(1)} async-done(((f32[16,1,136,128]{3,2,1,0:T(8,128)}), f32[16,1,136,128]{3,2,1,0:T(8,128)S(1)}, u32[]{:S(2)}, u32[]{:S(2)}) %all-to-all-start) | async-done | bytes 1114144 | tf_op jit(solution)/shard_map/all_to_all | solution.py:309
  37.1 0.0 copy-start.1
  37.1 0.0 copy-start.2
  37.1 4.3 %arrive.1 = (bf16[16,256,256]{2,1,0:T(8,128)(2,1)S(1)}, f32[16,1,128]{2,1,0:T(1,128)}) custom-call(f32[16,136,128]{2,1,0:T(8,128)S(1)} %bitcast.37, f32[20,264,128]{2,1,0:T(8,128)} %get-tuple-element.8.refs_1_.turned_hbm, bf16[80,128,256]{2,1,0:T(8,128)(2,1)} %get-tuple-element.9.refs_2_.parts_hbm), custom_call_target="tpu_custom_call" | custom-call | tf_op jit(solution)/shard_map/arrive/pallas_call | solution.py:344
  41.4 4.0 %all-to-all-start.1 = ((f32[16,1,128]{2,1,0:T(1,128)}), f32[16,1,128]{2,1,0:T(1,128)S(1)}, u32[]{:S(2)}, u32[]{:S(2)}) async-start(f32[16,1,128]{2,1,0:T(1,128)} %get-tuple-element.12), calls=%async_computation.1 | async-start | bytes 16384 | tf_op jit(solution)/shard_map/all_to_all | solution.py:366
  45.4 0.0 copy-done.1
  45.4 0.0 copy-done.2
  45.4 0.0 copy-start
  45.5 4.0 %remote_terms.1 = (f32[1024,128]{1,0:T(8,128)S(1)}, f32[1024,128]{1,0:T(8,128)}) custom-call(s32[1,2,16]{2,1,0:T(2,128)S(1)} %bitcast.39, s32[1,2,16]{2,1,0:T(2,128)S(1)} %bitcast.41, bf16[16,256,256]{2,1,0:T(8,128)(2,1)S(1)} %get-tuple-element.10.moved_ref, f32[20,264,128]{2,1,0:T(8,128)} %get-tuple-element.8.refs_1_.turned_hbm, ...), custom_call_target="tpu_custom_call" | custom-call | flops 4000000000 | bytes 6291456 | tf_op jit(solution)/shard_map/remote_terms/pallas_call | solution.py:368
  49.5 0.0 all-to-all-done.1.sums_ref
  49.5 0.0 copy-done
  49.5 1.0 %residual.1 = f32[1024,128]{1,0:T(8,128)} custom-call(f32[16,1,128]{2,1,0:T(1,128)S(1)} %all-to-all-done.1.sums_ref, f32[1024,128]{1,0:T(8,128)S(1)} %get-tuple-element.13.hpsi_rows, f32[1024,128]{1,0:T(8,128)S(1)} %bitcast.36), custom_call_target="tpu_custom_call" | custom-call | tf_op jit(solution)/shard_map/residual/pallas_call | solution.py:384
Async XLA Ops:
  2.9 34.2 %all-to-all-start = ((f32[16,1,136,128]{3,2,1,0:T(8,128)}), f32[16,1,136,128]{3,2,1,0:T(8,128)S(1)}, u32[]{:S(2)}, u32[]{:S(2)}) async-start(f32[16,1,136,128]{3,2,1,0:T(8,128)} %bitcast.42), calls=%async_computation | async-start | bytes 2228224 | tf_op jit(solution)/shard_map/all_to_all | solution.py:309
  37.1 8.3 %copy-start.1 = (s32[16,1,2]{0,2,1:T(2,128)S(1)}, s32[16,1,2]{0,2,1:T(2,128)}, u32[]{:S(2)}) copy-start(s32[16,1,2]{0,2,1:T(2,128)} %param.17) | copy-start | bytes 388
  37.1 8.3 %copy-start.2 = (s32[16,1,2]{0,2,1:T(2,128)S(1)}, s32[16,1,2]{0,2,1:T(2,128)}, u32[]{:S(2)}) copy-start(s32[16,1,2]{0,2,1:T(2,128)} %param.18) | copy-start | bytes 388
  41.4 8.1 %all-to-all-start.1 = ((f32[16,1,128]{2,1,0:T(1,128)}), f32[16,1,128]{2,1,0:T(1,128)S(1)}, u32[]{:S(2)}, u32[]{:S(2)}) async-start(f32[16,1,128]{2,1,0:T(1,128)} %get-tuple-element.12), calls=%async_computation.1 | async-start | bytes 16384 | tf_op jit(solution)/shard_map/all_to_all | solution.py:366
  45.4 4.1 %copy-start = (f32[8,16384]{1,0:T(8,128)S(1)}, f32[8,16384]{1,0:T(8,128)}, u32[]{:S(2)}) copy-start(f32[8,16384]{1,0:T(8,128)} %param.11) | copy-start | bytes 1572868

commit v10 on v9

--- a/solution.py
+++ b/solution.py
@@ -77,7 +77,7 @@
     if peers % 2:
         return position
     middle = peers // 2 + 1
-    return position + middle * (1 * (position == 0) - 1 * (position == middle))
+    return position + middle * (position == 0) - 1 * (position > 0) + 1 * (position > middle)
 
 
 def gather_kernel(block_ref, left_ref, live_ref, psi_rows, out_hbm, stage, sems):

time: 50.8 us -> 50.3 us (level)
  waiting for transfers between devices: 15 us -> 11 us
  starting transfers between devices: 11.6 us -> 15 us
    all_to_all x1, waiting for transfers between devices: 14.9 us -> 11 us  [shards(): lax.all_to_all(sent.reshape(peers, slots, height, sector), 'renv', split_...]
    all_to_all x1, starting transfers between devices: 4 us -> 7.46 us  [shards(): lax.all_to_all(sums, 'renv', split_axis=0, concat_axis=0, tiled=True, axi...]
where the time goes in v10:
time: 50.3 us; the launch traced here: 50 us
  Pallas kernels  23.3 us (46%)
  starting transfers between devices  15 us (30%)
  waiting for transfers between devices  11 us (22%)
  between operations  0.68 us (1%)
    pallas_call x1, Pallas kernels, shards(): pl.pallas_call(prepare_kernel, out_shape=(jax.ShapeDtypeStruct((count + s...  11.7 us
    all_to_all x1, waiting for transfers between devices, shards(): lax.all_to_all(sent.reshape(peers, slots, height, sector), 'renv', split_...  11 us
    all_to_all x1, starting transfers between devices, shards(): lax.all_to_all(sent.reshape(peers, slots, height, sector), 'renv', split_...  7.56 us
    all_to_all x1, starting transfers between devices, shards(): lax.all_to_all(sums, 'renv', split_axis=0, concat_axis=0, tiled=True, axi...  7.46 us
    pallas_call x1, Pallas kernels, shards(): pl.pallas_call(lambda *refs: arrive_kernel(terms, *refs), out_shape=(jax....  4.31 us
    pallas_call x1, Pallas kernels, shards(): pl.pallas_call(remote_kernel, out_shape=(rows, rows), in_specs=[SMEM] * 2...  4.05 us
    pallas_call x1, Pallas kernels, shards(): pl.pallas_call(gather_kernel, out_shape=blocks, in_specs=[SMEM] * 3 + [VM...  2.28 us
  transfers between devices with their start and end apart: 2, of which 1 were waited for; matrix products, arithmetic and copies ran while one was open for 0% of the time, Pallas kernels for 31%

profile of v10, /device:TPU:0, one launch (start us, length us, event | category | flops | bytes accessed | tf_op | source)
XLA Modules:
  0.0 50.0 jit_solution(15427580011779169906)
XLA Ops:
  0.6 2.3 %gather_blocks.1.sent_hbm = f32[16,136,128]{2,1,0:T(8,128)} custom-call(s32[16]{0:T(128)} %bitcast.48, s32[1,2,16]{2,1,0:T(2,128)} %bitcast.46, s32[1,2,16]{2,1,0:T(2,128)} %bitcast.47, f32[1024,128]{1,0:T(8,128)} %bitcast.34), custom_call_target="tpu_custom_call" | custom-call | tf_op jit(solution)/shard_map/gather_blocks/pallas_call | solution.py:300
  2.9 7.6 %all-to-all-start = ((f32[16,1,136,128]{3,2,1,0:T(8,128)}), f32[16,1,136,128]{3,2,1,0:T(8,128)S(1)}, u32[]{:S(2)}, u32[]{:S(2)}) async-start(f32[16,1,136,128]{3,2,1,0:T(8,128)} %bitcast.42), calls=%async_computation | async-start | bytes 2228224 | tf_op jit(solution)/shard_map/all_to_all | solution.py:309
  10.5 11.7 %prepare.1 = (f32[20,264,128]{2,1,0:T(8,128)}, bf16[80,128,256]{2,1,0:T(8,128)(2,1)}) custom-call(f32[16,136,128]{2,1,0:T(8,128)} %gather_blocks.1.sent_hbm, s32[1,2,16]{2,1,0:T(2,128)} %bitcast.38, s32[1,2,16]{2,1,0:T(2,128)} %bitcast.40, s32[32]{0:T(128)} %block_ref.1, s32[32]{0:T(128)} %left_ref.1, s32[32]{0:T(128)} %right_ref.1, f32[1024,128]{1,0:T(8,128)} %bitcast.35, ...), custom_call_target="tpu_custom_call" | custom-call | flops 1000000 | bytes 65536 | tf_op jit(solution)/shard_map/prepare/pallas_call | solution.py:320
  22.1 11.0 %all-to-all-done = f32[16,1,136,128]{3,2,1,0:T(8,128)S(1)} async-done(((f32[16,1,136,128]{3,2,1,0:T(8,128)}), f32[16,1,136,128]{3,2,1,0:T(8,128)S(1)}, u32[]{:S(2)}, u32[]{:S(2)}) %all-to-all-start) | async-done | bytes 1114144 | tf_op jit(solution)/shard_map/all_to_all | solution.py:309
  33.1 0.0 copy-start.1
  33.1 0.0 copy-start.2
  33.1 4.3 %arrive.1 = (bf16[16,256,256]{2,1,0:T(8,128)(2,1)S(1)}, f32[16,1,128]{2,1,0:T(1,128)}) custom-call(f32[16,136,128]{2,1,0:T(8,128)S(1)} %bitcast.37, f32[20,264,128]{2,1,0:T(8,128)} %get-tuple-element.8.refs_1_.turned_hbm, bf16[80,128,256]{2,1,0:T(8,128)(2,1)} %get-tuple-element.9.refs_2_.parts_hbm), custom_call_target="tpu_custom_call" | custom-call | tf_op jit(solution)/shard_map/arrive/pallas_call | solution.py:344
  37.4 7.5 %all-to-all-start.1 = ((f32[16,1,128]{2,1,0:T(1,128)}), f32[16,1,128]{2,1,0:T(1,128)S(1)}, u32[]{:S(2)}, u32[]{:S(2)}) async-start(f32[16,1,128]{2,1,0:T(1,128)} %get-tuple-element.12), calls=%async_computation.1 | async-start | bytes 16384 | tf_op jit(solution)/shard_map/all_to_all | solution.py:366
  44.9 0.0 copy-done.1
  44.9 0.0 copy-done.2
  44.9 0.0 copy-start
  44.9 4.0 %remote_terms.1 = (f32[1024,128]{1,0:T(8,128)S(1)}, f32[1024,128]{1,0:T(8,128)}) custom-call(s32[1,2,16]{2,1,0:T(2,128)S(1)} %bitcast.39, s32[1,2,16]{2,1,0:T(2,128)S(1)} %bitcast.41, bf16[16,256,256]{2,1,0:T(8,128)(2,1)S(1)} %get-tuple-element.10.moved_ref, f32[20,264,128]{2,1,0:T(8,128)} %get-tuple-element.8.refs_1_.turned_hbm, ...), custom_call_target="tpu_custom_call" | custom-call | flops 4000000000 | bytes 6291456 | tf_op jit(solution)/shard_map/remote_terms/pallas_call | solution.py:368
  49.0 0.0 all-to-all-done.1.sums_ref
  49.0 0.0 copy-done
  49.0 1.0 %residual.1 = f32[1024,128]{1,0:T(8,128)} custom-call(f32[16,1,128]{2,1,0:T(1,128)S(1)} %all-to-all-done.1.sums_ref, f32[1024,128]{1,0:T(8,128)S(1)} %get-tuple-element.13.hpsi_rows, f32[1024,128]{1,0:T(8,128)S(1)} %bitcast.36), custom_call_target="tpu_custom_call" | custom-call | tf_op jit(solution)/shard_map/residual/pallas_call | solution.py:384
Async XLA Ops:
  2.9 30.2 %all-to-all-start = ((f32[16,1,136,128]{3,2,1,0:T(8,128)}), f32[16,1,136,128]{3,2,1,0:T(8,128)S(1)}, u32[]{:S(2)}, u32[]{:S(2)}) async-start(f32[16,1,136,128]{3,2,1,0:T(8,128)} %bitcast.42), calls=%async_computation | async-start | bytes 2228224 | tf_op jit(solution)/shard_map/all_to_all | solution.py:309
  33.1 11.8 %copy-start.1 = (s32[16,1,2]{0,2,1:T(2,128)S(1)}, s32[16,1,2]{0,2,1:T(2,128)}, u32[]{:S(2)}) copy-start(s32[16,1,2]{0,2,1:T(2,128)} %param.17) | copy-start | bytes 388
  33.1 11.8 %copy-start.2 = (s32[16,1,2]{0,2,1:T(2,128)S(1)}, s32[16,1,2]{0,2,1:T(2,128)}, u32[]{:S(2)}) copy-start(s32[16,1,2]{0,2,1:T(2,128)} %param.18) | copy-start | bytes 388
  37.4 11.6 %all-to-all-start.1 = ((f32[16,1,128]{2,1,0:T(1,128)}), f32[16,1,128]{2,1,0:T(1,128)S(1)}, u32[]{:S(2)}, u32[]{:S(2)}) async-start(f32[16,1,128]{2,1,0:T(1,128)} %get-tuple-element.12), calls=%async_computation.1 | async-start | bytes 16384 | tf_op jit(solution)/shard_map/all_to_all | solution.py:366
  44.9 4.1 %copy-start = (f32[8,16384]{1,0:T(8,128)S(1)}, f32[8,16384]{1,0:T(8,128)}, u32[]{:S(2)}) copy-start(f32[8,16384]{1,0:T(8,128)} %param.11) | copy-start | bytes 1572868

commit v11 on v10

--- a/solution.py
+++ b/solution.py
@@ -223,20 +223,19 @@
         sums_ref[i] = shared
 
 
-def remote_kernel(rindex_ref, out_index_ref, moved_ref, turned_hbm, parts_hbm, hpsi_rows, hpsi_hbm, acc, near_ref, rights_ref, sems):
+def remote_kernel(rindex_ref, out_index_ref, moved_ref, turned_hbm, parts_hbm, hpsi_rows, acc, rights_ref, sems):
     slots, terms, peers = rindex_ref.shape
     senders, height, _ = moved_ref.shape
     sector = height // terms
     rights = rights_ref.shape[0]
-    get_rights = pltpu.make_async_copy(parts_hbm.at[pl.ds(parts_hbm.shape[0] - rights, rights)], rights_ref, sems.at[0])
-    get_rights.start()
-    slabs = []
+    copies = [pltpu.make_async_copy(parts_hbm.at[pl.ds(parts_hbm.shape[0] - rights, rights)], rights_ref, sems.at[0])]
     for k in range(acc.shape[0] // height):
         near = turned_hbm.at[senders + k, pl.ds(0, height)]
-        slabs.append(pltpu.make_async_copy(near, near_ref.at[pl.ds(k * height, height)], sems.at[1 + k]))
-        slabs[k].start()
-    acc[...] = jnp.zeros_like(acc)
-    get_rights.wait()
+        copies.append(pltpu.make_async_copy(near, acc.at[pl.ds(k * height, height)], sems.at[1 + k]))
+    for copy in copies:
+        copy.start()
+    for copy in copies:
+        copy.wait()
 
     def right_step(i, carry):
         slot, peer = i % slots, member(i // slots, peers)
@@ -246,19 +245,15 @@
             acc[pl.ds(spot, sector)] += product(moved_ref[i, g * sector : (g + 1) * sector], twice(right))
         return carry
 
-    lax.fori_loop(0, senders, right_step, 0, unroll=4)
-    for copy in slabs:
-        copy.wait()
+    lax.fori_loop(0, senders, right_step, 0, unroll=8)
     for b in range(acc.shape[0] // sector):
         start = (b // SUB) * (SUB * sector) + b % SUB
-        part = slice(b * sector, (b + 1) * sector)
-        hpsi_rows[pl.ds(start, sector, stride=SUB), :] = acc[part] + near_ref[part]
-    put = pltpu.make_async_copy(hpsi_rows, hpsi_hbm, sems.at[0])
-    put.start()
-    put.wait()
-
-
-def residual_kernel(sums_ref, hpsi_rows, psi_rows, out_ref):
+        hpsi_rows[pl.ds(start, sector, stride=SUB), :] = acc[b * sector : (b + 1) * sector]
+
+
+def residual_kernel(sums_ref, hpsi_rows, psi_rows, hpsi_hbm, out_hbm, out_ref, sems):
+    put_hpsi = pltpu.make_async_copy(hpsi_rows, hpsi_hbm, sems.at[0])
+    put_hpsi.start()
     total = jnp.sum(sums_ref[...], axis=0)
     lane = lax.broadcasted_iota(jnp.int32, total.shape, 1)
     first = lane < total.shape[1] // 2
@@ -266,6 +261,10 @@
     norm = jnp.sum(jnp.where(first, 0.0, total), axis=1, keepdims=True)
     theta = corr / (norm + 1e-06)
     out_ref[...] = hpsi_rows[...] - theta * psi_rows[...]
+    put_out = pltpu.make_async_copy(out_ref, out_hbm, sems.at[1])
+    put_out.start()
+    put_hpsi.wait()
+    put_out.wait()
 
 
 def shards(
@@ -365,13 +364,12 @@
     order = [member(position, peers) for position in range(peers)]
     totals = lax.all_to_all(sums, "renv", split_axis=0, concat_axis=0, tiled=True, axis_index_groups=[order])
 
-    hpsi_rows, hpsi = pl.pallas_call(
+    hpsi_rows = pl.pallas_call(
         remote_kernel,
-        out_shape=(rows, rows),
+        out_shape=rows,
         in_specs=[SMEM] * 2 + [VMEM] + [HBM] * 2,
-        out_specs=(VMEM, HBM),
+        out_specs=VMEM,
         scratch_shapes=[
-            pltpu.VMEM(rows.shape, F32),
             pltpu.VMEM(rows.shape, F32),
             pltpu.VMEM((rights, sector, 2 * sector), BF16),
             pltpu.SemaphoreType.DMA((1 + slabs,)),
@@ -381,11 +379,12 @@
         name="remote_terms",
     )(*by_slot[2:], moved, turned, parts)
 
-    residual_rows = pl.pallas_call(
+    hpsi, residual_rows = pl.pallas_call(
         residual_kernel,
-        out_shape=rows,
+        out_shape=(rows, rows),
         in_specs=[VMEM] * 3,
-        out_specs=VMEM,
+        out_specs=(HBM,) * 2,
+        scratch_shapes=[pltpu.VMEM(rows.shape, F32), pltpu.SemaphoreType.DMA((2,))],
         compiler_params=roomy(16),
         name="residual",
     )(totals, hpsi_rows, psi_rows)

time: 50.3 us -> 50.3 us (level)
  Pallas kernels: 23.3 us -> 22.3 us
  waiting for transfers between devices: 11 us -> 12 us
    all_to_all x1, waiting for transfers between devices: 0.03 us -> 1.05 us  [shards(): lax.all_to_all(sums, 'renv', split_axis=0, concat_axis=0, tiled=True, axi...]
    pallas_call x2, Pallas kernels: 5.03 us -> 4.03 us  [the longest x1 3.03 us: shards(): pl.pallas_call(remote_kernel, out_shape=rows, in_specs=[SMEM] * 2 + [VMEM...]
  transfers between devices with their start and end apart: 2 -> 2, of which waited for: 1 -> 2; matrix products, arithmetic and copies ran while one was open for 0% -> 0% of each run, Pallas kernels for 31% -> 29%
where the time goes in v11:
time: 50.3 us; the launch traced here: 50 us
  Pallas kernels  22.3 us (44%)
  starting transfers between devices  15 us (30%)
  waiting for transfers between devices  12 us (24%)
  between operations  0.68 us (1%)
    pallas_call x1, Pallas kernels, shards(): pl.pallas_call(prepare_kernel, out_shape=(jax.ShapeDtypeStruct((count + s...  11.7 us
    all_to_all x1, waiting for transfers between devices, shards(): lax.all_to_all(sent.reshape(peers, slots, height, sector), 'renv', split_...  11 us
    all_to_all x1, starting transfers between devices, shards(): lax.all_to_all(sent.reshape(peers, slots, height, sector), 'renv', split_...  7.56 us
    all_to_all x1, starting transfers between devices, shards(): lax.all_to_all(sums, 'renv', split_axis=0, concat_axis=0, tiled=True, axi...  7.47 us
    pallas_call x1, Pallas kernels, shards(): pl.pallas_call(lambda *refs: arrive_kernel(terms, *refs), out_shape=(jax....  4.34 us
    pallas_call x1, Pallas kernels, shards(): pl.pallas_call(remote_kernel, out_shape=rows, in_specs=[SMEM] * 2 + [VMEM...  3.03 us
    pallas_call x1, Pallas kernels, shards(): pl.pallas_call(gather_kernel, out_shape=blocks, in_specs=[SMEM] * 3 + [VM...  2.28 us
    all_to_all x1, waiting for transfers between devices, shards(): lax.all_to_all(sums, 'renv', split_axis=0, concat_axis=0, tiled=True, axi...  1.05 us
  transfers between devices with their start and end apart: 2, of which 2 were waited for; matrix products, arithmetic and copies ran while one was open for 0% of the time, Pallas kernels for 29%

profile of v11, /device:TPU:0, one launch (start us, length us, event | category | flops | bytes accessed | tf_op | source)
XLA Modules:
  0.0 50.0 jit_solution(895679573132981561)
XLA Ops:
  0.6 2.3 %gather_blocks.1.sent_hbm = f32[16,136,128]{2,1,0:T(8,128)} custom-call(s32[16]{0:T(128)} %bitcast.47, s32[1,2,16]{2,1,0:T(2,128)} %bitcast.45, s32[1,2,16]{2,1,0:T(2,128)} %bitcast.46, f32[1024,128]{1,0:T(8,128)} %bitcast.34), custom_call_target="tpu_custom_call" | custom-call | tf_op jit(solution)/shard_map/gather_blocks/pallas_call | solution.py:299
  2.9 7.6 %all-to-all-start = ((f32[16,1,136,128]{3,2,1,0:T(8,128)}), f32[16,1,136,128]{3,2,1,0:T(8,128)S(1)}, u32[]{:S(2)}, u32[]{:S(2)}) async-start(f32[16,1,136,128]{3,2,1,0:T(8,128)} %bitcast.42), calls=%async_computation | async-start | bytes 2228224 | tf_op jit(solution)/shard_map/all_to_all | solution.py:308
  10.5 11.7 %prepare.1 = (f32[20,264,128]{2,1,0:T(8,128)}, bf16[80,128,256]{2,1,0:T(8,128)(2,1)}) custom-call(f32[16,136,128]{2,1,0:T(8,128)} %gather_blocks.1.sent_hbm, s32[1,2,16]{2,1,0:T(2,128)} %bitcast.38, s32[1,2,16]{2,1,0:T(2,128)} %bitcast.40, s32[32]{0:T(128)} %block_ref.1, s32[32]{0:T(128)} %left_ref.1, s32[32]{0:T(128)} %right_ref.1, f32[1024,128]{1,0:T(8,128)} %bitcast.35, ...), custom_call_target="tpu_custom_call" | custom-call | flops 1000000 | bytes 65536 | tf_op jit(solution)/shard_map/prepare/pallas_call | solution.py:319
  22.1 11.0 %all-to-all-done = f32[16,1,136,128]{3,2,1,0:T(8,128)S(1)} async-done(((f32[16,1,136,128]{3,2,1,0:T(8,128)}), f32[16,1,136,128]{3,2,1,0:T(8,128)S(1)}, u32[]{:S(2)}, u32[]{:S(2)}) %all-to-all-start) | async-done | bytes 1114144 | tf_op jit(solution)/shard_map/all_to_all | solution.py:308
  33.1 0.0 copy-start.1
  33.1 0.0 copy-start.2
  33.1 4.3 %arrive.1 = (bf16[16,256,256]{2,1,0:T(8,128)(2,1)S(1)}, f32[16,1,128]{2,1,0:T(1,128)}) custom-call(f32[16,136,128]{2,1,0:T(8,128)S(1)} %bitcast.37, f32[20,264,128]{2,1,0:T(8,128)} %get-tuple-element.8.refs_1_.turned_hbm, bf16[80,128,256]{2,1,0:T(8,128)(2,1)} %get-tuple-element.9.refs_2_.parts_hbm), custom_call_target="tpu_custom_call" | custom-call | tf_op jit(solution)/shard_map/arrive/pallas_call | solution.py:343
  37.5 7.5 %all-to-all-start.1 = ((f32[16,1,128]{2,1,0:T(1,128)}), f32[16,1,128]{2,1,0:T(1,128)S(1)}, u32[]{:S(2)}, u32[]{:S(2)}) async-start(f32[16,1,128]{2,1,0:T(1,128)} %get-tuple-element.10), calls=%async_computation.1 | async-start | bytes 16384 | tf_op jit(solution)/shard_map/all_to_all | solution.py:365
  44.9 0.0 copy-done.1
  44.9 0.0 copy-done.2
  44.9 0.0 copy-start
  44.9 3.0 %remote_terms.1.hpsi_rows = f32[1024,128]{1,0:T(8,128)S(1)} custom-call(s32[1,2,16]{2,1,0:T(2,128)S(1)} %bitcast.39, s32[1,2,16]{2,1,0:T(2,128)S(1)} %bitcast.41, bf16[16,256,256]{2,1,0:T(8,128)(2,1)S(1)} %get-tuple-element.11.moved_ref, f32[20,264,128]{2,1,0:T(8,128)} %get-tuple-element.8.refs_1_.turned_hbm, ...), custom_call_target="tpu_custom_call" | custom-call | flops 4000000000 | bytes 6291456 | tf_op jit(solution)/shard_map/remote_terms/pallas_call | solution.py:367
  48.0 1.1 %all-to-all-done.1.sums_ref = f32[16,1,128]{2,1,0:T(1,128)S(1)} async-done(((f32[16,1,128]{2,1,0:T(1,128)}), f32[16,1,128]{2,1,0:T(1,128)S(1)}, u32[]{:S(2)}, u32[]{:S(2)}) %all-to-all-start.1) | async-done | bytes 8224 | tf_op jit(solution)/shard_map/all_to_all | solution.py:365
  49.0 0.0 copy-done
  49.0 1.0 %residual.1 = (f32[1024,128]{1,0:T(8,128)}, f32[1024,128]{1,0:T(8,128)}) custom-call(f32[16,1,128]{2,1,0:T(1,128)S(1)} %all-to-all-done.1.sums_ref, f32[1024,128]{1,0:T(8,128)S(1)} %remote_terms.1.hpsi_rows, f32[1024,128]{1,0:T(8,128)S(1)} %bitcast.36), custom_call_target="tpu_custom_call" | custom-call | tf_op jit(solution)/shard_map/residual/pallas_call | solution.py:382
Async XLA Ops:
  2.9 30.2 %all-to-all-start = ((f32[16,1,136,128]{3,2,1,0:T(8,128)}), f32[16,1,136,128]{3,2,1,0:T(8,128)S(1)}, u32[]{:S(2)}, u32[]{:S(2)}) async-start(f32[16,1,136,128]{3,2,1,0:T(8,128)} %bitcast.42), calls=%async_computation | async-start | bytes 2228224 | tf_op jit(solution)/shard_map/all_to_all | solution.py:308
  33.1 11.8 %copy-start.1 = (s32[16,1,2]{0,2,1:T(2,128)S(1)}, s32[16,1,2]{0,2,1:T(2,128)}, u32[]{:S(2)}) copy-start(s32[16,1,2]{0,2,1:T(2,128)} %param.17) | copy-start | bytes 388
  33.1 11.8 %copy-start.2 = (s32[16,1,2]{0,2,1:T(2,128)S(1)}, s32[16,1,2]{0,2,1:T(2,128)}, u32[]{:S(2)}) copy-start(s32[16,1,2]{0,2,1:T(2,128)} %param.18) | copy-start | bytes 388
  37.5 11.6 %all-to-all-start.1 = ((f32[16,1,128]{2,1,0:T(1,128)}), f32[16,1,128]{2,1,0:T(1,128)S(1)}, u32[]{:S(2)}, u32[]{:S(2)}) async-start(f32[16,1,128]{2,1,0:T(1,128)} %get-tuple-element.10), calls=%async_computation.1 | async-start | bytes 16384 | tf_op jit(solution)/shard_map/all_to_all | solution.py:365
  44.9 4.1 %copy-start = (f32[8,16384]{1,0:T(8,128)S(1)}, f32[8,16384]{1,0:T(8,128)}, u32[]{:S(2)}) copy-start(f32[8,16384]{1,0:T(8,128)} %param.11) | copy-start | bytes 1572868

commit v12 on v11

--- a/solution.py
+++ b/solution.py
@@ -362,6 +362,7 @@
         sums = share if count == chunk else sums + share
     moved = moved[0] if len(moved) == 1 else jnp.concatenate(moved, axis=0)
     order = [member(position, peers) for position in range(peers)]
+    order = order[:1] + order[:0:-1]
     totals = lax.all_to_all(sums, "renv", split_axis=0, concat_axis=0, tiled=True, axis_index_groups=[order])
 
     hpsi_rows = pl.pallas_call(

time: 50.3 us -> 50.3 us (level)
  no operation moved by 1% of the time
where the time goes in v12:
time: 50.3 us; the launch traced here: 50 us
  Pallas kernels  22.3 us (44%)
  starting transfers between devices  15.1 us (30%)
  waiting for transfers between devices  11.9 us (24%)
  between operations  0.68 us (1%)
    pallas_call x1, Pallas kernels, shards(): pl.pallas_call(prepare_kernel, out_shape=(jax.ShapeDtypeStruct((count + s...  11.7 us
    all_to_all x1, waiting for transfers between devices, shards(): lax.all_to_all(sent.reshape(peers, slots, height, sector), 'renv', split_...  11 us
    all_to_all x1, starting transfers between devices, shards(): lax.all_to_all(sums, 'renv', split_axis=0, concat_axis=0, tiled=True, axi...  7.59 us
    all_to_all x1, starting transfers between devices, shards(): lax.all_to_all(sent.reshape(peers, slots, height, sector), 'renv', split_...  7.56 us
    pallas_call x1, Pallas kernels, shards(): pl.pallas_call(lambda *refs: arrive_kernel(terms, *refs), out_shape=(jax....  4.34 us
    pallas_call x1, Pallas kernels, shards(): pl.pallas_call(remote_kernel, out_shape=rows, in_specs=[SMEM] * 2 + [VMEM...  3.04 us
    pallas_call x1, Pallas kernels, shards(): pl.pallas_call(gather_kernel, out_shape=blocks, in_specs=[SMEM] * 3 + [VM...  2.28 us
  transfers between devices with their start and end apart: 2, of which 2 were waited for; matrix products, arithmetic and copies ran while one was open for 0% of the time, Pallas kernels for 29%

profile of v12, /device:TPU:0, one launch (start us, length us, event | category | flops | bytes accessed | tf_op | source)
XLA Modules:
  0.0 50.0 jit_solution(8106566742310832862)
XLA Ops:
  0.6 2.3 %gather_blocks.1.sent_hbm = f32[16,136,128]{2,1,0:T(8,128)} custom-call(s32[16]{0:T(128)} %bitcast.47, s32[1,2,16]{2,1,0:T(2,128)} %bitcast.45, s32[1,2,16]{2,1,0:T(2,128)} %bitcast.46, f32[1024,128]{1,0:T(8,128)} %bitcast.34), custom_call_target="tpu_custom_call" | custom-call | tf_op jit(solution)/shard_map/gather_blocks/pallas_call | solution.py:299
  2.9 7.6 %all-to-all-start = ((f32[16,1,136,128]{3,2,1,0:T(8,128)}), f32[16,1,136,128]{3,2,1,0:T(8,128)S(1)}, u32[]{:S(2)}, u32[]{:S(2)}) async-start(f32[16,1,136,128]{3,2,1,0:T(8,128)} %bitcast.42), calls=%async_computation | async-start | bytes 2228224 | tf_op jit(solution)/shard_map/all_to_all | solution.py:308
  10.5 11.7 %prepare.1 = (f32[20,264,128]{2,1,0:T(8,128)}, bf16[80,128,256]{2,1,0:T(8,128)(2,1)}) custom-call(f32[16,136,128]{2,1,0:T(8,128)} %gather_blocks.1.sent_hbm, s32[1,2,16]{2,1,0:T(2,128)} %bitcast.38, s32[1,2,16]{2,1,0:T(2,128)} %bitcast.40, s32[32]{0:T(128)} %block_ref.1, s32[32]{0:T(128)} %left_ref.1, s32[32]{0:T(128)} %right_ref.1, f32[1024,128]{1,0:T(8,128)} %bitcast.35, ...), custom_call_target="tpu_custom_call" | custom-call | flops 1000000 | bytes 65536 | tf_op jit(solution)/shard_map/prepare/pallas_call | solution.py:319
  22.1 11.0 %all-to-all-done = f32[16,1,136,128]{3,2,1,0:T(8,128)S(1)} async-done(((f32[16,1,136,128]{3,2,1,0:T(8,128)}), f32[16,1,136,128]{3,2,1,0:T(8,128)S(1)}, u32[]{:S(2)}, u32[]{:S(2)}) %all-to-all-start) | async-done | bytes 1114144 | tf_op jit(solution)/shard_map/all_to_all | solution.py:308
  33.1 0.0 copy-start.1
  33.1 0.0 copy-start.2
  33.1 4.3 %arrive.1 = (bf16[16,256,256]{2,1,0:T(8,128)(2,1)S(1)}, f32[16,1,128]{2,1,0:T(1,128)}) custom-call(f32[16,136,128]{2,1,0:T(8,128)S(1)} %bitcast.37, f32[20,264,128]{2,1,0:T(8,128)} %get-tuple-element.8.refs_1_.turned_hbm, bf16[80,128,256]{2,1,0:T(8,128)(2,1)} %get-tuple-element.9.refs_2_.parts_hbm), custom_call_target="tpu_custom_call" | custom-call | tf_op jit(solution)/shard_map/arrive/pallas_call | solution.py:343
  37.5 7.6 %all-to-all-start.1 = ((f32[16,1,128]{2,1,0:T(1,128)}), f32[16,1,128]{2,1,0:T(1,128)S(1)}, u32[]{:S(2)}, u32[]{:S(2)}) async-start(f32[16,1,128]{2,1,0:T(1,128)} %get-tuple-element.10), calls=%async_computation.1 | async-start | bytes 16384 | tf_op jit(solution)/shard_map/all_to_all | solution.py:366
  45.0 0.0 copy-done.1
  45.0 0.0 copy-done.2
  45.1 0.0 copy-start
  45.1 3.0 %remote_terms.1.hpsi_rows = f32[1024,128]{1,0:T(8,128)S(1)} custom-call(s32[1,2,16]{2,1,0:T(2,128)S(1)} %bitcast.39, s32[1,2,16]{2,1,0:T(2,128)S(1)} %bitcast.41, bf16[16,256,256]{2,1,0:T(8,128)(2,1)S(1)} %get-tuple-element.11.moved_ref, f32[20,264,128]{2,1,0:T(8,128)} %get-tuple-element.8.refs_1_.turned_hbm, ...), custom_call_target="tpu_custom_call" | custom-call | flops 4000000000 | bytes 6291456 | tf_op jit(solution)/shard_map/remote_terms/pallas_call | solution.py:368
  48.1 0.9 %all-to-all-done.1.sums_ref = f32[16,1,128]{2,1,0:T(1,128)S(1)} async-done(((f32[16,1,128]{2,1,0:T(1,128)}), f32[16,1,128]{2,1,0:T(1,128)S(1)}, u32[]{:S(2)}, u32[]{:S(2)}) %all-to-all-start.1) | async-done | bytes 8224 | tf_op jit(solution)/shard_map/all_to_all | solution.py:366
  49.0 0.0 copy-done
  49.0 1.0 %residual.1 = (f32[1024,128]{1,0:T(8,128)}, f32[1024,128]{1,0:T(8,128)}) custom-call(f32[16,1,128]{2,1,0:T(1,128)S(1)} %all-to-all-done.1.sums_ref, f32[1024,128]{1,0:T(8,128)S(1)} %remote_terms.1.hpsi_rows, f32[1024,128]{1,0:T(8,128)S(1)} %bitcast.36), custom_call_target="tpu_custom_call" | custom-call | tf_op jit(solution)/shard_map/residual/pallas_call | solution.py:383
Async XLA Ops:
  2.9 30.2 %all-to-all-start = ((f32[16,1,136,128]{3,2,1,0:T(8,128)}), f32[16,1,136,128]{3,2,1,0:T(8,128)S(1)}, u32[]{:S(2)}, u32[]{:S(2)}) async-start(f32[16,1,136,128]{3,2,1,0:T(8,128)} %bitcast.42), calls=%async_computation | async-start | bytes 2228224 | tf_op jit(solution)/shard_map/all_to_all | solution.py:308
  33.1 11.9 %copy-start.1 = (s32[16,1,2]{0,2,1:T(2,128)S(1)}, s32[16,1,2]{0,2,1:T(2,128)}, u32[]{:S(2)}) copy-start(s32[16,1,2]{0,2,1:T(2,128)} %param.17) | copy-start | bytes 388
  33.1 11.9 %copy-start.2 = (s32[16,1,2]{0,2,1:T(2,128)S(1)}, s32[16,1,2]{0,2,1:T(2,128)}, u32[]{:S(2)}) copy-start(s32[16,1,2]{0,2,1:T(2,128)} %param.18) | copy-start | bytes 388
  37.5 11.6 %all-to-all-start.1 = ((f32[16,1,128]{2,1,0:T(1,128)}), f32[16,1,128]{2,1,0:T(1,128)S(1)}, u32[]{:S(2)}, u32[]{:S(2)}) async-start(f32[16,1,128]{2,1,0:T(1,128)} %get-tuple-element.10), calls=%async_computation.1 | async-start | bytes 16384 | tf_op jit(solution)/shard_map/all_to_all | solution.py:366
  45.1 4.0 %copy-start = (f32[8,16384]{1,0:T(8,128)S(1)}, f32[8,16384]{1,0:T(8,128)}, u32[]{:S(2)}) copy-start(f32[8,16384]{1,0:T(8,128)} %param.11) | copy-start | bytes 1572868

commit v13 on v12

--- a/solution.py
+++ b/solution.py
@@ -76,7 +76,7 @@
 def member(position, peers):
     if peers % 2:
         return position
-    middle = peers // 2 + 1
+    middle = min(peers // 2 + 3, peers - 1)
     return position + middle * (position == 0) - 1 * (position > 0) + 1 * (position > middle)
 
 

time: 50.3 us -> 50.4 us (level)
  starting transfers between devices: 15.1 us -> 18 us
  waiting for transfers between devices: 11.9 us -> 9.14 us
    all_to_all x1, starting transfers between devices: 7.59 us -> 10.1 us  [shards(): lax.all_to_all(sums, 'renv', split_axis=0, concat_axis=0, tiled=True, axi...]
    all_to_all x1, waiting for transfers between devices: 11 us -> 9.12 us  [shards(): lax.all_to_all(sent.reshape(peers, slots, height, sector), 'renv', split_...]
    all_to_all x1, waiting for transfers between devices: 0.9 us -> 0.02 us  [shards(): lax.all_to_all(sums, 'renv', split_axis=0, concat_axis=0, tiled=True, axi...]
  transfers between devices with their start and end apart: 2 -> 2, of which waited for: 2 -> 1; matrix products, arithmetic and copies ran while one was open for 0% -> 0% of each run, Pallas kernels for 29% -> 29%
where the time goes in v13:
time: 50.4 us; the launch traced here: 50.1 us
  Pallas kernels  22.3 us (44%)
  starting transfers between devices  18 us (36%)
  waiting for transfers between devices  9.14 us (18%)
  between operations  0.68 us (1%)
    pallas_call x1, Pallas kernels, shards(): pl.pallas_call(prepare_kernel, out_shape=(jax.ShapeDtypeStruct((count + s...  11.7 us
    all_to_all x1, starting transfers between devices, shards(): lax.all_to_all(sums, 'renv', split_axis=0, concat_axis=0, tiled=True, axi...  10.1 us
    all_to_all x1, waiting for transfers between devices, shards(): lax.all_to_all(sent.reshape(peers, slots, height, sector), 'renv', split_...  9.12 us
    all_to_all x1, starting transfers between devices, shards(): lax.all_to_all(sent.reshape(peers, slots, height, sector), 'renv', split_...  7.9 us
    pallas_call x1, Pallas kernels, shards(): pl.pallas_call(lambda *refs: arrive_kernel(terms, *refs), out_shape=(jax....  4.34 us
    pallas_call x1, Pallas kernels, shards(): pl.pallas_call(remote_kernel, out_shape=rows, in_specs=[SMEM] * 2 + [VMEM...  3.03 us
    pallas_call x1, Pallas kernels, shards(): pl.pallas_call(gather_kernel, out_shape=blocks, in_specs=[SMEM] * 3 + [VM...  2.28 us
  transfers between devices with their start and end apart: 2, of which 1 were waited for; matrix products, arithmetic and copies ran while one was open for 0% of the time, Pallas kernels for 29%

profile of v13, /device:TPU:0, one launch (start us, length us, event | category | flops | bytes accessed | tf_op | source)
XLA Modules:
  0.0 50.1 jit_solution(4827430632486413309)
XLA Ops:
  0.6 2.3 %gather_blocks.1.sent_hbm = f32[16,136,128]{2,1,0:T(8,128)} custom-call(s32[16]{0:T(128)} %bitcast.47, s32[1,2,16]{2,1,0:T(2,128)} %bitcast.45, s32[1,2,16]{2,1,0:T(2,128)} %bitcast.46, f32[1024,128]{1,0:T(8,128)} %bitcast.34), custom_call_target="tpu_custom_call" | custom-call | tf_op jit(solution)/shard_map/gather_blocks/pallas_call | solution.py:299
  2.9 7.9 %all-to-all-start = ((f32[16,1,136,128]{3,2,1,0:T(8,128)}), f32[16,1,136,128]{3,2,1,0:T(8,128)S(1)}, u32[]{:S(2)}, u32[]{:S(2)}) async-start(f32[16,1,136,128]{3,2,1,0:T(8,128)} %bitcast.42), calls=%async_computation | async-start | bytes 2228224 | tf_op jit(solution)/shard_map/all_to_all | solution.py:308
  10.8 11.7 %prepare.1 = (f32[20,264,128]{2,1,0:T(8,128)}, bf16[80,128,256]{2,1,0:T(8,128)(2,1)}) custom-call(f32[16,136,128]{2,1,0:T(8,128)} %gather_blocks.1.sent_hbm, s32[1,2,16]{2,1,0:T(2,128)} %bitcast.38, s32[1,2,16]{2,1,0:T(2,128)} %bitcast.40, s32[32]{0:T(128)} %block_ref.1, s32[32]{0:T(128)} %left_ref.1, s32[32]{0:T(128)} %right_ref.1, f32[1024,128]{1,0:T(8,128)} %bitcast.35, ...), custom_call_target="tpu_custom_call" | custom-call | flops 1000000 | bytes 65536 | tf_op jit(solution)/shard_map/prepare/pallas_call | solution.py:319
  22.5 9.1 %all-to-all-done = f32[16,1,136,128]{3,2,1,0:T(8,128)S(1)} async-done(((f32[16,1,136,128]{3,2,1,0:T(8,128)}), f32[16,1,136,128]{3,2,1,0:T(8,128)S(1)}, u32[]{:S(2)}, u32[]{:S(2)}) %all-to-all-start) | async-done | bytes 1114144 | tf_op jit(solution)/shard_map/all_to_all | solution.py:308
  31.6 0.0 copy-start.1
  31.6 0.0 copy-start.2
  31.6 4.3 %arrive.1 = (bf16[16,256,256]{2,1,0:T(8,128)(2,1)S(1)}, f32[16,1,128]{2,1,0:T(1,128)}) custom-call(f32[16,136,128]{2,1,0:T(8,128)S(1)} %bitcast.37, f32[20,264,128]{2,1,0:T(8,128)} %get-tuple-element.8.refs_1_.turned_hbm, bf16[80,128,256]{2,1,0:T(8,128)(2,1)} %get-tuple-element.9.refs_2_.parts_hbm), custom_call_target="tpu_custom_call" | custom-call | tf_op jit(solution)/shard_map/arrive/pallas_call | solution.py:343
  36.0 10.1 %all-to-all-start.1 = ((f32[16,1,128]{2,1,0:T(1,128)}), f32[16,1,128]{2,1,0:T(1,128)S(1)}, u32[]{:S(2)}, u32[]{:S(2)}) async-start(f32[16,1,128]{2,1,0:T(1,128)} %get-tuple-element.10), calls=%async_computation.1 | async-start | bytes 16384 | tf_op jit(solution)/shard_map/all_to_all | solution.py:366
  46.0 0.0 copy-done.1
  46.0 0.0 copy-done.2
  46.0 0.0 copy-start
  46.0 3.0 %remote_terms.1.hpsi_rows = f32[1024,128]{1,0:T(8,128)S(1)} custom-call(s32[1,2,16]{2,1,0:T(2,128)S(1)} %bitcast.39, s32[1,2,16]{2,1,0:T(2,128)S(1)} %bitcast.41, bf16[16,256,256]{2,1,0:T(8,128)(2,1)S(1)} %get-tuple-element.11.moved_ref, f32[20,264,128]{2,1,0:T(8,128)} %get-tuple-element.8.refs_1_.turned_hbm, ...), custom_call_target="tpu_custom_call" | custom-call | flops 4000000000 | bytes 6291456 | tf_op jit(solution)/shard_map/remote_terms/pallas_call | solution.py:368
  49.1 0.0 all-to-all-done.1.sums_ref
  49.1 0.0 copy-done
  49.1 1.0 %residual.1 = (f32[1024,128]{1,0:T(8,128)}, f32[1024,128]{1,0:T(8,128)}) custom-call(f32[16,1,128]{2,1,0:T(1,128)S(1)} %all-to-all-done.1.sums_ref, f32[1024,128]{1,0:T(8,128)S(1)} %remote_terms.1.hpsi_rows, f32[1024,128]{1,0:T(8,128)S(1)} %bitcast.36), custom_call_target="tpu_custom_call" | custom-call | tf_op jit(solution)/shard_map/residual/pallas_call | solution.py:383
Async XLA Ops:
  2.9 28.7 %all-to-all-start = ((f32[16,1,136,128]{3,2,1,0:T(8,128)}), f32[16,1,136,128]{3,2,1,0:T(8,128)S(1)}, u32[]{:S(2)}, u32[]{:S(2)}) async-start(f32[16,1,136,128]{3,2,1,0:T(8,128)} %bitcast.42), calls=%async_computation | async-start | bytes 2228224 | tf_op jit(solution)/shard_map/all_to_all | solution.py:308
  31.6 14.4 %copy-start.1 = (s32[16,1,2]{0,2,1:T(2,128)S(1)}, s32[16,1,2]{0,2,1:T(2,128)}, u32[]{:S(2)}) copy-start(s32[16,1,2]{0,2,1:T(2,128)} %param.17) | copy-start | bytes 388
  31.6 14.4 %copy-start.2 = (s32[16,1,2]{0,2,1:T(2,128)S(1)}, s32[16,1,2]{0,2,1:T(2,128)}, u32[]{:S(2)}) copy-start(s32[16,1,2]{0,2,1:T(2,128)} %param.18) | copy-start | bytes 388
  36.0 13.1 %all-to-all-start.1 = ((f32[16,1,128]{2,1,0:T(1,128)}), f32[16,1,128]{2,1,0:T(1,128)S(1)}, u32[]{:S(2)}, u32[]{:S(2)}) async-start(f32[16,1,128]{2,1,0:T(1,128)} %get-tuple-element.10), calls=%async_computation.1 | async-start | bytes 16384 | tf_op jit(solution)/shard_map/all_to_all | solution.py:366
  46.0 3.1 %copy-start = (f32[8,16384]{1,0:T(8,128)S(1)}, f32[8,16384]{1,0:T(8,128)}, u32[]{:S(2)}) copy-start(f32[8,16384]{1,0:T(8,128)} %param.11) | copy-start | bytes 1572868

commit v14 on v12

--- a/solution.py
+++ b/solution.py
@@ -80,22 +80,28 @@
     return position + middle * (position == 0) - 1 * (position > 0) + 1 * (position > middle)
 
 
-def gather_kernel(block_ref, left_ref, live_ref, psi_rows, out_hbm, stage, sems):
+def gather_kernel(block_ref, left_ref, live_ref, psi_rows, out_hbm, mats, tails, sems):
     slots, terms, peers = left_ref.shape
-    sector = psi_rows.shape[1]
+    owned, sector, _ = mats.shape
+    count = tails.shape[0]
+    for b in range(owned):
+        mats[b] = pick(psi_rows, b)
+    puts = []
+    for i in range(count):
+        slot, peer = i % slots, member(i // slots, peers)
+        block = mats.at[block_ref[peer * slots + slot]]
+        puts.append(pltpu.make_async_copy(block, out_hbm.at[i, pl.ds(0, sector)], sems.at[i]))
+        puts[i].start()
     lane = lax.broadcasted_iota(jnp.int32, (SUB, sector), 1)
-    puts = []
-    for i in range(stage.shape[0]):
+    for i in range(count):
         slot, peer = i % slots, member(i // slots, peers)
-        stage[i, :sector] = pick(psi_rows, block_ref[peer * slots + slot])
         values = jnp.zeros(lane.shape, jnp.int32)
         for g in range(terms):
             values = jnp.where(lane == g, left_ref[slot, g, peer], values)
             values = jnp.where(lane == terms + g, live_ref[slot, g, peer], values)
-        stage[i, sector:] = values.astype(F32)
-        put = pltpu.make_async_copy(stage.at[i], out_hbm.at[i], sems.at[i])
-        put.start()
-        puts.append(put)
+        tails[i] = values.astype(F32)
+    puts.append(pltpu.make_async_copy(tails, out_hbm.at[:, pl.ds(sector, SUB)], sems.at[count]))
+    puts[count].start()
     for put in puts:
         put.wait()
 
@@ -301,7 +307,11 @@
         out_shape=blocks,
         in_specs=[SMEM] * 3 + [VMEM],
         out_specs=HBM,
-        scratch_shapes=[pltpu.VMEM(blocks.shape, F32), pltpu.SemaphoreType.DMA((count,))],
+        scratch_shapes=[
+            pltpu.VMEM((owned, sector, sector), F32),
+            pltpu.VMEM((count, SUB, sector), F32),
+            pltpu.SemaphoreType.DMA((count + 1,)),
+        ],
         compiler_params=roomy(56),
         name="gather_blocks",
     )(send_block.reshape(-1), *by_slot[:2], psi_rows)

time: 50.3 us -> 50.4 us (level)
  no operation moved by 1% of the time
where the time goes in v14:
time: 50.4 us; the launch traced here: 50.1 us
  Pallas kernels  22.4 us (44%)
  starting transfers between devices  15.1 us (30%)
  waiting for transfers between devices  11.9 us (24%)
  between operations  0.68 us (1%)
    pallas_call x1, Pallas kernels, shards(): pl.pallas_call(prepare_kernel, out_shape=(jax.ShapeDtypeStruct((count + s...  11.7 us
    all_to_all x1, waiting for transfers between devices, shards(): lax.all_to_all(sent.reshape(peers, slots, height, sector), 'renv', split_...  11 us
    all_to_all x1, starting transfers between devices, shards(): lax.all_to_all(sums, 'renv', split_axis=0, concat_axis=0, tiled=True, axi...  7.59 us
    all_to_all x1, starting transfers between devices, shards(): lax.all_to_all(sent.reshape(peers, slots, height, sector), 'renv', split_...  7.56 us
    pallas_call x1, Pallas kernels, shards(): pl.pallas_call(lambda *refs: arrive_kernel(terms, *refs), out_shape=(jax....  4.34 us
    pallas_call x1, Pallas kernels, shards(): pl.pallas_call(remote_kernel, out_shape=rows, in_specs=[SMEM] * 2 + [VMEM...  3.03 us
    pallas_call x1, Pallas kernels, shards(): pl.pallas_call(gather_kernel, out_shape=blocks, in_specs=[SMEM] * 3 + [VM...  2.36 us
  transfers between devices with their start and end apart: 2, of which 2 were waited for; matrix products, arithmetic and copies ran while one was open for 0% of the time, Pallas kernels for 29%

profile of v14, /device:TPU:0, one launch (start us, length us, event | category | flops | bytes accessed | tf_op | source)
XLA Modules:
  0.0 50.1 jit_solution(15520676757728769587)
XLA Ops:
  0.6 2.4 %gather_blocks.1.sent_hbm = f32[16,136,128]{2,1,0:T(8,128)} custom-call(s32[16]{0:T(128)} %bitcast.47, s32[1,2,16]{2,1,0:T(2,128)} %bitcast.45, s32[1,2,16]{2,1,0:T(2,128)} %bitcast.46, f32[1024,128]{1,0:T(8,128)} %bitcast.34), custom_call_target="tpu_custom_call" | custom-call | tf_op jit(solution)/shard_map/gather_blocks/pallas_call | solution.py:305
  3.0 7.6 %all-to-all-start = ((f32[16,1,136,128]{3,2,1,0:T(8,128)}), f32[16,1,136,128]{3,2,1,0:T(8,128)S(1)}, u32[]{:S(2)}, u32[]{:S(2)}) async-start(f32[16,1,136,128]{3,2,1,0:T(8,128)} %bitcast.42), calls=%async_computation | async-start | bytes 2228224 | tf_op jit(solution)/shard_map/all_to_all | solution.py:318
  10.6 11.7 %prepare.1 = (f32[20,264,128]{2,1,0:T(8,128)}, bf16[80,128,256]{2,1,0:T(8,128)(2,1)}) custom-call(f32[16,136,128]{2,1,0:T(8,128)} %gather_blocks.1.sent_hbm, s32[1,2,16]{2,1,0:T(2,128)} %bitcast.38, s32[1,2,16]{2,1,0:T(2,128)} %bitcast.40, s32[32]{0:T(128)} %block_ref.1, s32[32]{0:T(128)} %left_ref.1, s32[32]{0:T(128)} %right_ref.1, f32[1024,128]{1,0:T(8,128)} %bitcast.35, ...), custom_call_target="tpu_custom_call" | custom-call | flops 1000000 | bytes 65536 | tf_op jit(solution)/shard_map/prepare/pallas_call | solution.py:329
  22.2 11.0 %all-to-all-done = f32[16,1,136,128]{3,2,1,0:T(8,128)S(1)} async-done(((f32[16,1,136,128]{3,2,1,0:T(8,128)}), f32[16,1,136,128]{3,2,1,0:T(8,128)S(1)}, u32[]{:S(2)}, u32[]{:S(2)}) %all-to-all-start) | async-done | bytes 1114144 | tf_op jit(solution)/shard_map/all_to_all | solution.py:318
  33.2 0.0 copy-start.1
  33.2 0.0 copy-start.2
  33.2 4.3 %arrive.1 = (bf16[16,256,256]{2,1,0:T(8,128)(2,1)S(1)}, f32[16,1,128]{2,1,0:T(1,128)}) custom-call(f32[16,136,128]{2,1,0:T(8,128)S(1)} %bitcast.37, f32[20,264,128]{2,1,0:T(8,128)} %get-tuple-element.8.refs_1_.turned_hbm, bf16[80,128,256]{2,1,0:T(8,128)(2,1)} %get-tuple-element.9.refs_2_.parts_hbm), custom_call_target="tpu_custom_call" | custom-call | tf_op jit(solution)/shard_map/arrive/pallas_call | solution.py:353
  37.5 7.6 %all-to-all-start.1 = ((f32[16,1,128]{2,1,0:T(1,128)}), f32[16,1,128]{2,1,0:T(1,128)S(1)}, u32[]{:S(2)}, u32[]{:S(2)}) async-start(f32[16,1,128]{2,1,0:T(1,128)} %get-tuple-element.10), calls=%async_computation.1 | async-start | bytes 16384 | tf_op jit(solution)/shard_map/all_to_all | solution.py:376
  45.1 0.0 copy-done.1
  45.1 0.0 copy-done.2
  45.1 0.0 copy-start
  45.2 3.0 %remote_terms.1.hpsi_rows = f32[1024,128]{1,0:T(8,128)S(1)} custom-call(s32[1,2,16]{2,1,0:T(2,128)S(1)} %bitcast.39, s32[1,2,16]{2,1,0:T(2,128)S(1)} %bitcast.41, bf16[16,256,256]{2,1,0:T(8,128)(2,1)S(1)} %get-tuple-element.11.moved_ref, f32[20,264,128]{2,1,0:T(8,128)} %get-tuple-element.8.refs_1_.turned_hbm, ...), custom_call_target="tpu_custom_call" | custom-call | flops 4000000000 | bytes 6291456 | tf_op jit(solution)/shard_map/remote_terms/pallas_call | solution.py:378
  48.2 0.9 %all-to-all-done.1.sums_ref = f32[16,1,128]{2,1,0:T(1,128)S(1)} async-done(((f32[16,1,128]{2,1,0:T(1,128)}), f32[16,1,128]{2,1,0:T(1,128)S(1)}, u32[]{:S(2)}, u32[]{:S(2)}) %all-to-all-start.1) | async-done | bytes 8224 | tf_op jit(solution)/shard_map/all_to_all | solution.py:376
  49.1 0.0 copy-done
  49.1 1.0 %residual.1 = (f32[1024,128]{1,0:T(8,128)}, f32[1024,128]{1,0:T(8,128)}) custom-call(f32[16,1,128]{2,1,0:T(1,128)S(1)} %all-to-all-done.1.sums_ref, f32[1024,128]{1,0:T(8,128)S(1)} %remote_terms.1.hpsi_rows, f32[1024,128]{1,0:T(8,128)S(1)} %bitcast.36), custom_call_target="tpu_custom_call" | custom-call | tf_op jit(solution)/shard_map/residual/pallas_call | solution.py:393
Async XLA Ops:
  3.0 30.2 %all-to-all-start = ((f32[16,1,136,128]{3,2,1,0:T(8,128)}), f32[16,1,136,128]{3,2,1,0:T(8,128)S(1)}, u32[]{:S(2)}, u32[]{:S(2)}) async-start(f32[16,1,136,128]{3,2,1,0:T(8,128)} %bitcast.42), calls=%async_computation | async-start | bytes 2228224 | tf_op jit(solution)/shard_map/all_to_all | solution.py:318
  33.2 11.9 %copy-start.1 = (s32[16,1,2]{0,2,1:T(2,128)S(1)}, s32[16,1,2]{0,2,1:T(2,128)}, u32[]{:S(2)}) copy-start(s32[16,1,2]{0,2,1:T(2,128)} %param.17) | copy-start | bytes 388
  33.2 11.9 %copy-start.2 = (s32[16,1,2]{0,2,1:T(2,128)S(1)}, s32[16,1,2]{0,2,1:T(2,128)}, u32[]{:S(2)}) copy-start(s32[16,1,2]{0,2,1:T(2,128)} %param.18) | copy-start | bytes 388
  37.5 11.6 %all-to-all-start.1 = ((f32[16,1,128]{2,1,0:T(1,128)}), f32[16,1,128]{2,1,0:T(1,128)S(1)}, u32[]{:S(2)}, u32[]{:S(2)}) async-start(f32[16,1,128]{2,1,0:T(1,128)} %get-tuple-element.10), calls=%async_computation.1 | async-start | bytes 16384 | tf_op jit(solution)/shard_map/all_to_all | solution.py:376
  45.1 4.0 %copy-start = (f32[8,16384]{1,0:T(8,128)S(1)}, f32[8,16384]{1,0:T(8,128)}, u32[]{:S(2)}) copy-start(f32[8,16384]{1,0:T(8,128)} %param.11) | copy-start | bytes 1572868
